TPU v7x, 32 devices: a whole 2x2x4 slice. The times are simulated.
32 devices in a mesh: head: 4 (over z), batch: 4 (over x, core), rep: 2 (over y).
Axes of the slice: x: 2, y: 2, z: 4, core: 2. Of those that a mesh axis runs over, the one named last changes fastest.
Arguments:
- tokens_in: bfloat16 [8192, 512], P(('batch', 'rep')), may hold values from -6 to 6
- out_grad: float32 [8192, 512], P(('batch', 'rep')), may hold values from -6 to 6
- lengths: int32 [64], P(('batch', 'rep')), may hold values from 32 to 128
- labels: int32 [64], P(('batch', 'rep')), may hold values from 0 to 2
- task_id: int32 [64], P(('batch', 'rep')), may hold values from 0 to 8
- qkv_weight: float32 [3, 512, 512], P(None, None, 'head')
- qkv_first: float32 [3, 512, 512], P(None, None, 'head')
- qkv_second: float32 [3, 512, 512], P(None, None, 'head'), as said below
- out_weight: float32 [512, 512], P('head')
- out_first: float32 [512, 512], P('head')
- out_second: float32 [512, 512], P('head'), as said below
- up_weight: float32 [512, 4, 512], P(None, None, 'head')
- up_first: float32 [512, 4, 512], P(None, None, 'head')
- up_second: float32 [512, 4, 512], P(None, None, 'head'), as said below
- down_weight: float32 [4, 512, 512], P(None, 'head')
- down_first: float32 [4, 512, 512], P(None, 'head')
- down_second: float32 [4, 512, 512], P(None, 'head'), as said below
- split_bias: float32 [6, 512], P(None, 'head'), may hold values from -3 to 3
- split_first: float32 [6, 512], P(None, 'head')
- split_second: float32 [6, 512], P(None, 'head'), as said below
- norm_params: float32 [6, 512], replicated
- norm_first: float32 [6, 512], replicated
- norm_second: float32 [6, 512], replicated, as said below
- class_weight: float32 [9, 512, 3], replicated, may hold values from -0.25 to 0.25
- class_first: float32 [9, 512, 3], replicated
- class_second: float32 [9, 512, 3], replicated, as said below
Outputs:
- output: float32 [8192, 512], P(('batch', 'rep'))
- input_grad: float32 [8192, 512], P(('batch', 'rep'))
- grad_norm: float32 [], replicated
- qkv_first_out: float32 [3, 512, 512], P(None, None, 'head')
- qkv_second_out: float32 [3, 512, 512], P(None, None, 'head')
- qkv_weight_out: float32 [3, 512, 512], P(None, None, 'head')
- out_first_out: float32 [512, 512], P('head')
- out_second_out: float32 [512, 512], P('head')
- out_weight_out: float32 [512, 512], P('head')
- up_first_out: float32 [512, 4, 512], P(None, None, 'head')
- up_second_out: float32 [512, 4, 512], P(None, None, 'head')
- up_weight_out: float32 [512, 4, 512], P(None, None, 'head')
- down_first_out: float32 [4, 512, 512], P(None, 'head')
- down_second_out: float32 [4, 512, 512], P(None, 'head')
- down_weight_out: float32 [4, 512, 512], P(None, 'head')
- split_first_out: float32 [6, 512], P(None, 'head')
- split_second_out: float32 [6, 512], P(None, 'head')
- split_bias_out: float32 [6, 512], P(None, 'head')
- norm_first_out: float32 [6, 512], replicated
- norm_second_out: float32 [6, 512], replicated
- norm_params_out: float32 [6, 512], replicated
- class_first_out: float32 [9, 512, 3], replicated
- class_second_out: float32 [9, 512, 3], replicated
- class_weight_out: float32 [9, 512, 3], replicated
Inputs may be any that keep to these rules, and one draw needn't show every extreme that they name: `qkv_second`: positive. `out_second`: positive. `up_second`: positive. `down_second`: positive. `split_second`: positive. `norm_second`: positive. `class_second`: positive.
All inputs are finite; a program needn't handle non-finite values.
Results may differ from a plain program's by a relative error of at most 0.012.
The roundings to bfloat16 on the way count: a program that leaves them out, or rounds other values in their place, can miss the bound.
Values sent between devices are 32-bit elements; how exact they have to be, the bound alone decides.
No kernel may reach another device: no remote copies, remote signals or barrier semaphores. Data moves between devices by JAX's collectives and lax.ppermute only.
A program may use at most 128 MiB of HBM per device.

v0:
```python
import math

import jax
import jax.numpy as jnp
from jax import lax
from jax.sharding import PartitionSpec as P

HEAD_DIM = 64
STEP = 10


beta_one = 0.9
beta_two = 0.999
learn_rate = 0.05
vector_rate = 0.4
weight_decay = 0.01
adam_eps = 1e-08
clip_at = 1.0
norm_eps = 1e-12
masked = -1e30


def normalized(values):
    row_mean = jnp.mean(values, -1, keepdims=True)
    centred = values - row_mean
    spread = jnp.mean(centred * centred, -1, keepdims=True)
    return centred * lax.rsqrt(spread + norm_eps)


def layer_norm(values, gain_row, shift_row):
    return normalized(values) * gain_row + shift_row


def adam_step(weight, first, second, grad, factor, with_decay):
    clipped = grad * factor
    first_new = beta_one * first + (1.0 - beta_one) * clipped
    second_new = beta_two * second + (1.0 - beta_two) * clipped * clipped
    first_hat = first_new / (1.0 - beta_one**STEP)
    second_hat = second_new / (1.0 - beta_two**STEP)
    update = first_hat / (jnp.sqrt(second_hat) + adam_eps)
    if with_decay:
        update = update + weight_decay * weight
        rate = learn_rate
    else:
        rate = vector_rate
    return (first_new, second_new, weight - rate * update)


def row_step(partial_value, extras, held_rows, row_work):
    pieces = extras
    if partial_value is not None:
        pieces = (lax.psum(partial_value, "head"),) + pieces
    sent_rows, held_new, row_terms = row_work(*pieces + held_rows)
    group_count = lax.axis_size("head")
    share_rows = sent_rows.shape[0] // group_count
    row_start = lax.axis_index("head") * share_rows
    return (
        sent_rows,
        held_new,
        tuple(
            (
                jnp.sum(lax.dynamic_slice_in_dim(element, row_start, share_rows, 0), 0)
                for element in row_terms
            )
        ),
    )


def shards(
    tokens_in,
    out_grad,
    lengths,
    labels,
    task_id,
    qkv_weight,
    qkv_first,
    qkv_second,
    out_weight,
    out_first,
    out_second,
    up_weight,
    up_first,
    up_second,
    down_weight,
    down_first,
    down_second,
    split_bias,
    split_first,
    split_second,
    norm_params,
    norm_first,
    norm_second,
    class_weight,
    class_first,
    class_second,
):
    row_count = tokens_in.shape[0]
    seq_count = lengths.shape[0]
    seq_len = row_count // seq_count
    model_width = tokens_in.shape[1]
    local_cols = qkv_weight.shape[2]
    heads_here = local_cols // HEAD_DIM
    hidden_here = 4 * local_cols
    scale_factor = 1.0 / math.sqrt(HEAD_DIM)
    tokens_f = tokens_in.astype(jnp.float32)
    qkv_low = qkv_weight.astype(jnp.bfloat16)
    out_low = out_weight.astype(jnp.bfloat16)
    up_low = up_weight.reshape(model_width, hidden_here).astype(jnp.bfloat16)
    down_low = down_weight.reshape(hidden_here, model_width).astype(jnp.bfloat16)
    projected = jnp.einsum("td,jdc->jtc", tokens_in, qkv_low, preferred_element_type=jnp.float32)
    query = (projected[0] + split_bias[0]).astype(jnp.bfloat16)
    key_low = projected[1].astype(jnp.bfloat16)
    value = (projected[2] + split_bias[1]).astype(jnp.bfloat16)

    def per_head(matrix):
        return matrix.reshape(seq_count, seq_len, heads_here, HEAD_DIM)

    position = jnp.arange(seq_len, dtype=jnp.int32)
    visible = (position[None, :] < lengths[:, None])[:, None, None, :]

    def scores_of():
        raw = jnp.einsum(
            "sqhd,skhd->shqk",
            per_head(query),
            per_head(key_low),
            preferred_element_type=jnp.float32,
        )
        return jnp.where(visible, raw * scale_factor, masked)

    scores = scores_of()
    row_top = jnp.max(scores, -1, keepdims=True)
    exponent = jnp.exp(scores - row_top)
    row_total = jnp.sum(exponent, -1, keepdims=True)
    prob_low = (exponent / row_total).astype(jnp.bfloat16)
    log_total = row_top + jnp.log(row_total)
    context = jnp.einsum(
        "shqk,skhd->sqhd", prob_low, per_head(value), preferred_element_type=jnp.float32
    )
    context = context.reshape(row_count, local_cols).astype(jnp.bfloat16)
    attn_part = jnp.dot(context, out_low, preferred_element_type=jnp.float32)

    def first_norm(part_total, rows_in):
        summed = rows_in + part_total + norm_params[0]
        return (layer_norm(summed, norm_params[1], norm_params[2]), (summed,), ())

    hidden_one, (pre_one,), unused = row_step(attn_part, (tokens_f,), (), first_norm)
    hidden_low = hidden_one.astype(jnp.bfloat16)
    up_bias = split_bias[2:].reshape(hidden_here)
    pre_act = jnp.dot(hidden_low, up_low, preferred_element_type=jnp.float32) + up_bias
    act_low = jax.nn.gelu(pre_act, approximate=False).astype(jnp.bfloat16)
    ffn_part = jnp.dot(act_low, down_low, preferred_element_type=jnp.float32)

    def second_norm(part_total, rows_in):
        summed = rows_in + part_total + norm_params[3]
        return (layer_norm(summed, norm_params[4], norm_params[5]), (summed,), ())

    output, (pre_two,), unused = row_step(ffn_part, (hidden_one,), (), second_norm)
    first_rows = output.reshape(seq_count, seq_len, model_width)[:, 0]
    task_pick = (
        jnp.arange(class_weight.shape[0], dtype=jnp.int32)[None, :] == task_id[:, None]
    ).astype(jnp.float32)
    task_table = jnp.einsum("st,tdc->sdc", task_pick, class_weight, precision=lax.Precision.HIGHEST)
    logits = jnp.einsum("sd,sdc->sc", first_rows, task_table, precision=lax.Precision.HIGHEST)
    top_logit = jnp.max(logits, -1, keepdims=True)
    logit_exp = jnp.exp(logits - top_logit)
    class_prob = logit_exp / jnp.sum(logit_exp, -1, keepdims=True)
    target = (
        jnp.arange(class_weight.shape[2], dtype=jnp.int32)[None, :] == labels[:, None]
    ).astype(jnp.float32)
    logit_grad = class_prob - target
    class_grad = jnp.einsum(
        "st,sd,sc->tdc", task_pick, first_rows, logit_grad, precision=lax.Precision.HIGHEST
    )
    first_grad = jnp.einsum("sc,sdc->sd", logit_grad, task_table, precision=lax.Precision.HIGHEST)
    spread_grad = jnp.concatenate(
        [first_grad[:, None, :], jnp.zeros((seq_count, seq_len - 1, model_width), jnp.float32)], 1
    )
    top_grad = out_grad + spread_grad.reshape(row_count, model_width)

    def second_back(grad_rows, pre_rows):

        def second_apply_norm(values):
            return layer_norm(values, norm_params[4], norm_params[5])

        unused_out, pull_back = jax.vjp(second_apply_norm, pre_rows)
        (pre_grad,) = pull_back(grad_rows)
        return (pre_grad, (), (grad_rows * normalized(pre_rows), grad_rows, pre_grad))

    pre_grad_two, unused, (gain_two, shift_two, bias_two) = row_step(
        None, (top_grad,), (pre_two,), second_back
    )
    branch_low = pre_grad_two.astype(jnp.bfloat16)
    down_grad = jnp.einsum("th,td->hd", act_low, branch_low, preferred_element_type=jnp.float32)
    act_grad = jnp.einsum("td,hd->th", branch_low, down_low, preferred_element_type=jnp.float32)

    def gelu_only(values):
        return jax.nn.gelu(values, approximate=False)

    unused_out, gelu_pull = jax.vjp(gelu_only, pre_act)
    (up_grad,) = gelu_pull(act_grad)
    up_grad_low = up_grad.astype(jnp.bfloat16)
    up_weight_grad = jnp.einsum(
        "td,th->dh", hidden_low, up_grad_low, preferred_element_type=jnp.float32
    )
    up_bias_grad = jnp.sum(up_grad_low, 0, dtype=jnp.float32)
    hidden_part = jnp.einsum("th,dh->td", up_grad_low, up_low, preferred_element_type=jnp.float32)

    def first_back(part_total, carried, pre_rows):
        grad_rows = part_total + carried

        def first_apply_norm(values):
            return layer_norm(values, norm_params[1], norm_params[2])

        unused_out, pull_back = jax.vjp(first_apply_norm, pre_rows)
        (pre_grad,) = pull_back(grad_rows)
        return (pre_grad, (), (grad_rows * normalized(pre_rows), grad_rows, pre_grad))

    pre_grad_one, unused, (gain_one, shift_one, bias_one) = row_step(
        hidden_part, (pre_grad_two,), (pre_one,), first_back
    )
    attn_low = pre_grad_one.astype(jnp.bfloat16)
    out_weight_grad = jnp.einsum("tc,td->cd", context, attn_low, preferred_element_type=jnp.float32)
    context_grad = jnp.einsum(
        "td,cd->tc", attn_low, out_low, preferred_element_type=jnp.float32
    ).astype(jnp.bfloat16)
    attn_prob = jnp.exp(scores_of() - log_total)
    prob_again = attn_prob.astype(jnp.bfloat16)
    context_heads = per_head(context_grad)
    prob_grad = jnp.einsum(
        "sqhd,skhd->shqk", context_heads, per_head(value), preferred_element_type=jnp.float32
    )
    value_grad = jnp.einsum(
        "shqk,sqhd->skhd", prob_again, context_heads, preferred_element_type=jnp.float32
    )
    value_grad = value_grad.reshape(row_count, local_cols).astype(jnp.bfloat16)
    row_inner = jnp.sum(attn_prob * prob_grad, -1, keepdims=True)
    raw_grad = (attn_prob * (prob_grad - row_inner) * scale_factor).astype(jnp.bfloat16)
    query_grad = jnp.einsum(
        "shqk,skhd->sqhd", raw_grad, per_head(key_low), preferred_element_type=jnp.float32
    )
    query_grad = query_grad.reshape(row_count, local_cols).astype(jnp.bfloat16)
    key_grad = jnp.einsum(
        "shqk,sqhd->skhd", raw_grad, per_head(query), preferred_element_type=jnp.float32
    )
    key_grad = key_grad.reshape(row_count, local_cols).astype(jnp.bfloat16)
    stacked_grad = jnp.stack([query_grad, key_grad, value_grad])
    qkv_weight_grad = jnp.einsum(
        "td,jtc->jdc", tokens_in, stacked_grad, preferred_element_type=jnp.float32
    )
    input_part = jnp.einsum(
        "jtc,jdc->td", stacked_grad, qkv_low, preferred_element_type=jnp.float32
    )
    split_grad = jnp.concatenate(
        [
            jnp.sum(query_grad, 0, dtype=jnp.float32)[None],
            jnp.sum(value_grad, 0, dtype=jnp.float32)[None],
            up_bias_grad.reshape(4, local_cols),
        ],
        0,
    )

    def input_back(part_total, carried):
        return (part_total + carried, (), ())

    input_grad, unused, unused_terms = row_step(input_part, (pre_grad_one,), (), input_back)
    summed = lax.psum(
        (
            qkv_weight_grad,
            out_weight_grad,
            up_weight_grad.reshape(model_width, 4, local_cols),
            down_grad.reshape(4, local_cols, model_width),
            split_grad,
            class_grad,
        ),
        ("batch", "rep"),
    )
    vector_grad = lax.psum(
        jnp.stack([bias_one, gain_one, shift_one, bias_two, gain_two, shift_two]),
        ("head", "batch", "rep"),
    )
    local_square = sum((jnp.sum(element * element) for element in summed[:5]))
    shared_square = lax.psum(local_square, "head")
    grad_norm = jnp.sqrt(
        shared_square + jnp.sum(vector_grad * vector_grad) + jnp.sum(summed[5] * summed[5])
    )
    factor = jnp.minimum(1.0, clip_at / (grad_norm + 1e-06))
    params = (qkv_weight, out_weight, up_weight, down_weight, split_bias, norm_params, class_weight)
    grads = (summed[0], summed[1], summed[2], summed[3], summed[4], vector_grad, summed[5])
    states = (
        (qkv_first, qkv_second, True),
        (out_first, out_second, True),
        (up_first, up_second, True),
        (down_first, down_second, True),
        (split_first, split_second, False),
        (norm_first, norm_second, False),
        (class_first, class_second, True),
    )
    results = ()
    for weight, gradient, state in zip(params, grads, states):
        results = results + adam_step(weight, state[0], state[1], gradient, factor, state[2])
    return (output, input_grad, grad_norm) + results


def solution(mesh):
    in_specs = (
        P(("batch", "rep"), None),
        P(("batch", "rep"), None),
        P(("batch", "rep")),
        P(("batch", "rep")),
        P(("batch", "rep")),
        P(None, None, "head"),
        P(None, None, "head"),
        P(None, None, "head"),
        P("head", None),
        P("head", None),
        P("head", None),
        P(None, None, "head"),
        P(None, None, "head"),
        P(None, None, "head"),
        P(None, "head", None),
        P(None, "head", None),
        P(None, "head", None),
        P(None, "head"),
        P(None, "head"),
        P(None, "head"),
        P(),
        P(),
        P(),
        P(),
        P(),
        P(),
    )
    out_specs = (
        P(("batch", "rep"), None),
        P(("batch", "rep"), None),
        P(),
        P(None, None, "head"),
        P(None, None, "head"),
        P(None, None, "head"),
        P("head", None),
        P("head", None),
        P("head", None),
        P(None, None, "head"),
        P(None, None, "head"),
        P(None, None, "head"),
        P(None, "head", None),
        P(None, "head", None),
        P(None, "head", None),
        P(None, "head"),
        P(None, "head"),
        P(None, "head"),
        P(),
        P(),
        P(),
        P(),
        P(),
        P(),
    )
    return jax.shard_map(shards, mesh=mesh, in_specs=in_specs, out_specs=out_specs, check_vma=False)
```

profile of v0, /device:TPU:0, one launch (start us, length us, event | category | flops | bytes accessed | tf_op | source)
XLA Modules:
  0.0 536.7 jit_solution(18346543418419586306)
XLA Ops:
  7.2 2.1 convolution_bitcast_fusion.1
  16.5 86.6 %all-reduce.9.cloned.1.call-done = f32[1024,512]{1,0:T(8,128)} async-done(((f32[1024,512]{1,0:T(8,128)}), f32[1024,512]{1,0:T(8,128)}) %all-reduce.9.cloned.1.call-update) | async-done | bytes 2097168 | tf_op jit(solution)/shard_map/psum | solution.py:52
  103.2 2.2 fusion.114
  106.9 6.5 %multiply_convert_fusion = (bf16[1024,512]{1,0:T(8,128)(2,1)S(1)}, f32[1024,512]{1,0:T(8,128)}, f32[1024,512]{1,0:T(8,128)}) fusion(f32[512]{0:T(512)S(1)} %slice_bitcast_fusion.2, bf16[64,8,4,128]{3,2,1,0:T(4,128)(2,1)S(1)} %bitcast.121, f32[1024,512]{1,0:T(8,128)S(1)} %subtract_multiply_fusion.1, f32[512]{0:T(512)S(1)} %bitcast.155, f32[512]{0:T(512)S(1)} %bitcast.136), kind=kOutput, calls=%fused_computation.13 | convolution fusion | flops 573046784 | bytes 7870464 | tf_op jit(solution)/shard_map/dot_general | solution.py:149
  116.8 85.2 %all-reduce.11.cloned.1.call-done = f32[1024,512]{1,0:T(8,128)} async-done(((f32[1024,512]{1,0:T(8,128)}), f32[1024,512]{1,0:T(8,128)}) %all-reduce.11.cloned.1.call-update) | async-done | bytes 2097168 | tf_op jit(solution)/shard_map/psum | solution.py:52
  202.0 2.3 fusion.112
  216.6 2.3 multiply_reduce_fusion.1
  226.2 2.1 fusion.27
  228.6 3.6 fusion.53
  232.2 2.7 copy.101
  234.9 3.6 fusion.38
  238.5 75.4 %all-reduce.13.cloned.1.call-done = f32[1024,512]{1,0:T(8,128)} async-done(((f32[1024,512]{1,0:T(8,128)}), f32[1024,512]{1,0:T(8,128)}) %all-reduce.13.cloned.1.call-update) | async-done | bytes 2097168 | tf_op jit(solution)/shard_map/psum | solution.py:52
  313.9 3.0 multiply_reduce_fusion
  324.6 2.5 fusion.73
  327.1 2.1 convert_reduce_fusion.1
  329.3 2.9 convert_reduce_fusion.2
  332.1 3.0 fusion.14
  337.9 2.1 reshape.229
  349.8 2.3 copy.102
  352.1 2.3 copy.103
  358.1 28.0 %all-reduce.1 = (f32[6,128]{1,0:T(8,128)S(1)}, f32[9,512,3]{1,0,2:T(8,128)S(1)}) all-reduce(f32[6,128]{1,0:T(8,128)S(1)} %pad_maximum_fusion, f32[9,512,3]{1,0,2:T(8,128)S(1)} %convolution_bitcast_fusion.3), channel_id=1, replica_groups=mesh['head'=4,'batch'=4,'rep'=2] {'batch','rep'}, use_global_device_ids=true, to_apply=%region_28.29 | all-reduce | flops 14592 | bytes 116736 | tf_op jit(solution)/shard_map/psum | solution.py:266
  386.1 38.4 %psum.94 = f32[6,512]{1,0:T(8,128)S(1)} all-reduce(f32[6,512]{1,0:T(8,128)S(1)} %stack.34), channel_id=1, replica_groups=mesh['head'=4,'batch'=4,'rep'=2] {'head','batch','rep'}, use_global_device_ids=true, to_apply=%region_37.38 | all-reduce | flops 3072 | bytes 24576 | tf_op jit(solution)/shard_map/psum | solution.py:277
  426.4 2.1 convolution_bitcast_fusion
  432.1 2.4 multiply_reduce_fusion.5
  438.6 11.6 %psum.93 = f32[]{:T(128)} all-reduce(f32[]{:T(128)S(6)} %add.305), channel_id=1, replica_groups=mesh['head'=4,'batch'=4,'rep'=2] {'head'}, use_global_device_ids=true, to_apply=%region_30.31 | all-reduce | flops 1 | bytes 8 | tf_op jit(solution)/shard_map/psum | solution.py:282
  454.5 3.3 multiply_subtract_fusion.2
  457.8 2.4 copy.110
  463.8 2.0 multiply_subtract_fusion.3
  465.9 3.6 multiply_subtract_fusion
  469.5 3.2 multiply_subtract_fusion.1
  472.8 53.1 %all-reduce.15.cloned.1.call-done = f32[1024,512]{1,0:T(8,128)} async-done(((f32[1024,512]{1,0:T(8,128)}), f32[1024,512]{1,0:T(8,128)}) %all-reduce.15.cloned.1.call-update) | async-done | bytes 2097168 | tf_op jit(solution)/shard_map/psum | solution.py:52
  525.9 3.2 fusion.131
  (276 shorter events, 67.5 us)
Async XLA Ops:
  7.2 96.0 %all-reduce.9.cloned.1.call-start = ((), (), s32[]{:S(2)}) async-start(), calls=%async_computation | async-start | bytes 4194304 | tf_op jit(solution)/shard_map/psum | solution.py:52
  13.8 188.2 %all-reduce.11.cloned.1.call-start = ((), (), s32[]{:S(2)}) async-start(), calls=%async_computation.1 | async-start | bytes 4194304 | tf_op jit(solution)/shard_map/psum | solution.py:52
  15.9 90.5 %copy-start.79 = (f32[512]{0:T(512)}, f32[512]{0:T(512)S(1)}, u32[]{:S(2)}) copy-start(f32[512]{0:T(512)S(1)} %slice_bitcast_fusion.2) | copy-start | bytes 6148
  16.5 185.5 %copy-start.58 = (f32[1,512]{1,0:T(1,128)}, f32[1,512]{1,0:T(1,128)S(1)}, u32[]{:S(2)}) copy-start(f32[1,512]{1,0:T(1,128)S(1)} %get-tuple-element.123) | copy-start | bytes 6148
  16.5 185.5 %copy-start.68 = (f32[1,512]{1,0:T(1,128)}, f32[1,512]{1,0:T(1,128)S(1)}, u32[]{:S(2)}) copy-start(f32[1,512]{1,0:T(1,128)S(1)} %get-tuple-element.126) | copy-start | bytes 6148
  16.5 188.3 %copy-start.62 = (f32[1,512]{1,0:T(1,128)}, f32[1,512]{1,0:T(1,128)S(1)}, u32[]{:S(2)}) copy-start(f32[1,512]{1,0:T(1,128)S(1)} %get-tuple-element.124) | copy-start | bytes 6148
  105.8 96.2 %copy-start.47 = (f32[1024]{0:T(1024)}, f32[1024]{0:T(1024)S(1)}, u32[]{:S(2)}) copy-start(f32[1024]{0:T(1024)S(1)} %fusion.93) | copy-start | bytes 12292
  106.4 6.9 %copy-start.19 = (f32[1024,512]{1,0:T(8,128)}, f32[1024,512]{1,0:T(8,128)S(1)}, u32[]{:S(2)}) copy-start(f32[1024,512]{1,0:T(8,128)S(1)} %subtract_multiply_fusion.1) | copy-start | bytes 6291460
  106.9 7.4 %copy-start.30 = (bf16[4,128,512]{2,1,0:T(8,128)(2,1)S(1)}, bf16[4,128,512]{2,1,0:T(8,128)(2,1)}, u32[]{:S(2)}) copy-start(bf16[4,128,512]{2,1,0:T(8,128)(2,1)} %convert_element_type.153) | copy-start | bytes 1572868
  116.4 197.5 %all-reduce.13.cloned.1.call-start = ((), (), s32[]{:S(2)}) async-start(), calls=%async_computation.2 | async-start | bytes 4194304 | tf_op jit(solution)/shard_map/psum | solution.py:52
  228.3 200.2 %all-reduce.17.cloned.1.call-start = ((), (), s32[]{:S(2)}) async-start(), calls=%async_computation.4 | async-start | bytes 6291456 | tf_op jit(solution)/shard_map/psum | solution.py:266
  238.5 78.4 %copy-start.53 = (f32[1024]{0:T(1024)S(1)}, f32[1024]{0:T(1024)}, u32[]{:S(2)}) copy-start(f32[1024]{0:T(1024)} %copy-done.52) | copy-start | bytes 12292
  238.5 78.4 %copy-start.48 = (f32[1024]{0:T(1024)S(1)}, f32[1024]{0:T(1024)}, u32[]{:S(2)}) copy-start(f32[1024]{0:T(1024)} %copy-done.47) | copy-start | bytes 12292
  337.9 8.1 %copy-start.8 = (bf16[1024,512]{1,0:T(8,128)(2,1)S(1)}, bf16[1024,512]{1,0:T(8,128)(2,1)}, u32[]{:S(2)}) copy-start(bf16[1024,512]{1,0:T(8,128)(2,1)} %param.26) | copy-start | bytes 3145732
  347.5 178.4 %all-reduce.15.cloned.1.call-start = ((), (), s32[]{:S(2)}) async-start(), calls=%async_computation.3 | async-start | bytes 4194304 | tf_op jit(solution)/shard_map/psum | solution.py:52
  348.6 5.8 %copy-start.78 = (s32[8]{0:T(128)S(1)}, s32[8]{0:T(128)}, u32[]{:S(2)}) copy-start(s32[8]{0:T(128)} %param.30) | copy-start | bytes 100
  348.7 5.9 %copy-start.49 = (f32[8,1,3]{0,2,1:T(4,128)S(1)}, f32[8,1,3]{0,2,1:T(4,128)}, u32[]{:S(2)}) copy-start(f32[8,1,3]{0,2,1:T(4,128)} %copy.120) | copy-start | bytes 292
  348.7 5.9 %copy-start.72 = (f32[8]{0:T(128)S(1)}, f32[8]{0:T(128)}, u32[]{:S(2)}) copy-start(f32[8]{0:T(128)} %copy-done.71) | copy-start | bytes 100
  348.7 5.9 %copy-start.74 = (f32[8]{0:T(128)S(1)}, f32[8]{0:T(128)}, u32[]{:S(2)}) copy-start(f32[8]{0:T(128)} %copy-done.73) | copy-start | bytes 100
  348.7 5.9 %copy-start.81 = (s32[8]{0:T(128)S(1)}, s32[8]{0:T(128)}, u32[]{:S(2)}) copy-start(s32[8]{0:T(128)} %param.29) | copy-start | bytes 100
  356.2 70.2 %copy-start.11 = (bf16[3,1024,128]{2,1,0:T(8,128)(2,1)S(1)}, bf16[3,1024,128]{2,1,0:T(8,128)(2,1)}, u32[]{:S(2)}) copy-start(bf16[3,1024,128]{2,1,0:T(8,128)(2,1)} %copy-done.10) | copy-start | bytes 2359300
  428.4 6.1 %copy-start.18 = (f32[4,128,512]{2,1,0:T(8,128)S(1)}, f32[4,128,512]{2,1,0:T(8,128)}, u32[]{:S(2)}) copy-start(f32[4,128,512]{2,1,0:T(8,128)} %get-tuple-element.83) | copy-start | bytes 3145732
  432.1 20.2 %copy-start.45 = (f32[9,512,3]{1,2,0:T(4,128)S(1)}, f32[9,512,3]{1,2,0:T(4,128)}, u32[]{:S(2)}) copy-start(f32[9,512,3]{1,2,0:T(4,128)} %param.51) | copy-start | bytes 165892
  432.1 20.2 %copy-start.46 = (f32[9,512,3]{1,2,0:T(4,128)S(1)}, f32[9,512,3]{1,2,0:T(4,128)}, u32[]{:S(2)}) copy-start(f32[9,512,3]{1,2,0:T(4,128)} %param.50) | copy-start | bytes 165892
  434.5 19.9 %copy-start.20 = (f32[3,512,128]{1,2,0:T(8,128)S(1)}, f32[3,512,128]{1,2,0:T(8,128)}, u32[]{:S(2)}) copy-start(f32[3,512,128]{1,2,0:T(8,128)} %copy.105) | copy-start | bytes 2359300
  434.5 19.9 %copy-start.21 = (f32[3,512,128]{1,2,0:T(8,128)S(1)}, f32[3,512,128]{1,2,0:T(8,128)}, u32[]{:S(2)}) copy-start(f32[3,512,128]{1,2,0:T(8,128)} %copy.102) | copy-start | bytes 2359300
  457.7 5.4 %copy-start.51 = (f32[6,512]{1,0:T(8,128)S(1)}, f32[6,512]{1,0:T(8,128)}, u32[]{:S(2)}) copy-start(f32[6,512]{1,0:T(8,128)} %param.46) | copy-start | bytes 36868
  457.8 5.4 %copy-start.64 = (f32[6,512]{1,0:T(8,128)S(1)}, f32[6,512]{1,0:T(8,128)}, u32[]{:S(2)}) copy-start(f32[6,512]{1,0:T(8,128)} %param.48) | copy-start | bytes 36868
  457.8 5.4 %copy-start.65 = (f32[6,512]{1,0:T(8,128)S(1)}, f32[6,512]{1,0:T(8,128)}, u32[]{:S(2)}) copy-start(f32[6,512]{1,0:T(8,128)} %param.47) | copy-start | bytes 36868
  457.8 6.0 %copy-start.26 = (f32[128,512]{1,0:T(8,128)S(1)}, f32[128,512]{1,0:T(8,128)}, u32[]{:S(2)}) copy-start(f32[128,512]{1,0:T(8,128)} %param.34) | copy-start | bytes 786436
  457.8 6.0 %copy-start.37 = (f32[128,512]{1,0:T(8,128)S(1)}, f32[128,512]{1,0:T(8,128)}, u32[]{:S(2)}) copy-start(f32[128,512]{1,0:T(8,128)} %get-tuple-element.81) | copy-start | bytes 786436
  469.5 56.4 %copy-start.4 = (f32[1024,512]{1,0:T(8,128)S(1)}, f32[1024,512]{1,0:T(8,128)}, u32[]{:S(2)}) copy-start(f32[1024,512]{1,0:T(8,128)} %copy-done.3) | copy-start | bytes 6291460
  (62 other events, 130.4 us)
Sparse Core Ops, SparseCore 0:
  13.9 89.1 all-reduce.8
  116.5 85.4 all-reduce.10
  228.4 85.4 all-reduce.12
  347.7 72.3 all-reduce.16
  438.8 87.0 all-reduce.14
where the time goes:
time: 538 us; the launch traced here: 537 us
  waiting for transfers between devices  300 us (56%)
  blocking collectives  78 us (14%)
  other arithmetic  48.1 us (9%)
  local copies, waits for them, and re-layouts  45.9 us (9%)
  matrix products  42.7 us (8%)
  between operations  21.1 us (4%)
    psum x4, waiting for transfers between devices, row_step(): pieces = (lax.psum(partial_value, 'head'),) + pieces  300 us
    psum x1, blocking collectives, shards(): lax.psum(jnp.stack([bias_one, gain_one, shift_one, bias_two, gain_two, sh...  38.4 us
    psum x1, blocking collectives, shards(): lax.psum((qkv_weight_grad, out_weight_grad, up_weight_grad.reshape(model_...  28 us
    unnamed x195, local copies, waits for them, and re-layouts  27.3 us
    sub x7, other arithmetic, adam_step(): return (first_new, second_new, weight - rate * update)  13.5 us
    psum x1, blocking collectives, shards(): shared_square = lax.psum(local_square, 'head')  11.6 us
  transfers between devices with their start and end apart: 5, of which 4 were waited for; matrix products, arithmetic and copies ran while one was open for 9% of the time, Pallas kernels for 0%

commit v1 on v0

v1 whole, which is shorter than its diff:
```python
import functools
import math

import jax
import jax.numpy as jnp
from jax import lax
from jax.experimental import pallas as pl
from jax.experimental.pallas import tpu as pltpu
from jax.sharding import PartitionSpec as P

HEAD_DIM = 64
STEP = 10
LANES = 128
BLOCK = 256

F32 = jnp.float32
LOW = jnp.bfloat16

beta_one = 0.9
beta_two = 0.999
learn_rate = 0.05
vector_rate = 0.4
weight_decay = 0.01
adam_eps = 1e-08
clip_at = 1.0
norm_eps = 1e-12
masked = -1e30


def mul(left, right, left_dim=1, right_dim=0):
    return lax.dot_general(
        left, right, (((left_dim,), (right_dim,)), ((), ())), preferred_element_type=F32
    )


def whole(array):
    rank = len(array.shape)
    return pl.BlockSpec(array.shape, lambda *_: (0,) * rank, pipeline_mode=pl.Buffered(1))


def params(mib=52):
    return pltpu.CompilerParams(vmem_limit_bytes=mib << 20)


def shape(dims, kind=F32):
    return jax.ShapeDtypeStruct(tuple(dims), kind)


def centred_parts(values):
    centred = values - jnp.mean(values, -1, keepdims=True)
    spread = jnp.mean(centred * centred, -1, keepdims=True)
    scale = lax.rsqrt(spread + norm_eps)
    return centred * scale, scale


def norm_back(grad, hat, scale, gain):
    scaled = grad * gain
    inner = jnp.mean(scaled * hat, -1, keepdims=True)
    return scale * (scaled - jnp.mean(scaled, -1, keepdims=True) - hat * inner)


def gelu_parts(x):
    density = jnp.exp(x * x * -0.5)
    t = 1.0 / (jnp.abs(x) * (0.3275911 * math.sqrt(0.5)) + 1.0)
    poly = 0.5 * 1.061405429 * t + 0.5 * -1.453152027
    poly = poly * t + 0.5 * 1.421413741
    poly = poly * t + 0.5 * -0.284496736
    poly = poly * t + 0.5 * 0.254829592
    tail = poly * t * density
    below = jnp.where(x < 0.0, tail, 1.0 - tail)
    return x * below, below + x * density * (1.0 / math.sqrt(2.0 * math.pi))


def head_masks():
    lane = lax.broadcasted_iota(jnp.int32, (1, LANES), 1)
    return [(lane // HEAD_DIM == h).astype(LOW) for h in range(LANES // HEAD_DIM)]


def stacked(matrix, masks):
    return jnp.concatenate([matrix * m for m in masks], 0)


def side_by_side(matrix, rows):
    return jnp.concatenate([matrix[:rows], matrix[rows:]], 1)


def adam_math(weight, first, second, grad, factor, with_decay):
    clipped = grad * factor
    first_new = beta_one * first + (1.0 - beta_one) * clipped
    second_new = beta_two * second + (1.0 - beta_two) * clipped * clipped
    first_hat = first_new / (1.0 - beta_one**STEP)
    second_hat = second_new / (1.0 - beta_two**STEP)
    update = first_hat / (jnp.sqrt(second_hat) + adam_eps)
    if with_decay:
        return first_new, second_new, weight - learn_rate * (update + weight_decay * weight)
    return first_new, second_new, weight - vector_rate * update


def pairs(size, bit):
    return [(i, i ^ bit) for i in range(size)]


class Plane:
    def __init__(self, mesh):
        self.heads = mesh.shape["head"]
        self.batch = mesh.shape["batch"]
        self.rep = mesh.shape["rep"]

    def core(self, value):
        return lax.ppermute(value, "batch", pairs(self.batch, 1))

    def side(self, value):
        return lax.ppermute(value, "batch", pairs(self.batch, 2))

    def other(self, value):
        return lax.ppermute(value, "rep", pairs(self.rep, 1))

    def corner(self, value):
        return lax.ppermute(value, ("batch", "rep"), pairs(self.batch * self.rep, 2 * self.rep + 1))

    def along(self, value, bit):
        return lax.ppermute(value, "head", pairs(self.heads, bit))

    def spread(self, block):
        half = block.shape[0] // 2
        from_side, from_other = self.side(block), self.other(block)
        corner = (self.other(from_side[:half]), self.side(from_other[half:]))
        near = (block, from_side, from_other) + corner
        return near[1:] + tuple(self.core(v) for v in near)

    def total(self, keep, send, quarter):
        both = keep + self.core(send)
        rows = both.shape[0] // 4

        def part(bits):
            return lax.dynamic_slice_in_dim(both, (quarter ^ bits) * rows, rows, 0)

        own = part(0) + self.side(part(2)) + self.other(part(1)) + self.corner(part(3))
        near = (own, self.other(own), self.side(own), self.corner(own))
        return near + tuple(self.core(v) for v in near)


def pack_kernel(meta, qkv, out, bias, up, down, a_send, b_send):
    rows = qkv.shape[1]
    width = out.shape[1] // LANES
    for j in range(3):
        a_send[j * rows : (j + 1) * rows, :] = qkv[j]
    base = 3 * rows
    few = out.shape[0]
    for b in range(width):
        a_send[base + b * few : base + (b + 1) * few, :] = out[:, b * LANES : (b + 1) * LANES]
    base += width * few
    a_send[base : base + bias.shape[0], :] = bias[...]
    a_send[base + bias.shape[0] :, :] = jnp.zeros((a_send.shape[0] - base - bias.shape[0], LANES), F32)
    b_send[: up.shape[0], :] = up[...]
    base = up.shape[0]
    few = down.shape[0]
    for b in range(width):
        b_send[base + b * few : base + (b + 1) * few, :] = down[:, b * LANES : (b + 1) * LANES]


def pack(meta, qkv, out, bias, up, down, places):
    width = out.shape[1]
    a_rows = 4 * width // places + 8
    b_rows = (up.shape[0] + down.shape[0] * width // LANES) // places
    grid = pltpu.PrefetchScalarGridSpec(
        num_scalar_prefetch=1,
        grid=(1,),
        in_specs=[
            pl.BlockSpec((3, width // places, LANES), lambda i, m: (0, m[1], 0)),
            pl.BlockSpec((LANES // places, width), lambda i, m: (m[1], 0)),
            whole(bias),
            pl.BlockSpec((up.shape[0] // places, LANES), lambda i, m: (m[1], 0)),
            pl.BlockSpec((down.shape[0] // places, width), lambda i, m: (m[1], 0)),
        ],
        out_specs=[
            pl.BlockSpec((a_rows, LANES), lambda i, m: (0, 0)),
            pl.BlockSpec((b_rows, LANES), lambda i, m: (0, 0)),
        ],
    )
    return pl.pallas_call(
        pack_kernel,
        grid_spec=grid,
        out_shape=[shape((a_rows, LANES)), shape((b_rows, LANES))],
        compiler_params=params(),
        name="pack",
    )(meta, qkv, out, bias, up, down)


def gathered(meta, refs, first_refs):
    here, place = meta[0], meta[1]
    side, other, corner_top, corner_end = refs[:4]
    far = refs[4:]
    groups = [
        (0, None, None),
        (4, side, None),
        (1, other, None),
        (5, corner_top, corner_end),
        (2, far[0], None),
        (6, far[1], None),
        (3, far[2], None),
        (7, far[3], far[4]),
    ]
    for bits, top, end in groups:
        for r in range(1, len(first_refs) + 1):

            def take(row, count, stride=1, top=top, end=end, r=r, bits=bits):
                def read(ref, start):
                    return ref[pl.ds(start, count, stride=stride), :] if stride > 1 else ref[start : start + count, :]

                if bits == 0:
                    return read(first_refs[r - 1], row)
                share = top.shape[0] // (len(first_refs) if end is None else 1)
                if end is None:
                    return read(top, (r - 1) * share + row)
                total = top.shape[0] + end.shape[0]
                start = (r - 1) * (total // len(first_refs)) + row
                if start < top.shape[0]:
                    return read(top, start)
                return read(end, start - top.shape[0])

            yield place ^ bits, here ^ r, take


def at(start, size):
    return pl.ds(pl.multiple_of(start, size), size)


def attention_forward(count, given, meta, lengths, *refs):
    tokens, norm = refs[0], refs[1]
    step = pl.program_id(0)
    if given:
        wqkv, wout, bias = refs[2:5]
        qkv_out, prob_out, context_out, pre_out = refs[5:]
    else:
        own_qkv, own_out, own_bias = refs[2:5]
        first_refs = refs[5 : 5 + count]
        moved = refs[5 + count : 14 + count]
        qkv_out, prob_out, context_out, pre_out, wqkv, wout, bias = refs[14 + count :]
    width = norm.shape[1]

    if not given:

        @pl.when(step == 0)
        def unpack():
            here = meta[0]
            for j in range(3):
                wqkv[here, :, j * LANES : (j + 1) * LANES] = own_qkv[j].astype(LOW)
            wout[at(here * LANES, LANES), :] = own_out[...].astype(LOW)
            bias[here, : own_bias.shape[0], :] = own_bias[...]
            for r in range(1, count + 1):
                piece = first_refs[r - 1]
                bias[here ^ r] = piece[piece.shape[0] - 8 :, :]
            places = 8
            rows = width // places
            few = LANES // places
            for place, shard, take in gathered(meta, moved, first_refs):
                for j in range(3):
                    wqkv[shard, at(place * rows, rows), j * LANES : (j + 1) * LANES] = take(j * rows, rows).astype(LOW)
                for b in range(width // LANES):
                    wout[at(shard * LANES + place * few, few), b * LANES : (b + 1) * LANES] = take(
                        3 * rows + b * few, few
                    ).astype(LOW)

    rows_in = tokens[...]
    groups = wqkv.shape[0]
    masks = head_masks()
    seq_len = LANES
    per_step = rows_in.shape[0] // seq_len
    heads = len(masks)
    col = lax.broadcasted_iota(jnp.int32, (heads * seq_len, seq_len), 1)
    for g in range(groups):
        projected = mul(rows_in, wqkv[g])
        query = (projected[:, :LANES] + bias[g, 0:1, :]).astype(LOW)
        key = projected[:, LANES : 2 * LANES].astype(LOW)
        value = (projected[:, 2 * LANES :] + bias[g, 1:2, :]).astype(LOW)
        qkv_out[g, :, :LANES] = query
        qkv_out[g, :, LANES : 2 * LANES] = key
        qkv_out[g, :, 2 * LANES :] = value
        for t in range(per_step):
            part = slice(t * seq_len, (t + 1) * seq_len)
            scores = mul(stacked(query[part], masks), key[part], 1, 1) * (1.0 / math.sqrt(HEAD_DIM))
            scores = jnp.where(col < lengths[step * per_step + t], scores, masked)
            exponent = jnp.exp(scores - jnp.max(scores, -1, keepdims=True))
            prob = exponent * (1.0 / jnp.sum(exponent, -1, keepdims=True))
            prob_out[g, t] = prob
            low_prob = side_by_side(prob.astype(LOW), seq_len)
            context_out[part, g * LANES : (g + 1) * LANES] = mul(low_prob, stacked(value[part], masks)).astype(LOW)
    attn = mul(context_out[...], wout[...])
    pre_out[...] = rows_in.astype(F32) + attn + norm[0:1, :]


def run_attention_forward(meta, lengths, tokens, norm, weights, first, moved, given):
    rows, width = tokens.shape
    groups = width // LANES
    steps = rows // BLOCK
    seqs = BLOCK // LANES
    heads = LANES // HEAD_DIM
    args = (tokens, norm) + tuple(weights) + tuple(first) + tuple(moved)
    in_specs = [pl.BlockSpec((BLOCK, width), lambda i, *_: (i, 0))] + [whole(a) for a in args[1:]]
    out_shape = [
        shape((groups, rows, 3 * LANES), LOW),
        shape((groups, rows // LANES, heads * LANES, LANES)),
        shape((rows, width), LOW),
        shape((rows, width)),
    ]
    out_specs = [
        pl.BlockSpec((groups, BLOCK, 3 * LANES), lambda i, *_: (0, i, 0)),
        pl.BlockSpec((groups, seqs, heads * LANES, LANES), lambda i, *_: (0, i, 0, 0)),
        pl.BlockSpec((BLOCK, width), lambda i, *_: (i, 0)),
        pl.BlockSpec((BLOCK, width), lambda i, *_: (i, 0)),
    ]
    scratch = []
    if not given:
        extra = [shape((groups, width, 3 * LANES), LOW), shape((width, width), LOW)]
        out_shape += extra
        out_specs += [whole(e) for e in extra]
        scratch = [pltpu.VMEM((groups, 8, LANES), F32)]
    flops = 2 * rows * width * 4 * width + 4 * rows * LANES * width * 2
    return pl.pallas_call(
        functools.partial(attention_forward, len(first), given),
        grid_spec=pltpu.PrefetchScalarGridSpec(
            num_scalar_prefetch=2,
            grid=(steps,),
            in_specs=in_specs,
            out_specs=out_specs,
            scratch_shapes=scratch,
        ),
        out_shape=out_shape,
        compiler_params=params(),
        cost_estimate=pl.CostEstimate(flops=flops, bytes_accessed=16 << 20, transcendentals=0),
        name="attention_forward",
    )(meta, lengths, *args)


def feed_kernel(count, given, meta, labels, tasks, *refs):
    pre_one_ref, out_grad_ref, norm, classes = refs[:4]
    step = pl.program_id(0)
    last = pl.num_programs(0) - 1
    if given:
        wup, wdown, bias = refs[4:7]
        output_ref, back_ref, norm_grad, class_grad, bias_grad, up_grad, down_grad = refs[7:14]
        act_keep, slope_keep, grad_keep = refs[14:]
    else:
        own_up, own_down, own_bias = refs[4:7]
        bias_refs = refs[7 : 7 + count]
        first_refs = refs[7 + count : 7 + 2 * count]
        moved = refs[7 + 2 * count : 16 + 2 * count]
        output_ref, back_ref, norm_grad, class_grad, bias_grad, keep, send = refs[16 + 2 * count : 23 + 2 * count]
        act_keep, slope_keep, grad_keep, wup, wdown, bias, up_grad, down_grad = refs[23 + 2 * count :]
    width = norm.shape[1]
    here = meta[0]

    @pl.when(step == 0)
    def start():
        norm_grad[...] = jnp.zeros_like(norm_grad)
        class_grad[...] = jnp.zeros_like(class_grad)
        bias_grad[...] = jnp.zeros_like(bias_grad)
        up_grad[...] = jnp.zeros_like(up_grad)
        down_grad[...] = jnp.zeros_like(down_grad)

    if not given:

        @pl.when(step == 0)
        def unpack():
            for r in range(4):
                wup[here, :, r * LANES : (r + 1) * LANES] = own_up[pl.ds(r, width, stride=4), :].astype(LOW)
                bias[here, 0:1, r * LANES : (r + 1) * LANES] = own_bias[2 + r : 3 + r, :]
            wdown[here] = own_down[...].astype(LOW)
            for j in range(1, count + 1):
                piece = bias_refs[j - 1]
                base = piece.shape[0] - 6
                for r in range(4):
                    bias[here ^ j, 0:1, r * LANES : (r + 1) * LANES] = piece[base + r : base + r + 1, :]
            rows = width // 8
            for place, shard, take in gathered(meta, moved, first_refs):
                for r in range(4):
                    wup[shard, at(place * rows, rows), r * LANES : (r + 1) * LANES] = take(r, rows, 4).astype(LOW)
                for b in range(width // LANES):
                    wdown[shard, at(place * rows, rows), b * LANES : (b + 1) * LANES] = take(
                        4 * rows + b * rows, rows
                    ).astype(LOW)

    shards = wup.shape[0]
    hat_one, scale_one = centred_parts(pre_one_ref[...])
    hidden = hat_one * norm[1:2, :] + norm[2:3, :]
    low_hidden = hidden.astype(LOW)
    ffn = None
    for s in range(shards):
        act, slope = gelu_parts(mul(low_hidden, wup[s]) + bias[s, 0:1, :])
        low_act = act.astype(LOW)
        act_keep[s] = low_act
        slope_keep[s] = slope
        term = mul(low_act, wdown[s])
        ffn = term if ffn is None else ffn + term
    hat_two, scale_two = centred_parts(hidden + ffn + norm[3:4, :])
    output = hat_two * norm[4:5, :] + norm[5:6, :]
    output_ref[...] = output

    grad = out_grad_ref[...]
    per_step = grad.shape[0] // LANES
    row = lax.broadcasted_iota(jnp.int32, grad.shape, 0)
    class_row = lax.broadcasted_iota(jnp.int32, (classes.shape[1], 1), 0)
    for t in range(per_step):
        task = tasks[step * per_step + t]
        table = classes[task]
        first_row = output[t * LANES : t * LANES + 1, :]
        logits = jnp.sum(table * first_row, -1, keepdims=True)
        logit_exp = jnp.exp(logits - jnp.max(logits, 0, keepdims=True))
        class_prob = logit_exp / jnp.sum(logit_exp, 0, keepdims=True)
        logit_grad = class_prob - (class_row == labels[step * per_step + t]).astype(F32)
        class_grad[task] += logit_grad * first_row
        grad = jnp.where(row == t * LANES, grad + jnp.sum(logit_grad * table, 0, keepdims=True), grad)

    norm_grad[4:5, :] += jnp.sum(grad * hat_two, 0, keepdims=True)
    norm_grad[5:6, :] += jnp.sum(grad, 0, keepdims=True)
    back_two = norm_back(grad, hat_two, scale_two, norm[4:5, :])
    norm_grad[3:4, :] += jnp.sum(back_two, 0, keepdims=True)
    low_back = back_two.astype(LOW)
    back_hidden = back_two
    for s in range(shards):
        up_back = (mul(low_back, wdown[s], 1, 1) * slope_keep[s]).astype(LOW)
        grad_keep[s] = up_back
        back_hidden = back_hidden + mul(up_back, wup[s], 1, 1)
    own_back = grad_keep[here]
    down_grad[...] += mul(act_keep[here], low_back, 0, 0)
    up_grad[...] += mul(low_hidden, own_back, 0, 0)
    bias_grad[0:1, :] += jnp.sum(own_back.astype(F32), 0, keepdims=True)

    norm_grad[1:2, :] += jnp.sum(back_hidden * hat_one, 0, keepdims=True)
    norm_grad[2:3, :] += jnp.sum(back_hidden, 0, keepdims=True)
    back_one = norm_back(back_hidden, hat_one, scale_one, norm[1:2, :])
    norm_grad[0:1, :] += jnp.sum(back_one, 0, keepdims=True)
    back_ref[...] = back_one

    if not given:

        def give_up(ref):
            for r in range(4):
                ref[pl.ds(r, width, stride=4), :] = up_grad[:, r * LANES : (r + 1) * LANES]

        def give_down(ref):
            for b in range(width // LANES):
                ref[b * 4 * LANES : (b + 1) * 4 * LANES, :] = down_grad[:, b * LANES : (b + 1) * LANES]

        @pl.when((step == last) & (meta[2] == 0))
        def give_first():
            give_up(keep)
            give_down(send)

        @pl.when((step == last) & (meta[2] == 1))
        def give_second():
            give_up(send)
            give_down(keep)


def run_feed(meta, labels, tasks, pre_one, out_grad, norm, classes, weights, biases, first, moved, given):
    rows, width = pre_one.shape
    steps = rows // BLOCK
    if given:
        shards, _, hidden = weights[0].shape
    else:
        shards, hidden = len(first) + 1, 4 * LANES
    args = (pre_one, out_grad, norm, classes) + tuple(weights) + tuple(biases) + tuple(first) + tuple(moved)
    by_rows = pl.BlockSpec((BLOCK, width), lambda i, *_: (i, 0))
    in_specs = [by_rows, by_rows] + [whole(a) for a in args[2:]]
    fixed = [shape((8, width)), shape(classes.shape), shape((8, hidden))]
    scratch = [
        pltpu.VMEM((shards, BLOCK, hidden), LOW),
        pltpu.VMEM((shards, BLOCK, hidden), F32),
        pltpu.VMEM((shards, BLOCK, hidden), LOW),
    ]
    if given:
        fixed += [shape((width, hidden)), shape((hidden, width))]
    else:
        half = hidden * width // LANES
        fixed += [shape((half, LANES)), shape((half, LANES))]
        scratch += [
            pltpu.VMEM((shards, width, hidden), LOW),
            pltpu.VMEM((shards, hidden, width), LOW),
            pltpu.VMEM((shards, 8, hidden), F32),
            pltpu.VMEM((width, hidden), F32),
            pltpu.VMEM((hidden, width), F32),
        ]
    flops = 2 * rows * width * hidden * (4 * shards + 2)
    return pl.pallas_call(
        functools.partial(feed_kernel, len(first), given),
        grid_spec=pltpu.PrefetchScalarGridSpec(
            num_scalar_prefetch=3,
            grid=(steps,),
            in_specs=in_specs,
            out_specs=[by_rows, by_rows] + [whole(f) for f in fixed],
            scratch_shapes=scratch,
        ),
        out_shape=[shape((rows, width)), shape((rows, width))] + fixed,
        compiler_params=params(),
        cost_estimate=pl.CostEstimate(flops=4 * flops, bytes_accessed=20 << 20, transcendentals=0),
        name="feed_both",
    )(meta, labels, tasks, *args)


def pair_back(qkv, prob, context_back, masks):
    query, key, value = (qkv[:, j * LANES : (j + 1) * LANES] for j in range(3))
    seq_len = query.shape[0]
    wide_back = stacked(context_back, masks)
    prob_back = mul(wide_back, value, 1, 1)
    value_back = mul(prob.astype(LOW), wide_back, 0, 0).astype(LOW)
    inner = jnp.sum(prob * prob_back, -1, keepdims=True)
    raw = (prob * (prob_back - inner) * (1.0 / math.sqrt(HEAD_DIM))).astype(LOW)
    query_back = mul(side_by_side(raw, seq_len), stacked(key, masks)).astype(LOW)
    key_back = mul(raw, stacked(query, masks), 0, 0).astype(LOW)
    return query_back, key_back, value_back


def group_back(low_back, qkv_ref, prob_ref, wout_rows, masks, store):
    context_back = mul(low_back, wout_rows, 1, 1).astype(LOW)
    for t in range(low_back.shape[0] // LANES):
        part = slice(t * LANES, (t + 1) * LANES)
        for j, grad in enumerate(pair_back(qkv_ref[part, :], prob_ref[t], context_back[part], masks)):
            store(part, j, grad)


def own_kernel(given, meta, back_ref, tokens, qkv, prob, context, wout, *refs):
    if given:
        grads, qkv_grad, out_grad, split_grad = refs
    else:
        norm_grad, class_grad, up_bias, grads, keep, send, qkv_grad, out_grad, split_grad, packed = refs
    step = pl.program_id(0)
    last = pl.num_programs(0) - 1

    @pl.when(step == 0)
    def start():
        qkv_grad[...] = jnp.zeros_like(qkv_grad)
        out_grad[...] = jnp.zeros_like(out_grad)
        split_grad[...] = jnp.zeros_like(split_grad)

    masks = head_masks()
    low_back = back_ref[...].astype(LOW)

    def store(part, j, grad):
        grads[part, j * LANES : (j + 1) * LANES] = grad

    group_back(low_back, qkv.at[0], prob.at[0], wout[...], masks, store)
    out_grad[...] += mul(context[...], low_back, 0, 0)
    both = grads[...]
    qkv_grad[...] += mul(tokens[...], both, 0, 0)
    split_grad[0:1, :] += jnp.sum(both[:, :LANES].astype(F32), 0, keepdims=True)
    split_grad[1:2, :] += jnp.sum(both[:, 2 * LANES :].astype(F32), 0, keepdims=True)

    if not given:
        width = back_ref.shape[1]
        blocks = width // LANES

        @pl.when(step == last)
        def fill():
            for j in range(3):
                packed[j * width : (j + 1) * width, :] = qkv_grad[:, j * LANES : (j + 1) * LANES]
            base = 3 * width
            for b in range(blocks):
                packed[base + b * LANES : base + (b + 1) * LANES, :] = out_grad[:, b * LANES : (b + 1) * LANES]
            base += width
            packed[base:, :] = jnp.zeros((packed.shape[0] - base, LANES), F32)
            packed[base : base + 2, :] = split_grad[0:2, :]
            for r in range(4):
                packed[base + 2 + r : base + 3 + r, :] = up_bias[0:1, r * LANES : (r + 1) * LANES]
            base += 8
            for b in range(blocks):
                packed[base + 8 * b : base + 8 * b + 6, :] = norm_grad[0:6, b * LANES : (b + 1) * LANES]
            base += 8 * blocks
            tasks, kinds, _ = class_grad.shape
            each = small_rows(tasks, kinds)
            for b in range(blocks):
                for t in range(tasks):
                    row = base + each * b + kinds * t
                    packed[row : row + kinds, :] = class_grad[t, :, b * LANES : (b + 1) * LANES]

        half = keep.shape[0]

        @pl.when((step == last) & (meta[2] == 0))
        def give_first():
            keep[...] = packed[:half, :]
            send[...] = packed[half:, :]

        @pl.when((step == last) & (meta[2] == 1))
        def give_second():
            keep[...] = packed[half:, :]
            send[...] = packed[:half, :]


def small_rows(tasks, kinds):
    return -(-tasks * kinds // 8) * 8


def packed_rows(width, tasks, kinds):
    blocks = width // LANES
    rows = 4 * width + 8 + 8 * blocks + blocks * small_rows(tasks, kinds)
    return -(-rows // 64) * 64


def run_own(meta, back, tokens, qkv, prob, context, wout, smalls, given):
    rows, width = back.shape
    steps = rows // BLOCK
    seqs = BLOCK // LANES
    heads = LANES // HEAD_DIM
    by_rows = pl.BlockSpec((BLOCK, width), lambda i, m: (i, 0))
    in_specs = [
        by_rows,
        by_rows,
        pl.BlockSpec((1, BLOCK, 3 * LANES), lambda i, m: (m[3], i, 0)),
        pl.BlockSpec((1, seqs, heads * LANES, LANES), lambda i, m: (m[3], i, 0, 0)),
        pl.BlockSpec((BLOCK, LANES), lambda i, m: (i, m[3])),
        pl.BlockSpec((LANES, width), lambda i, m: (m[3], 0)),
    ] + [whole(s) for s in smalls]
    out_shape = [shape((rows, 3 * LANES), LOW)]
    out_specs = [pl.BlockSpec((BLOCK, 3 * LANES), lambda i, m: (i, 0))]
    sums = [shape((width, 3 * LANES)), shape((LANES, width)), shape((8, LANES))]
    scratch = []
    if given:
        fixed = sums
    else:
        count = packed_rows(width, *smalls[1].shape[:2])
        fixed = [shape((count // 2, LANES))] * 2
        scratch = [pltpu.VMEM(s.shape, F32) for s in sums] + [pltpu.VMEM((count, LANES), F32)]
    return pl.pallas_call(
        functools.partial(own_kernel, given),
        grid_spec=pltpu.PrefetchScalarGridSpec(
            num_scalar_prefetch=1,
            grid=(steps,),
            in_specs=in_specs,
            out_specs=out_specs + [whole(f) for f in fixed],
            scratch_shapes=scratch,
        ),
        out_shape=out_shape + fixed,
        compiler_params=params(),
        cost_estimate=pl.CostEstimate(flops=4 << 30, bytes_accessed=8 << 20, transcendentals=0),
        name="attention_own",
    )(meta, back, tokens, qkv, prob, context, wout, *smalls)


def rest_kernel(meta, back_ref, qkv, prob, wout, wqkv, own, input_grad, grads):
    group = meta[3]
    groups = qkv.shape[0]
    masks = head_masks()
    back = back_ref[...]
    low_back = back.astype(LOW)
    grads[group] = own[...]
    for r in range(1, groups):
        g = group ^ r

        def store(part, j, grad, g=g):
            grads[g, part, j * LANES : (j + 1) * LANES] = grad

        group_back(low_back, qkv.at[g], prob.at[g], wout[at(g * LANES, LANES), :], masks, store)
    total = None
    for g in range(groups):
        term = mul(grads[g], wqkv[g], 1, 1)
        total = term if total is None else total + term
    input_grad[...] = back + total


def run_rest(meta, back, qkv, prob, wout, wqkv, own):
    rows, width = back.shape
    groups = width // LANES
    seqs = BLOCK // LANES
    heads = LANES // HEAD_DIM
    by_rows = pl.BlockSpec((BLOCK, width), lambda i, m: (i, 0))
    return pl.pallas_call(
        rest_kernel,
        grid_spec=pltpu.PrefetchScalarGridSpec(
            num_scalar_prefetch=1,
            grid=(rows // BLOCK,),
            in_specs=[
                by_rows,
                pl.BlockSpec((groups, BLOCK, 3 * LANES), lambda i, m: (0, i, 0)),
                pl.BlockSpec((groups, seqs, heads * LANES, LANES), lambda i, m: (0, i, 0, 0)),
                whole(wout),
                whole(wqkv),
                pl.BlockSpec((BLOCK, 3 * LANES), lambda i, m: (i, 0)),
            ],
            out_specs=by_rows,
            scratch_shapes=[pltpu.VMEM((groups, BLOCK, 3 * LANES), LOW)],
        ),
        out_shape=shape((rows, width)),
        compiler_params=params(),
        cost_estimate=pl.CostEstimate(flops=8 << 30, bytes_accessed=12 << 20, transcendentals=0),
        name="attention_rest",
    )(meta, back, qkv, prob, wout, wqkv, own)


def collect_kernel(split_rows, meta, *refs):
    parts, full, squares = refs[:8], refs[8], refs[9]
    rows = parts[0].shape[0]
    for half in range(2):
        for bits in range(4):
            place = (meta[2] ^ half) * 4 + (meta[4] ^ bits)
            full[pl.ds(pl.multiple_of(place * rows, 8), rows), :] = parts[half * 4 + bits][...]
    squares[...] = jnp.zeros_like(squares)
    head = full[:split_rows, :]
    squares[0:1, :] = jnp.sum(head * head, 0, keepdims=True)
    if split_rows < full.shape[0]:
        tail = full[split_rows:, :]
        squares[1:2, :] = jnp.sum(tail * tail, 0, keepdims=True)


def collect(meta, parts, split_rows=None):
    rows = 8 * parts[0].shape[0]
    outs = [shape((rows, LANES)), shape((8, LANES))]
    return pl.pallas_call(
        functools.partial(collect_kernel, split_rows or rows),
        grid_spec=pltpu.PrefetchScalarGridSpec(
            num_scalar_prefetch=1,
            grid=(1,),
            in_specs=[whole(p) for p in parts],
            out_specs=[whole(o) for o in outs],
        ),
        out_shape=outs,
        compiler_params=params(),
        name="collect",
    )(meta, *parts)


def adam_kernel(count, meta, squares, *refs):
    moved = refs[:count]
    a_full, b_full = refs[count : count + 2]
    states = refs[count + 2 : count + 23]
    norm_ref = refs[count + 23]
    outs = refs[count + 24 : count + 45]
    sums = refs[count + 45]
    sums[meta[0]] = squares[...]
    for r in range(1, count + 1):
        sums[meta[0] ^ r] = moved[r - 1][...]
    total = sums[0]
    for s in range(1, count + 1):
        total = total + sums[s]
    all_squares = jnp.sum(total[0:1, :], -1, keepdims=True) + jnp.sum(squares[1:2, :], -1, keepdims=True)
    grad_norm = jnp.sqrt(all_squares)
    norm_ref[...] = grad_norm
    factor = jnp.minimum(1.0, clip_at / (grad_norm + 1e-06))
    width = states[5 * 3].shape[1]
    blocks = width // LANES

    def update(index, where, grad, with_decay):
        first, second, weight = (states[3 * index + j][where] for j in range(3))
        for j, value in enumerate(adam_math(weight, first, second, grad, factor, with_decay)):
            outs[3 * index + j][where] = value

    for j in range(3):
        update(0, (j,), a_full[j * width : (j + 1) * width, :], True)
    base = 3 * width
    for b in range(blocks):
        lanes = slice(b * LANES, (b + 1) * LANES)
        update(1, (slice(None), lanes), a_full[base + b * LANES : base + (b + 1) * LANES, :], True)
    base += width
    update(4, (slice(None), slice(None)), a_full[base : base + 6, :], False)
    base += 8
    for b in range(blocks):
        lanes = slice(b * LANES, (b + 1) * LANES)
        update(5, (slice(None), lanes), a_full[base + 8 * b : base + 8 * b + 6, :], False)
    base += 8 * blocks
    tasks, kinds, _ = states[6 * 3].shape
    each = small_rows(tasks, kinds)
    for b in range(blocks):
        lanes = slice(b * LANES, (b + 1) * LANES)
        for t in range(tasks):
            row = base + each * b + kinds * t
            update(6, (t, slice(None), lanes), a_full[row : row + kinds, :], True)
    rows = 4 * width
    update(2, (slice(None), slice(None)), b_full[:rows, :], True)
    for b in range(blocks):
        lanes = slice(b * LANES, (b + 1) * LANES)
        update(3, (slice(None), lanes), b_full[rows + b * 4 * LANES : rows + (b + 1) * 4 * LANES, :], True)


def run_adam(meta, squares, moved, a_full, b_full, states):
    outs = [shape((1, 1))] + [shape(s.shape) for s in states]
    args = (squares,) + tuple(moved) + (a_full, b_full) + tuple(states)
    return pl.pallas_call(
        functools.partial(adam_kernel, len(moved)),
        grid_spec=pltpu.PrefetchScalarGridSpec(
            num_scalar_prefetch=1,
            grid=(1,),
            in_specs=[whole(a) for a in args],
            out_specs=[whole(o) for o in outs],
            scratch_shapes=[pltpu.VMEM((len(moved) + 1, 8, LANES), F32)],
        ),
        out_shape=outs,
        compiler_params=params(),
        name="adam",
    )(meta, *args)


def shares(mesh, *args):
    fast = (
        mesh.shape["batch"] == 4
        and mesh.shape["rep"] == 2
        and args[5].shape[2] == LANES
        and mesh.shape["head"] * LANES == args[0].shape[1]
    )
    return (by_permutes if fast else by_gathers)(mesh, *args)


def by_permutes(
    mesh,
    tokens_in,
    out_grad,
    lengths,
    labels,
    task_id,
    qkv_weight,
    qkv_first,
    qkv_second,
    out_weight,
    out_first,
    out_second,
    up_weight,
    up_first,
    up_second,
    down_weight,
    down_first,
    down_second,
    split_bias,
    split_first,
    split_second,
    norm_params,
    norm_first,
    norm_second,
    class_weight,
    class_first,
    class_second,
):
    plane = Plane(mesh)
    width = tokens_in.shape[1]
    here = lax.axis_index("head")
    batch = lax.axis_index("batch")
    rep = lax.axis_index("rep")
    quarter = (batch // 2) * 2 + rep
    meta = jnp.stack([here, batch * plane.rep + rep, batch % 2, here, quarter]).astype(jnp.int32)

    def flat_up(value):
        return value.reshape(-1, LANES)

    def flat_down(value):
        return value.reshape(-1, width)

    def flat_class(value):
        return jnp.transpose(value, (0, 2, 1))

    up_flat, down_flat, classes = flat_up(up_weight), flat_down(down_weight), flat_class(class_weight)
    a_send, b_send = pack(meta, qkv_weight, out_weight, split_bias, up_flat, down_flat, plane.batch * plane.rep)
    turns = range(1, plane.heads)
    a_first = [plane.along(a_send, r) for r in turns]
    b_first = [plane.along(b_send, r) for r in turns]
    a_moved = plane.spread(jnp.concatenate([v[:-8] for v in a_first], 0))
    b_moved = plane.spread(jnp.concatenate(b_first, 0))

    qkv, prob, context, pre_one, wqkv, wout = run_attention_forward(
        meta, lengths, tokens_in, norm_params, (qkv_weight, out_weight, split_bias), a_first, a_moved, False
    )
    output, back_one, norm_grad, class_grad, up_bias_grad, b_keep, b_give = run_feed(
        meta,
        labels,
        task_id,
        pre_one,
        out_grad,
        norm_params,
        classes,
        (up_flat, down_flat, split_bias),
        a_first,
        b_first,
        b_moved,
        False,
    )
    own, a_keep, a_give = run_own(
        meta, back_one, tokens_in, qkv, prob, context, wout, (norm_grad, class_grad, up_bias_grad), False
    )
    input_grad = run_rest(meta, back_one, qkv, prob, wout, wqkv, own)
    b_full, b_squares = collect(meta, plane.total(b_keep, b_give, quarter))
    a_full, a_squares = collect(meta, plane.total(a_keep, a_give, quarter), 4 * width + 8)
    squares = a_squares + b_squares
    states = (
        (qkv_first, qkv_second, qkv_weight)
        + (out_first, out_second, out_weight)
        + (flat_up(up_first), flat_up(up_second), up_flat)
        + (flat_down(down_first), flat_down(down_second), down_flat)
        + (split_first, split_second, split_bias)
        + (norm_first, norm_second, norm_params)
        + (flat_class(class_first), flat_class(class_second), classes)
    )
    grad_norm, *new = run_adam(meta, squares, [plane.along(squares, r) for r in turns], a_full, b_full, states)
    new[6:9] = [v.reshape(up_weight.shape) for v in new[6:9]]
    new[9:12] = [v.reshape(down_weight.shape) for v in new[9:12]]
    new[18:21] = [jnp.transpose(v, (0, 2, 1)) for v in new[18:21]]
    return (output, input_grad, grad_norm[0, 0]) + tuple(new)


def by_gathers(
    mesh,
    tokens_in,
    out_grad,
    lengths,
    labels,
    task_id,
    qkv_weight,
    qkv_first,
    qkv_second,
    out_weight,
    out_first,
    out_second,
    up_weight,
    up_first,
    up_second,
    down_weight,
    down_first,
    down_second,
    split_bias,
    split_first,
    split_second,
    norm_params,
    norm_first,
    norm_second,
    class_weight,
    class_first,
    class_second,
):
    width = tokens_in.shape[1]
    cols = qkv_weight.shape[2]
    groups = width // LANES
    hidden = 4 * cols
    here = lax.axis_index("head")
    zero = jnp.zeros_like(here)
    meta = jnp.stack([here, zero, zero, here * cols // LANES, zero]).astype(jnp.int32)
    full_qkv = lax.all_gather(qkv_weight, "head", axis=2, tiled=True)
    full_out = lax.all_gather(out_weight, "head", axis=0, tiled=True)
    full_up = lax.all_gather(up_weight.reshape(width, hidden), "head", axis=0)
    full_down = lax.all_gather(down_weight.reshape(hidden, width), "head", axis=0)
    full_bias = lax.all_gather(split_bias, "head", axis=1, tiled=True)
    full_qkv, full_out, full_up, full_down, full_bias = lax.optimization_barrier(
        (full_qkv, full_out, full_up, full_down, full_bias)
    )
    wqkv = full_qkv.reshape(3, width, groups, LANES).transpose(2, 1, 0, 3).reshape(groups, width, 3 * LANES).astype(LOW)
    wout = full_out.astype(LOW)
    qv_bias = jnp.pad(full_bias[:2].reshape(2, groups, LANES).transpose(1, 0, 2), ((0, 0), (0, 6), (0, 0)))
    shards = width // cols
    up_bias = full_bias[2:].reshape(4, shards, cols).transpose(1, 0, 2).reshape(shards, 1, hidden)
    up_bias = jnp.pad(up_bias, ((0, 0), (0, 7), (0, 0)))
    classes = jnp.transpose(class_weight, (0, 2, 1))

    qkv, prob, context, pre_one = run_attention_forward(
        meta, lengths, tokens_in, norm_params, (wqkv, wout, qv_bias), (), (), True
    )
    output, back_one, norm_grad, class_grad, up_bias_grad, up_grad, down_grad = run_feed(
        meta,
        labels,
        task_id,
        pre_one,
        out_grad,
        norm_params,
        classes,
        (full_up.astype(LOW), full_down.astype(LOW), up_bias),
        (),
        (),
        (),
        True,
    )
    own, qkv_grad, out_w_grad, split_grad = run_own(meta, back_one, tokens_in, qkv, prob, context, wout, (), True)
    input_grad = run_rest(meta, back_one, qkv, prob, wout, wqkv, own)
    start = here * cols % LANES
    qkv_grad = qkv_grad.reshape(width, 3, LANES).transpose(1, 0, 2)
    qkv_grad = lax.dynamic_slice_in_dim(qkv_grad, start, cols, 2)
    out_w_grad = lax.dynamic_slice_in_dim(out_w_grad, start, cols, 0)
    split_grad = lax.dynamic_slice_in_dim(split_grad[:2], start, cols, 1)
    split_grad = jnp.concatenate([split_grad, up_bias_grad[0].reshape(4, cols)], 0)
    summed = lax.psum(
        (
            qkv_grad,
            out_w_grad,
            up_grad.reshape(up_weight.shape),
            down_grad.reshape(down_weight.shape),
            split_grad,
            norm_grad[:6],
            jnp.transpose(class_grad, (0, 2, 1)),
        ),
        ("batch", "rep"),
    )
    split_square = lax.psum(sum(jnp.sum(v * v) for v in summed[:5]), "head")
    grad_norm = jnp.sqrt(split_square + sum(jnp.sum(v * v) for v in summed[5:]))
    factor = jnp.minimum(1.0, clip_at / (grad_norm + 1e-06))
    states = (
        (qkv_weight, qkv_first, qkv_second, True),
        (out_weight, out_first, out_second, True),
        (up_weight, up_first, up_second, True),
        (down_weight, down_first, down_second, True),
        (split_bias, split_first, split_second, False),
        (norm_params, norm_first, norm_second, False),
        (class_weight, class_first, class_second, True),
    )
    results = ()
    for grad, (weight, first, second, decay) in zip(summed, states):
        results += adam_math(weight, first, second, grad, factor, decay)
    return (output, input_grad, grad_norm) + results


def solution(mesh):
    rows = P(("batch", "rep"), None)
    seqs = P(("batch", "rep"))
    kinds = (
        (P(None, None, "head"),) * 3
        + (P("head", None),) * 3
        + (P(None, None, "head"),) * 3
        + (P(None, "head", None),) * 3
        + (P(None, "head"),) * 3
        + (P(),) * 6
    )
    return jax.shard_map(
        functools.partial(shares, mesh),
        mesh=mesh,
        in_specs=(rows, rows, seqs, seqs, seqs) + kinds,
        out_specs=(rows, rows, P()) + kinds,
        check_vma=False,
    )
```

time: 538 us -> 212 us (0.39)
  waiting for transfers between devices: 300 us -> 74.1 us
  blocking collectives: 78 us -> 0 us
  Pallas kernels: 0 us -> 77.7 us
  starting transfers between devices: 0.61 us -> 44.9 us
  other arithmetic: 48.1 us -> 4.96 us
  matrix products: 42.7 us -> 0 us
  local copies, waits for them, and re-layouts: 45.9 us -> 7.94 us
  between operations: 21.1 us -> 1.39 us
    psum x5 -> x0, waiting for transfers between devices: 300 us -> none  [the longest x4 300 us: row_step(): pieces = (lax.psum(partial_value, 'head'),) + pieces]
    psum x3 -> x0, blocking collectives: 78 us -> none  [the longest x1 38.4 us: shards(): lax.psum(jnp.stack([bias_one, gain_one, shift_one, bias_two, gain_two, sh...]
    pallas_call x0 -> x8, Pallas kernels: none -> 77.7 us  [the longest x1 27.2 us: run_feed(): pl.pallas_call(functools.partial(feed_kernel, len(first), given), grid_sp...]
    ppermute x0 -> x49, waiting for transfers between devices: none -> 74.1 us  [the longest x8 33.4 us: other(): return lax.ppermute(value, 'rep', pairs(self.rep, 1))]
    ppermute x0 -> x49, starting transfers between devices: none -> 44.9 us  [the longest x9 19.1 us: along(): return lax.ppermute(value, 'head', pairs(self.heads, bit))]
    dot_general x22 -> x0, matrix products: 42.7 us -> none  [the longest x1 6.45 us: shards(): jnp.dot(hidden_low, up_low, preferred_element_type=jnp.float32) + up_bias]
    reduce_sum x19 -> x0, other arithmetic: 24.9 us -> none  [the longest x5 7.52 us: shards(): local_square = sum((jnp.sum(element * element) for element in summed[:5]))]
    unnamed x195 -> x72, local copies, waits for them, and re-layouts: 27.3 us -> 6.17 us
  transfers between devices with their start and end apart: 5 -> 49, of which waited for: 4 -> 18; matrix products, arithmetic and copies ran while one was open for 9% -> 3% of each run, Pallas kernels for 0% -> 16%
where the time goes in v1:
time: 212 us; the launch traced here: 211 us
  Pallas kernels  77.7 us (37%)
  waiting for transfers between devices  74.1 us (35%)
  starting transfers between devices  44.9 us (21%)
  local copies, waits for them, and re-layouts  7.94 us (4%)
  other arithmetic  4.96 us (2%)
    ppermute x8, waiting for transfers between devices, other(): return lax.ppermute(value, 'rep', pairs(self.rep, 1))  33.4 us
    pallas_call x1, Pallas kernels, run_feed(): pl.pallas_call(functools.partial(feed_kernel, len(first), given), grid_sp...  27.2 us
    ppermute x9, waiting for transfers between devices, along(): return lax.ppermute(value, 'head', pairs(self.heads, bit))  21.5 us
    ppermute x9, starting transfers between devices, along(): return lax.ppermute(value, 'head', pairs(self.heads, bit))  19.1 us
    pallas_call x1, Pallas kernels, run_rest(): pl.pallas_call(rest_kernel, grid_spec=pltpu.PrefetchScalarGridSpec(num_sc...  13.4 us
    pallas_call x1, Pallas kernels, run_attention_forward(): pl.pallas_call(functools.partial(attention_forward, len(first), given), g...  12.3 us
    ppermute x4, waiting for transfers between devices, corner(): lax.ppermute(value, ('batch', 'rep'), pairs(self.batch * self.rep, 2 * se...  11.2 us
    pallas_call x1, Pallas kernels, run_adam(): pl.pallas_call(functools.partial(adam_kernel, len(moved)), grid_spec=pltp...  11.1 us
  transfers between devices with their start and end apart: 49, of which 18 were waited for; matrix products, arithmetic and copies ran while one was open for 3% of the time, Pallas kernels for 16%

profile of v1, /device:TPU:0, one launch (start us, length us, event | category | flops | bytes accessed | tf_op | source)
XLA Modules:
  0.0 211.0 jit_solution(13392330322028201603)
XLA Ops:
  3.5 1.5 pack.1
  5.1 3.1 %collective-permute-start.12 = (f32[512,128]{1,0:T(8,128)S(1)}, f32[512,128]{1,0:T(8,128)S(1)}, u32[]{:S(2)}, u32[]{:S(2)}) collective-permute-start(f32[512,128]{1,0:T(8,128)S(1)} %get-tuple-element.70), channel_id=1, source_target_pairs={{0,8},{8,0},{16,24},{24,16},{1,9},{9,1},{17,25},{25,17},{2,10},{10... | collective-permute-start | bytes 786440 | tf_op jit(solution)/shard_map/ppermute | solution.py:122
  8.2 2.5 %collective-permute-start.2 = (f32[264,128]{1,0:T(8,128)S(1)}, f32[264,128]{1,0:T(8,128)S(1)}, u32[]{:S(2)}, u32[]{:S(2)}) collective-permute-start(f32[264,128]{1,0:T(8,128)S(1)} %get-tuple-element.68), channel_id=1, source_target_pairs={{0,24},{8,16},{16,8},{24,0},{1,25},{9,17},{17,9},{25,1},{2,26},{10... | collective-permute-start | bytes 405512 | tf_op jit(solution)/shard_map/ppermute | solution.py:122
  10.8 1.8 collective-permute-start
  12.6 1.7 collective-permute-start.13
  14.2 6.5 %collective-permute-done.2.refs_7_.refs_9_ = f32[264,128]{1,0:T(8,128)S(1)} collective-permute-done((f32[264,128]{1,0:T(8,128)S(1)}, f32[264,128]{1,0:T(8,128)S(1)}, u32[]{:S(2)}, u32[]{:S(2)}) %collective-permute-start.2) | collective-permute-done | bytes 135200 | tf_op jit(solution)/shard_map/ppermute | solution.py:122
  22.2 1.8 collective-permute-done.1.refs_6_.refs_8_
  25.0 1.9 collective-permute-start.3
  26.9 1.5 collective-permute-start.4
  28.5 12.3 %collective-permute-done.13.refs_11_ = f32[512,128]{1,0:T(8,128)S(1)} collective-permute-done((f32[512,128]{1,0:T(8,128)S(1)}, f32[512,128]{1,0:T(8,128)S(1)}, u32[]{:S(2)}, u32[]{:S(2)}) %collective-permute-start.13) | collective-permute-done | bytes 262176 | tf_op jit(solution)/shard_map/ppermute | solution.py:122
  40.8 1.6 collective-permute-start.15
  42.4 1.5 collective-permute-start.16
  45.1 18.5 %collective-permute-done.5.refs_10_ = f32[384,128]{1,0:T(8,128)S(1)} collective-permute-done((f32[384,128]{1,0:T(8,128)S(1)}, f32[384,128]{1,0:T(8,128)S(1)}, u32[]{:S(2)}, u32[]{:S(2)}) %collective-permute-start.5) | collective-permute-done | bytes 196640 | tf_op jit(solution)/shard_map/ppermute | solution.py:116
  68.0 8.6 %collective-permute-done.17.refs_15_ = f32[768,128]{1,0:T(8,128)S(1)} collective-permute-done((f32[768,128]{1,0:T(8,128)S(1)}, f32[768,128]{1,0:T(8,128)S(1)}, u32[]{:S(2)}, u32[]{:S(2)}) %collective-permute-start.17) | collective-permute-done | bytes 393248 | tf_op jit(solution)/shard_map/ppermute | solution.py:116
  76.5 2.0 collective-permute-done.18.refs_16_
  78.6 12.3 %attention_forward.1 = (bf16[4,1024,384]{2,1,0:T(8,128)(2,1)}, f32[4,8,256,128]{3,2,1,0:T(8,128)}, bf16[1024,512]{1,0:T(8,128)(2,1)}, f32[1024,512]{1,0:T(8,128)...) custom-call(s32[5]{0:T(128)S(1)} %stack.20.meta, s32[8]{0:T(128)S(1)} %copy-done.16, bf16[1024,512]{1,0:T(8,128)(2,1)} %tokens.1, ...), custom_call_target="tpu_custom_call" | custom-call | flops 2684354560 | bytes 16777216 | tf_op jit(solution)/shard_map/attention_forward/pallas_call | solution.py:320
  92.6 27.2 %feed_both.1 = (f32[1024,512]{1,0:T(8,128)}, f32[1024,512]{1,0:T(8,128)}, f32[8,512]{1,0:T(8,128)S(1)}, f32[9,3,512]{2,1,0:T(4,128)S(1)}, f32[8,512]{1,0:T(8,128...) custom-call(s32[5]{0:T(128)S(1)} %stack.20.meta, s32[8]{0:T(128)S(1)} %copy-done.17, s32[8]{0:T(128)S(1)} %copy-done.18, ...), custom_call_target="tpu_custom_call" | custom-call | flops 38654705664 | bytes 20971520 | tf_op jit(solution)/shard_map/feed_both/pallas_call | solution.py:486
  120.4 7.4 %attention_own.1 = (bf16[1024,384]{1,0:T(8,128)(2,1)}, f32[1120,128]{1,0:T(8,128)S(1)}, f32[1120,128]{1,0:T(8,128)S(1)}) custom-call(s32[5]{0:T(128)S(1)} %stack.20.meta, f32[1024,512]{1,0:T(8,128)} %get-tuple-element.72.back_ref, bf16[1024,512]{1,0:T(8,128)(2,1)} %tokens.1, bf16[4,1024,384]{2,1,0:T(8,128)(2,1)} %get-tuple-element.73.qkv, ...), custom_call_target="tpu_custom_call" | custom-call | flops 4294967296 | bytes 8388608 | tf_op jit(solution)/shard_map/attention_own/pallas_call | solution.py:624
  127.8 2.1 collective-permute-done.24
  136.2 1.6 add.73
  144.5 4.6 %collective-permute-done.38 = f32[512,128]{1,0:T(8,128)} collective-permute-done((f32[512,128]{1,0:T(8,128)}, f32[512,128]{1,0:T(8,128)}, u32[]{:S(2)}, u32[]{:S(2)}) %collective-permute-start.38) | collective-permute-done | bytes 262176 | tf_op jit(solution)/shard_map/ppermute | solution.py:119
  149.9 3.3 %collective-permute-done.37 = f32[512,128]{1,0:T(8,128)} collective-permute-done((f32[512,128]{1,0:T(8,128)}, f32[512,128]{1,0:T(8,128)}, u32[]{:S(2)}, u32[]{:S(2)}) %collective-permute-start.37) | collective-permute-done | bytes 262176 | tf_op jit(solution)/shard_map/ppermute | solution.py:116
  157.2 1.7 collective-permute-start.41
  158.8 2.0 collective-permute-done.30.refs_3_
  162.3 3.0 %collective-permute-done.39.refs_1_ = f32[512,128]{1,0:T(8,128)S(1)} collective-permute-done((f32[512,128]{1,0:T(8,128)S(1)}, f32[512,128]{1,0:T(8,128)S(1)}, u32[]{:S(2)}, u32[]{:S(2)}) %collective-permute-start.39) | collective-permute-done | bytes 262176 | tf_op jit(solution)/shard_map/ppermute | solution.py:116
  165.8 4.6 %collective-permute-done.41.refs_3_ = f32[512,128]{1,0:T(8,128)S(1)} collective-permute-done((f32[512,128]{1,0:T(8,128)S(1)}, f32[512,128]{1,0:T(8,128)S(1)}, u32[]{:S(2)}, u32[]{:S(2)}) %collective-permute-start.41) | collective-permute-done | bytes 262176 | tf_op jit(solution)/shard_map/ppermute | solution.py:119
  172.2 1.6 collect.2
  174.6 3.0 %collect.3 = (f32[4096,128]{1,0:T(8,128)}, f32[8,128]{1,0:T(8,128)S(1)}) custom-call(s32[5]{0:T(128)S(1)} %stack.20.meta, f32[512,128]{1,0:T(8,128)S(1)} %add_add_fusion.refs_0_, f32[512,128]{1,0:T(8,128)S(1)} %collective-permute-done.39.refs_1_, f32[512,128]{1,0:T(8,128)S(1)} %collective-permute-done.40.refs_2_, ...), custom_call_target="tpu_custom_call" | custom-call | tf_op jit(solution)/shard_map/collect/pallas_call | solution.py:708
  177.5 6.1 %collective-permute-start.46 = (f32[8,128]{1,0:T(8,128)S(1)}, f32[8,128]{1,0:T(8,128)S(1)}, u32[]{:S(2)}, u32[]{:S(2)}) collective-permute-start(f32[8,128]{1,0:T(8,128)S(1)} %add.81.squares), channel_id=1, source_target_pairs={{0,8},{8,0},{16,24},{24,16},{1,9},{9,1},{17,25},{25,17},{2,10},{10... | collective-permute-start | bytes 12296 | tf_op jit(solution)/shard_map/ppermute | solution.py:122
  184.5 1.6 collective-permute-start.48
  186.1 13.4 %attention_rest.1 = f32[1024,512]{1,0:T(8,128)} custom-call(s32[5]{0:T(128)S(1)} %stack.20.meta, f32[1024,512]{1,0:T(8,128)} %get-tuple-element.72.back_ref, bf16[4,1024,384]{2,1,0:T(8,128)(2,1)} %get-tuple-element.73.qkv, f32[4,8,256,128]{3,2,1,0:T(8,128)} %get-tuple-element.74.prob, bf16[512,512]{1,0:T(8,128)(2,1)S(1)} %copy-done.20, ...), custom_call_target="tpu_custom_call" | custom-call | flops 8589934592 | bytes 12582912 | tf_op jit(solution)/shard_map/attention_rest/pallas_call | solution.py:667
  199.7 11.1 %adam.1 = (f32[1,1]{1,0:T(1,128)}, f32[3,512,128]{2,1,0:T(8,128)}, f32[3,512,128]{2,1,0:T(8,128)}, f32[3,512,128]{2,1,0:T(8,128)}, f32[128,512]{1,0:T(8,128)}, /...) custom-call(s32[5]{0:T(128)S(1)} %stack.20.meta, ...), custom_call_target="tpu_custom_call" | custom-call | tf_op jit(solution)/shard_map/adam/pallas_call | solution.py:777
  (163 shorter events, 36.1 us)
Async XLA Ops:
  5.1 23.4 %collective-permute-start.12 = (f32[512,128]{1,0:T(8,128)S(1)}, f32[512,128]{1,0:T(8,128)S(1)}, u32[]{:S(2)}, u32[]{:S(2)}) collective-permute-start(f32[512,128]{1,0:T(8,128)S(1)} %get-tuple-element.70), channel_id=1, source_target_pairs={{0,8},{8,0},{16,24},{24,16},{1,9},{9,1},{17,25},{25,17},{2,10},{10... | collective-permute-start | bytes 786440 | tf_op jit(solution)/shard_map/ppermute | solution.py:122
  8.2 12.5 %collective-permute-start.2 = (f32[264,128]{1,0:T(8,128)S(1)}, f32[264,128]{1,0:T(8,128)S(1)}, u32[]{:S(2)}, u32[]{:S(2)}) collective-permute-start(f32[264,128]{1,0:T(8,128)S(1)} %get-tuple-element.68), channel_id=1, source_target_pairs={{0,24},{8,16},{16,8},{24,0},{1,25},{9,17},{17,9},{25,1},{2,26},{10... | collective-permute-start | bytes 405512 | tf_op jit(solution)/shard_map/ppermute | solution.py:122
  10.6 13.4 %collective-permute-start.1 = (f32[264,128]{1,0:T(8,128)S(1)}, f32[264,128]{1,0:T(8,128)S(1)}, u32[]{:S(2)}, u32[]{:S(2)}) collective-permute-start(f32[264,128]{1,0:T(8,128)S(1)} %get-tuple-element.68), channel_id=1, source_target_pairs={{0,16},{8,24},{16,0},{24,8},{1,17},{9,25},{17,1},{25,9},{2,18},{10... | collective-permute-start | bytes 405512 | tf_op jit(solution)/shard_map/ppermute | solution.py:122
  10.8 14.2 %collective-permute-start = (f32[264,128]{1,0:T(8,128)S(1)}, f32[264,128]{1,0:T(8,128)S(1)}, u32[]{:S(2)}, u32[]{:S(2)}) collective-permute-start(f32[264,128]{1,0:T(8,128)S(1)} %get-tuple-element.68), channel_id=1, source_target_pairs={{0,8},{8,0},{16,24},{24,16},{1,9},{9,1},{17,25},{25,17},{2,10},{10... | collective-permute-start | bytes 405512 | tf_op jit(solution)/shard_map/ppermute | solution.py:122
  12.6 28.2 %collective-permute-start.13 = (f32[512,128]{1,0:T(8,128)S(1)}, f32[512,128]{1,0:T(8,128)S(1)}, u32[]{:S(2)}, u32[]{:S(2)}) collective-permute-start(f32[512,128]{1,0:T(8,128)S(1)} %get-tuple-element.70), channel_id=1, source_target_pairs={{0,16},{8,24},{16,0},{24,8},{1,17},{9,25},{17,1},{25,9},{2,18},{10... | collective-permute-start | bytes 786440 | tf_op jit(solution)/shard_map/ppermute | solution.py:122
  20.7 20.1 %collective-permute-start.14 = (f32[512,128]{1,0:T(8,128)S(1)}, f32[512,128]{1,0:T(8,128)S(1)}, u32[]{:S(2)}, u32[]{:S(2)}) collective-permute-start(f32[512,128]{1,0:T(8,128)S(1)} %get-tuple-element.70), channel_id=1, source_target_pairs={{0,24},{8,16},{16,8},{24,0},{1,25},{9,17},{17,9},{25,1},{2,26},{10... | collective-permute-start | bytes 786440 | tf_op jit(solution)/shard_map/ppermute | solution.py:122
  25.0 18.9 %collective-permute-start.3 = (f32[768,128]{1,0:T(8,128)S(1)}, f32[768,128]{1,0:T(8,128)S(1)}, u32[]{:S(2)}, u32[]{:S(2)}) collective-permute-start(f32[768,128]{1,0:T(8,128)S(1)} %pad_maximum_fusion), channel_id=1, source_target_pairs={{0,4},{2,6},{4,0},{6,2},{1,5},{3,7},{5,1},{7,3},{8,12},{10,14},{12... | collective-permute-start | bytes 1179656 | tf_op jit(solution)/shard_map/ppermute | solution.py:113
  26.9 17.6 %collective-permute-start.4 = (f32[768,128]{1,0:T(8,128)S(1)}, f32[768,128]{1,0:T(8,128)S(1)}, u32[]{:S(2)}, u32[]{:S(2)}) collective-permute-start(f32[768,128]{1,0:T(8,128)S(1)} %pad_maximum_fusion), channel_id=1, source_target_pairs={{0,1},{1,0},{2,3},{3,2},{4,5},{5,4},{6,7},{7,6},{8,9},{9,8},{10,11... | collective-permute-start | bytes 1179656 | tf_op jit(solution)/shard_map/ppermute | solution.py:116
  40.8 23.3 %collective-permute-start.15 = (f32[1536,128]{1,0:T(8,128)S(1)}, f32[1536,128]{1,0:T(8,128)S(1)}, u32[]{:S(2)}, u32[]{:S(2)}) collective-permute-start(f32[1536,128]{1,0:T(8,128)S(1)} %constant_dynamic-update-slice_fusion), channel_id=1, source_target_pairs={{0,4},{2,6},{4,0},{6,2},{1,5},{3,7},{5,1},{7,3},{8,12},{10,14},{12... | collective-permute-start | bytes 2359304 | tf_op jit(solution)/shard_map/ppermute | solution.py:113
  42.4 21.9 %collective-permute-start.16 = (f32[1536,128]{1,0:T(8,128)S(1)}, f32[1536,128]{1,0:T(8,128)S(1)}, u32[]{:S(2)}, u32[]{:S(2)}) collective-permute-start(f32[1536,128]{1,0:T(8,128)S(1)} %constant_dynamic-update-slice_fusion), channel_id=1, source_target_pairs={{0,1},{1,0},{2,3},{3,2},{4,5},{5,4},{6,7},{7,6},{8,9},{9,8},{10,11... | collective-permute-start | bytes 2359304 | tf_op jit(solution)/shard_map/ppermute | solution.py:116
  43.9 19.7 %collective-permute-start.5 = (f32[384,128]{1,0:T(8,128)S(1)}, f32[384,128]{1,0:T(8,128)S(1)}, u32[]{:S(2)}, u32[]{:S(2)}) collective-permute-start(f32[384,128]{1,0:T(8,128)S(1)} %slice.31), channel_id=1, source_target_pairs={{0,1},{1,0},{2,3},{3,2},{4,5},{5,4},{6,7},{7,6},{8,9},{9,8},{10,11... | collective-permute-start | bytes 589832 | tf_op jit(solution)/shard_map/ppermute | solution.py:116
  44.5 19.1 %collective-permute-start.6 = (f32[384,128]{1,0:T(8,128)S(1)}, f32[384,128]{1,0:T(8,128)S(1)}, u32[]{:S(2)}, u32[]{:S(2)}) collective-permute-start(f32[384,128]{1,0:T(8,128)S(1)} %slice.32), channel_id=1, source_target_pairs={{0,4},{2,6},{4,0},{6,2},{1,5},{3,7},{5,1},{7,3},{8,12},{10,14},{12... | collective-permute-start | bytes 589832 | tf_op jit(solution)/shard_map/ppermute | solution.py:113
  45.1 19.7 %collective-permute-start.7 = (f32[768,128]{1,0:T(8,128)S(1)}, f32[768,128]{1,0:T(8,128)S(1)}, u32[]{:S(2)}, u32[]{:S(2)}) collective-permute-start(f32[768,128]{1,0:T(8,128)S(1)} %pad_maximum_fusion), channel_id=1, source_target_pairs={{0,2},{2,0},{4,6},{6,4},{1,3},{3,1},{5,7},{7,5},{8,10},{10,8},{12,... | collective-permute-start | bytes 1179656 | tf_op jit(solution)/shard_map/ppermute | solution.py:110
  64.8 26.1 %collective-permute-start.19 = (f32[1536,128]{1,0:T(8,128)S(1)}, f32[1536,128]{1,0:T(8,128)S(1)}, u32[]{:S(2)}, u32[]{:S(2)}) collective-permute-start(f32[1536,128]{1,0:T(8,128)S(1)} %constant_dynamic-update-slice_fusion), channel_id=1, source_target_pairs={{0,2},{2,0},{4,6},{6,4},{1,3},{3,1},{5,7},{7,5},{8,10},{10,8},{12,... | collective-permute-start | bytes 2359304 | tf_op jit(solution)/shard_map/ppermute | solution.py:110
  65.4 11.2 %collective-permute-start.17 = (f32[768,128]{1,0:T(8,128)S(1)}, f32[768,128]{1,0:T(8,128)S(1)}, u32[]{:S(2)}, u32[]{:S(2)}) collective-permute-start(f32[768,128]{1,0:T(8,128)S(1)} %slice.33), channel_id=1, source_target_pairs={{0,1},{1,0},{2,3},{3,2},{4,5},{5,4},{6,7},{7,6},{8,9},{9,8},{10,11... | collective-permute-start | bytes 1179656 | tf_op jit(solution)/shard_map/ppermute | solution.py:116
  66.9 24.1 %collective-permute-start.20 = (f32[1536,128]{1,0:T(8,128)S(1)}, f32[1536,128]{1,0:T(8,128)S(1)}, u32[]{:S(2)}, u32[]{:S(2)}) collective-permute-start(f32[1536,128]{1,0:T(8,128)S(1)} %collective-permute-done.15.refs_13_), channel_id=1, source_target_pairs={{0,2},{2,0},{4,6},{6,4},{1,3},{3,1},{5,7},{7,5},{8,10},{10,8},{12,... | collective-permute-start | bytes 2359304 | tf_op jit(solution)/shard_map/ppermute | solution.py:110
  66.9 24.1 %collective-permute-start.21 = (f32[1536,128]{1,0:T(8,128)S(1)}, f32[1536,128]{1,0:T(8,128)S(1)}, u32[]{:S(2)}, u32[]{:S(2)}) collective-permute-start(f32[1536,128]{1,0:T(8,128)S(1)} %collective-permute-done.16.refs_14_), channel_id=1, source_target_pairs={{0,2},{2,0},{4,6},{6,4},{1,3},{3,1},{5,7},{7,5},{8,10},{10,8},{12,... | collective-permute-start | bytes 2359304 | tf_op jit(solution)/shard_map/ppermute | solution.py:110
  67.4 11.1 %collective-permute-start.18 = (f32[768,128]{1,0:T(8,128)S(1)}, f32[768,128]{1,0:T(8,128)S(1)}, u32[]{:S(2)}, u32[]{:S(2)}) collective-permute-start(f32[768,128]{1,0:T(8,128)S(1)} %slice.34), channel_id=1, source_target_pairs={{0,4},{2,6},{4,0},{6,2},{1,5},{3,7},{5,1},{7,3},{8,12},{10,14},{12... | collective-permute-start | bytes 1179656 | tf_op jit(solution)/shard_map/ppermute | solution.py:113
  76.5 14.5 %collective-permute-start.22 = (f32[768,128]{1,0:T(8,128)S(1)}, f32[768,128]{1,0:T(8,128)S(1)}, u32[]{:S(2)}, u32[]{:S(2)}) collective-permute-start(f32[768,128]{1,0:T(8,128)S(1)} %collective-permute-done.17.refs_15_), channel_id=1, source_target_pairs={{0,2},{2,0},{4,6},{6,4},{1,3},{3,1},{5,7},{7,5},{8,10},{10,8},{12,... | collective-permute-start | bytes 1179656 | tf_op jit(solution)/shard_map/ppermute | solution.py:110
  78.5 12.5 %collective-permute-start.23 = (f32[768,128]{1,0:T(8,128)S(1)}, f32[768,128]{1,0:T(8,128)S(1)}, u32[]{:S(2)}, u32[]{:S(2)}) collective-permute-start(f32[768,128]{1,0:T(8,128)S(1)} %collective-permute-done.18.refs_16_), channel_id=1, source_target_pairs={{0,2},{2,0},{4,6},{6,4},{1,3},{3,1},{5,7},{7,5},{8,10},{10,8},{12,... | collective-permute-start | bytes 1179656 | tf_op jit(solution)/shard_map/ppermute | solution.py:110
  119.8 15.4 %collective-permute-start.35 = (f32[2048,128]{1,0:T(8,128)}, f32[2048,128]{1,0:T(8,128)S(1)}, u32[]{:S(2)}, u32[]{:S(2)}) collective-permute-start(f32[2048,128]{1,0:T(8,128)} %get-tuple-element.86), channel_id=1, source_target_pairs={{0,2},{2,0},{4,6},{6,4},{1,3},{3,1},{5,7},{7,5},{8,10},{10,8},{12,... | collective-permute-start | bytes 3145736 | tf_op jit(solution)/shard_map/ppermute | solution.py:110
  138.7 10.5 %collective-permute-start.38 = (f32[512,128]{1,0:T(8,128)}, f32[512,128]{1,0:T(8,128)}, u32[]{:S(2)}, u32[]{:S(2)}) collective-permute-start(f32[512,128]{1,0:T(8,128)} %get-tuple-element.113), channel_id=1, source_target_pairs={{0,5},{1,4},{2,7},{3,6},{4,1},{5,0},{6,3},{7,2},{8,13},{9,12},{10,... | collective-permute-start | bytes 786440 | tf_op jit(solution)/shard_map/ppermute | solution.py:119
  139.4 13.8 %collective-permute-start.37 = (f32[512,128]{1,0:T(8,128)}, f32[512,128]{1,0:T(8,128)}, u32[]{:S(2)}, u32[]{:S(2)}) collective-permute-start(f32[512,128]{1,0:T(8,128)} %get-tuple-element.114), channel_id=1, source_target_pairs={{0,1},{1,0},{2,3},{3,2},{4,5},{5,4},{6,7},{7,6},{8,9},{9,8},{10,11... | collective-permute-start | bytes 786440 | tf_op jit(solution)/shard_map/ppermute | solution.py:116
  140.7 13.4 %collective-permute-start.36 = (f32[512,128]{1,0:T(8,128)S(1)}, f32[512,128]{1,0:T(8,128)}, u32[]{:S(2)}, u32[]{:S(2)}) collective-permute-start(f32[512,128]{1,0:T(8,128)S(1)} %get-tuple-element.112), channel_id=1, source_target_pairs={{0,4},{2,6},{4,0},{6,2},{1,5},{3,7},{5,1},{7,3},{8,12},{10,14},{12... | collective-permute-start | bytes 786440 | tf_op jit(solution)/shard_map/ppermute | solution.py:113
  143.2 14.0 %collective-permute-start.28 = (f32[280,128]{1,0:T(8,128)S(1)}, f32[280,128]{1,0:T(8,128)S(1)}, u32[]{:S(2)}, u32[]{:S(2)}) collective-permute-start(f32[280,128]{1,0:T(8,128)S(1)} %add_add_fusion.1.refs_0_), channel_id=1, source_target_pairs={{0,1},{1,0},{2,3},{3,2},{4,5},{5,4},{6,7},{7,6},{8,9},{9,8},{10,11... | collective-permute-start | bytes 430088 | tf_op jit(solution)/shard_map/ppermute | solution.py:116
  144.0 14.8 %collective-permute-start.29 = (f32[280,128]{1,0:T(8,128)S(1)}, f32[280,128]{1,0:T(8,128)S(1)}, u32[]{:S(2)}, u32[]{:S(2)}) collective-permute-start(f32[280,128]{1,0:T(8,128)S(1)} %add_add_fusion.1.refs_0_), channel_id=1, source_target_pairs={{0,4},{2,6},{4,0},{6,2},{1,5},{3,7},{5,1},{7,3},{8,12},{10,14},{12... | collective-permute-start | bytes 430088 | tf_op jit(solution)/shard_map/ppermute | solution.py:113
  149.2 11.7 %collective-permute-start.30 = (f32[280,128]{1,0:T(8,128)S(1)}, f32[280,128]{1,0:T(8,128)S(1)}, u32[]{:S(2)}, u32[]{:S(2)}) collective-permute-start(f32[280,128]{1,0:T(8,128)S(1)} %add_add_fusion.1.refs_0_), channel_id=1, source_target_pairs={{0,5},{1,4},{2,7},{3,6},{4,1},{5,0},{6,3},{7,2},{8,13},{9,12},{10,... | collective-permute-start | bytes 430088 | tf_op jit(solution)/shard_map/ppermute | solution.py:119
  157.2 13.3 %collective-permute-start.41 = (f32[512,128]{1,0:T(8,128)S(1)}, f32[512,128]{1,0:T(8,128)S(1)}, u32[]{:S(2)}, u32[]{:S(2)}) collective-permute-start(f32[512,128]{1,0:T(8,128)S(1)} %add_add_fusion.refs_0_), channel_id=1, source_target_pairs={{0,5},{1,4},{2,7},{3,6},{4,1},{5,0},{6,3},{7,2},{8,13},{9,12},{10,... | collective-permute-start | bytes 786440 | tf_op jit(solution)/shard_map/ppermute | solution.py:119
  162.2 11.6 %collective-permute-start.42 = (f32[512,128]{1,0:T(8,128)S(1)}, f32[512,128]{1,0:T(8,128)S(1)}, u32[]{:S(2)}, u32[]{:S(2)}) collective-permute-start(f32[512,128]{1,0:T(8,128)S(1)} %add_add_fusion.refs_0_), channel_id=1, source_target_pairs={{0,2},{2,0},{4,6},{6,4},{1,3},{3,1},{5,7},{7,5},{8,10},{10,8},{12,... | collective-permute-start | bytes 786440 | tf_op jit(solution)/shard_map/ppermute | solution.py:110
  177.5 22.0 %collective-permute-start.46 = (f32[8,128]{1,0:T(8,128)S(1)}, f32[8,128]{1,0:T(8,128)S(1)}, u32[]{:S(2)}, u32[]{:S(2)}) collective-permute-start(f32[8,128]{1,0:T(8,128)S(1)} %add.81.squares), channel_id=1, source_target_pairs={{0,8},{8,0},{16,24},{24,16},{1,9},{9,1},{17,25},{25,17},{2,10},{10... | collective-permute-start | bytes 12296 | tf_op jit(solution)/shard_map/ppermute | solution.py:122
  183.7 15.9 %collective-permute-start.47 = (f32[8,128]{1,0:T(8,128)S(1)}, f32[8,128]{1,0:T(8,128)S(1)}, u32[]{:S(2)}, u32[]{:S(2)}) collective-permute-start(f32[8,128]{1,0:T(8,128)S(1)} %add.81.squares), channel_id=1, source_target_pairs={{0,16},{8,24},{16,0},{24,8},{1,17},{9,25},{17,1},{25,9},{2,18},{10... | collective-permute-start | bytes 12296 | tf_op jit(solution)/shard_map/ppermute | solution.py:122
  184.5 15.1 %collective-permute-start.48 = (f32[8,128]{1,0:T(8,128)S(1)}, f32[8,128]{1,0:T(8,128)S(1)}, u32[]{:S(2)}, u32[]{:S(2)}) collective-permute-start(f32[8,128]{1,0:T(8,128)S(1)} %add.81.squares), channel_id=1, source_target_pairs={{0,24},{8,16},{16,8},{24,0},{1,25},{9,17},{17,9},{25,1},{2,26},{10... | collective-permute-start | bytes 12296 | tf_op jit(solution)/shard_map/ppermute | solution.py:122
  (52 other events, 693.8 us)

commit v2 on v1

--- a/solution.py
+++ b/solution.py
@@ -11,7 +11,7 @@
 HEAD_DIM = 64
 STEP = 10
 LANES = 128
-BLOCK = 256
+BLOCK = 512
 
 F32 = jnp.float32
 LOW = jnp.bfloat16
@@ -42,6 +42,14 @@
     return pltpu.CompilerParams(vmem_limit_bytes=mib << 20)
 
 
+def in_hbm(value):
+    return pltpu.with_memory_space_constraint(value, pltpu.HBM)
+
+
+def in_vmem(value):
+    return pltpu.with_memory_space_constraint(value, pltpu.VMEM)
+
+
 def shape(dims, kind=F32):
     return jax.ShapeDtypeStruct(tuple(dims), kind)
 
@@ -60,15 +68,9 @@
 
 
 def gelu_parts(x):
-    density = jnp.exp(x * x * -0.5)
-    t = 1.0 / (jnp.abs(x) * (0.3275911 * math.sqrt(0.5)) + 1.0)
-    poly = 0.5 * 1.061405429 * t + 0.5 * -1.453152027
-    poly = poly * t + 0.5 * 1.421413741
-    poly = poly * t + 0.5 * -0.284496736
-    poly = poly * t + 0.5 * 0.254829592
-    tail = poly * t * density
-    below = jnp.where(x < 0.0, tail, 1.0 - tail)
-    return x * below, below + x * density * (1.0 / math.sqrt(2.0 * math.pi))
+    below = lax.erf(x * math.sqrt(0.5)) * 0.5 + 0.5
+    density = jnp.exp2(x * x * (-0.5 * math.log2(math.e))) * (1.0 / math.sqrt(2.0 * math.pi))
+    return x * below, below + x * density
 
 
 def head_masks():
@@ -121,70 +123,91 @@
     def along(self, value, bit):
         return lax.ppermute(value, "head", pairs(self.heads, bit))
 
+    def round(self, block):
+        return self.along(block, 1), self.along(block, 2), lax.ppermute(block, "head", [(1, 2), (2, 1)])
+
+    def round_on(self, got):
+        near, far, last = got
+        return near, far, last + lax.ppermute(far, "head", [(1, 0), (2, 3)])
+
     def spread(self, block):
+        return block, self.side(block), self.other(block)
+
+    def corners(self, near):
+        block, from_side, from_other = near
         half = block.shape[0] // 2
-        from_side, from_other = self.side(block), self.other(block)
-        corner = (self.other(from_side[:half]), self.side(from_other[half:]))
-        near = (block, from_side, from_other) + corner
+        return self.other(from_side[:half]), self.side(from_other[half:])
+
+    def shared(self, near, corner):
+        near = near + corner
         return near[1:] + tuple(self.core(v) for v in near)
 
-    def total(self, keep, send, quarter):
-        both = keep + self.core(send)
+    def quarters(self, keep, send, quarter, *others):
+        both = keep + after(self.core(send), *others)
         rows = both.shape[0] // 4
-
-        def part(bits):
-            return lax.dynamic_slice_in_dim(both, (quarter ^ bits) * rows, rows, 0)
-
-        own = part(0) + self.side(part(2)) + self.other(part(1)) + self.corner(part(3))
-        near = (own, self.other(own), self.side(own), self.corner(own))
-        return near + tuple(self.core(v) for v in near)
-
-
-def pack_kernel(meta, qkv, out, bias, up, down, a_send, b_send):
-    rows = qkv.shape[1]
-    width = out.shape[1] // LANES
-    for j in range(3):
-        a_send[j * rows : (j + 1) * rows, :] = qkv[j]
+        return tuple(lax.dynamic_slice_in_dim(both, (quarter ^ bits) * rows, rows, 0) for bits in range(4))
+
+    def scatter(self, parts, *others):
+        moved = (self.side(parts[2]), self.other(parts[1]), self.corner(parts[3]))
+        moved = after(moved, *others)
+        return parts[0] + moved[0] + moved[1] + moved[2]
+
+    def rejoin(self, own):
+        return self.core(own), (self.other(own), self.side(own), self.corner(own))
+
+    def rejoin_on(self, own, crossed, near):
+        return (own,) + near + (crossed,) + tuple(self.core(v) for v in near)
+
+
+def after(value, *others):
+    return lax.optimization_barrier((value, others))[0]
+
+
+def pack_kernel(meta, qkv, out, bias, up, down, a_send, b_send, done):
+    place = meta[1]
+    places = 8
+    rows = qkv.shape[1] // places
+    few = out.shape[0] // places
+    moves = [(qkv.at[j, at(place * rows, rows), :], a_send.at[j * rows : (j + 1) * rows, :]) for j in range(3)]
     base = 3 * rows
-    few = out.shape[0]
-    for b in range(width):
-        a_send[base + b * few : base + (b + 1) * few, :] = out[:, b * LANES : (b + 1) * LANES]
-    base += width * few
-    a_send[base : base + bias.shape[0], :] = bias[...]
-    a_send[base + bias.shape[0] :, :] = jnp.zeros((a_send.shape[0] - base - bias.shape[0], LANES), F32)
-    b_send[: up.shape[0], :] = up[...]
-    base = up.shape[0]
-    few = down.shape[0]
-    for b in range(width):
-        b_send[base + b * few : base + (b + 1) * few, :] = down[:, b * LANES : (b + 1) * LANES]
-
-
-def pack(meta, qkv, out, bias, up, down, places):
+    for b in range(out.shape[1] // LANES):
+        lanes = slice(b * LANES, (b + 1) * LANES)
+        moves.append((out.at[at(place * few, few), lanes], a_send.at[base + b * few : base + (b + 1) * few, :]))
+    moves.append((bias, a_send.at[a_send.shape[0] - 8 : a_send.shape[0] - 2, :]))
+    base = up.shape[0] // places
+    moves.append((up.at[at(place * base, base), :], b_send.at[:base, :]))
+    few = down.shape[0] // places
+    for b in range(down.shape[1] // LANES):
+        lanes = slice(b * LANES, (b + 1) * LANES)
+        moves.append((down.at[at(place * few, few), lanes], b_send.at[base + b * few : base + (b + 1) * few, :]))
+    copies = [pltpu.make_async_copy(source, target, done.at[n]) for n, (source, target) in enumerate(moves)]
+    for copy in copies:
+        copy.start()
+    for copy in copies:
+        copy.wait()
+
+
+def pack(meta, qkv, out, bias, up, down):
+    places = 8
     width = out.shape[1]
-    a_rows = 4 * width // places + 8
-    b_rows = (up.shape[0] + down.shape[0] * width // LANES) // places
-    grid = pltpu.PrefetchScalarGridSpec(
-        num_scalar_prefetch=1,
-        grid=(1,),
-        in_specs=[
-            pl.BlockSpec((3, width // places, LANES), lambda i, m: (0, m[1], 0)),
-            pl.BlockSpec((LANES // places, width), lambda i, m: (m[1], 0)),
-            whole(bias),
-            pl.BlockSpec((up.shape[0] // places, LANES), lambda i, m: (m[1], 0)),
-            pl.BlockSpec((down.shape[0] // places, width), lambda i, m: (m[1], 0)),
-        ],
-        out_specs=[
-            pl.BlockSpec((a_rows, LANES), lambda i, m: (0, 0)),
-            pl.BlockSpec((b_rows, LANES), lambda i, m: (0, 0)),
-        ],
-    )
+    outs = [
+        shape((4 * width // places + 8, LANES)),
+        shape(((up.shape[0] + down.shape[0] * width // LANES) // places, LANES)),
+    ]
+    held = pl.BlockSpec(memory_space=pltpu.HBM)
     return pl.pallas_call(
         pack_kernel,
-        grid_spec=grid,
-        out_shape=[shape((a_rows, LANES)), shape((b_rows, LANES))],
+        grid_spec=pltpu.PrefetchScalarGridSpec(
+            num_scalar_prefetch=1,
+            grid=(1,),
+            in_specs=[held] * 5,
+            out_specs=[held] * 2,
+            scratch_shapes=[pltpu.SemaphoreType.DMA((5 + 2 * (width // LANES),))],
+        ),
+        out_shape=outs,
         compiler_params=params(),
         name="pack",
-    )(meta, qkv, out, bias, up, down)
+    )(meta, *(in_hbm(v) for v in (qkv, out, bias, up, down)))
 
 
 def gathered(meta, refs, first_refs):
@@ -299,10 +322,10 @@
     args = (tokens, norm) + tuple(weights) + tuple(first) + tuple(moved)
     in_specs = [pl.BlockSpec((BLOCK, width), lambda i, *_: (i, 0))] + [whole(a) for a in args[1:]]
     out_shape = [
-        shape((groups, rows, 3 * LANES), LOW),
-        shape((groups, rows // LANES, heads * LANES, LANES)),
-        shape((rows, width), LOW),
-        shape((rows, width)),
+        pltpu.HBM((groups, rows, 3 * LANES), LOW),
+        pltpu.HBM((groups, rows // LANES, heads * LANES, LANES), F32),
+        pltpu.HBM((rows, width), LOW),
+        pltpu.HBM((rows, width), F32),
     ]
     out_specs = [
         pl.BlockSpec((groups, BLOCK, 3 * LANES), lambda i, *_: (0, i, 0)),
@@ -327,7 +350,7 @@
             scratch_shapes=scratch,
         ),
         out_shape=out_shape,
-        compiler_params=params(),
+        compiler_params=params(32),
         cost_estimate=pl.CostEstimate(flops=flops, bytes_accessed=16 << 20, transcendentals=0),
         name="attention_forward",
     )(meta, lengths, *args)
@@ -474,7 +497,7 @@
         fixed += [shape((width, hidden)), shape((hidden, width))]
     else:
         half = hidden * width // LANES
-        fixed += [shape((half, LANES)), shape((half, LANES))]
+        fixed += [pltpu.HBM((half, LANES), F32), pltpu.HBM((half, LANES), F32)]
         scratch += [
             pltpu.VMEM((shards, width, hidden), LOW),
             pltpu.VMEM((shards, hidden, width), LOW),
@@ -492,32 +515,38 @@
             out_specs=[by_rows, by_rows] + [whole(f) for f in fixed],
             scratch_shapes=scratch,
         ),
-        out_shape=[shape((rows, width)), shape((rows, width))] + fixed,
-        compiler_params=params(),
+        out_shape=[pltpu.HBM((rows, width), F32), pltpu.HBM((rows, width), F32)] + fixed,
+        compiler_params=params(44),
         cost_estimate=pl.CostEstimate(flops=4 * flops, bytes_accessed=20 << 20, transcendentals=0),
         name="feed_both",
     )(meta, labels, tasks, *args)
 
 
-def pair_back(qkv, prob, context_back, masks):
-    query, key, value = (qkv[:, j * LANES : (j + 1) * LANES] for j in range(3))
-    seq_len = query.shape[0]
-    wide_back = stacked(context_back, masks)
-    prob_back = mul(wide_back, value, 1, 1)
-    value_back = mul(prob.astype(LOW), wide_back, 0, 0).astype(LOW)
-    inner = jnp.sum(prob * prob_back, -1, keepdims=True)
-    raw = (prob * (prob_back - inner) * (1.0 / math.sqrt(HEAD_DIM))).astype(LOW)
-    query_back = mul(side_by_side(raw, seq_len), stacked(key, masks)).astype(LOW)
-    key_back = mul(raw, stacked(query, masks), 0, 0).astype(LOW)
-    return query_back, key_back, value_back
-
-
-def group_back(low_back, qkv_ref, prob_ref, wout_rows, masks, store):
-    context_back = mul(low_back, wout_rows, 1, 1).astype(LOW)
-    for t in range(low_back.shape[0] // LANES):
-        part = slice(t * LANES, (t + 1) * LANES)
-        for j, grad in enumerate(pair_back(qkv_ref[part, :], prob_ref[t], context_back[part], masks)):
-            store(part, j, grad)
+def pairs_back(items, masks):
+    wide = [stacked(back, masks) for _, _, back in items]
+    prob_back = [mul(w, qkv[:, 2 * LANES :], 1, 1) for w, (qkv, _, _) in zip(wide, items)]
+    value_back = [mul(prob.astype(LOW), w, 0, 0).astype(LOW) for w, (_, prob, _) in zip(wide, items)]
+    inner = [jnp.sum(prob * b, -1, keepdims=True) for b, (_, prob, _) in zip(prob_back, items)]
+    raw = [
+        (prob * (b - n) * (1.0 / math.sqrt(HEAD_DIM))).astype(LOW) for b, n, (_, prob, _) in zip(prob_back, inner, items)
+    ]
+    query_back = [
+        mul(side_by_side(r, LANES), stacked(qkv[:, LANES : 2 * LANES], masks)).astype(LOW)
+        for r, (qkv, _, _) in zip(raw, items)
+    ]
+    key_back = [mul(r, stacked(qkv[:, :LANES], masks), 0, 0).astype(LOW) for r, (qkv, _, _) in zip(raw, items)]
+    return zip(query_back, key_back, value_back)
+
+
+def groups_back(low_back, sources, masks):
+    seqs = low_back.shape[0] // LANES
+    parts = [slice(t * LANES, (t + 1) * LANES) for t in range(seqs)]
+    backs = [mul(low_back, wout, 1, 1).astype(LOW) for _, _, wout, _ in sources]
+    for t, part in enumerate(parts):
+        items = [(qkv[part, :], prob[t], back[part]) for (qkv, prob, _, _), back in zip(sources, backs)]
+        for source, grads in zip(sources, pairs_back(items, masks)):
+            for j, grad in enumerate(grads):
+                source[3][part, j * LANES : (j + 1) * LANES] = grad
 
 
 def own_kernel(given, meta, back_ref, tokens, qkv, prob, context, wout, *refs):
@@ -537,10 +566,7 @@
     masks = head_masks()
     low_back = back_ref[...].astype(LOW)
 
-    def store(part, j, grad):
-        grads[part, j * LANES : (j + 1) * LANES] = grad
-
-    group_back(low_back, qkv.at[0], prob.at[0], wout[...], masks, store)
+    groups_back(low_back, [(qkv.at[0], prob.at[0], wout[...], grads)], masks)
     out_grad[...] += mul(context[...], low_back, 0, 0)
     both = grads[...]
     qkv_grad[...] += mul(tokens[...], both, 0, 0)
@@ -611,7 +637,7 @@
         pl.BlockSpec((BLOCK, LANES), lambda i, m: (i, m[3])),
         pl.BlockSpec((LANES, width), lambda i, m: (m[3], 0)),
     ] + [whole(s) for s in smalls]
-    out_shape = [shape((rows, 3 * LANES), LOW)]
+    out_shape = [pltpu.HBM((rows, 3 * LANES), LOW)]
     out_specs = [pl.BlockSpec((BLOCK, 3 * LANES), lambda i, m: (i, 0))]
     sums = [shape((width, 3 * LANES)), shape((LANES, width)), shape((8, LANES))]
     scratch = []
@@ -619,7 +645,7 @@
         fixed = sums
     else:
         count = packed_rows(width, *smalls[1].shape[:2])
-        fixed = [shape((count // 2, LANES))] * 2
+        fixed = [pltpu.HBM((count // 2, LANES), F32)] * 2
         scratch = [pltpu.VMEM(s.shape, F32) for s in sums] + [pltpu.VMEM((count, LANES), F32)]
     return pl.pallas_call(
         functools.partial(own_kernel, given),
@@ -631,26 +657,23 @@
             scratch_shapes=scratch,
         ),
         out_shape=out_shape + fixed,
-        compiler_params=params(),
+        compiler_params=params(28),
         cost_estimate=pl.CostEstimate(flops=4 << 30, bytes_accessed=8 << 20, transcendentals=0),
         name="attention_own",
-    )(meta, back, tokens, qkv, prob, context, wout, *smalls)
-
-
-def rest_kernel(meta, back_ref, qkv, prob, wout, wqkv, own, input_grad, grads):
+    )(meta, in_hbm(back), tokens, in_hbm(qkv), in_hbm(prob), in_hbm(context), wout, *smalls)
+
+
+def rest_kernel(meta, back_ref, qkv, prob, wout, wqkv, own, *refs):
+    input_grad, grads = refs[-2:]
     group = meta[3]
     groups = qkv.shape[0]
-    masks = head_masks()
     back = back_ref[...]
-    low_back = back.astype(LOW)
     grads[group] = own[...]
+    sources = []
     for r in range(1, groups):
         g = group ^ r
-
-        def store(part, j, grad, g=g):
-            grads[g, part, j * LANES : (j + 1) * LANES] = grad
-
-        group_back(low_back, qkv.at[g], prob.at[g], wout[at(g * LANES, LANES), :], masks, store)
+        sources.append((qkv.at[g], prob.at[g], wout[at(g * LANES, LANES), :], grads.at[g]))
+    groups_back(back.astype(LOW), sources, head_masks())
     total = None
     for g in range(groups):
         term = mul(grads[g], wqkv[g], 1, 1)
@@ -658,74 +681,91 @@
     input_grad[...] = back + total
 
 
-def run_rest(meta, back, qkv, prob, wout, wqkv, own):
+def run_rest(meta, back, qkv, prob, wout, wqkv, own, block, before=None):
     rows, width = back.shape
     groups = width // LANES
-    seqs = BLOCK // LANES
+    few = BLOCK // 2
+    seqs = few // LANES
     heads = LANES // HEAD_DIM
-    by_rows = pl.BlockSpec((BLOCK, width), lambda i, m: (i, 0))
+    by_rows = pl.BlockSpec((few, width), lambda i, m: (2 * block + i, 0))
+    held = () if before is None else (before,)
     return pl.pallas_call(
         rest_kernel,
         grid_spec=pltpu.PrefetchScalarGridSpec(
             num_scalar_prefetch=1,
-            grid=(rows // BLOCK,),
+            grid=(2,),
             in_specs=[
                 by_rows,
-                pl.BlockSpec((groups, BLOCK, 3 * LANES), lambda i, m: (0, i, 0)),
-                pl.BlockSpec((groups, seqs, heads * LANES, LANES), lambda i, m: (0, i, 0, 0)),
+                pl.BlockSpec((groups, few, 3 * LANES), lambda i, m: (0, 2 * block + i, 0)),
+                pl.BlockSpec((groups, seqs, heads * LANES, LANES), lambda i, m: (0, 2 * block + i, 0, 0)),
                 whole(wout),
                 whole(wqkv),
-                pl.BlockSpec((BLOCK, 3 * LANES), lambda i, m: (i, 0)),
-            ],
+                pl.BlockSpec((few, 3 * LANES), lambda i, m: (2 * block + i, 0)),
+            ]
+            + [pl.BlockSpec(memory_space=pl.ANY)] * len(held),
             out_specs=by_rows,
-            scratch_shapes=[pltpu.VMEM((groups, BLOCK, 3 * LANES), LOW)],
+            scratch_shapes=[pltpu.VMEM((groups, few, 3 * LANES), LOW)],
         ),
         out_shape=shape((rows, width)),
-        compiler_params=params(),
-        cost_estimate=pl.CostEstimate(flops=8 << 30, bytes_accessed=12 << 20, transcendentals=0),
+        input_output_aliases={7: 0} if held else {},
+        compiler_params=params(28),
+        cost_estimate=pl.CostEstimate(flops=8 << 30, bytes_accessed=8 << 20, transcendentals=0),
         name="attention_rest",
-    )(meta, back, qkv, prob, wout, wqkv, own)
-
-
-def collect_kernel(split_rows, meta, *refs):
-    parts, full, squares = refs[:8], refs[8], refs[9]
+    )(meta, in_hbm(back), in_hbm(qkv), in_hbm(prob), wout, wqkv, in_hbm(own), *held)
+
+
+def places_of(meta):
+    return [(meta[2] ^ half) * 4 + (meta[4] ^ bits) for half in range(2) for bits in range(4)]
+
+
+def squares_kernel(split_rows, meta, *refs):
+    parts, before, out, sums = refs[:8], refs[8:-2], refs[-2], refs[-1]
     rows = parts[0].shape[0]
-    for half in range(2):
-        for bits in range(4):
-            place = (meta[2] ^ half) * 4 + (meta[4] ^ bits)
-            full[pl.ds(pl.multiple_of(place * rows, 8), rows), :] = parts[half * 4 + bits][...]
-    squares[...] = jnp.zeros_like(squares)
-    head = full[:split_rows, :]
-    squares[0:1, :] = jnp.sum(head * head, 0, keepdims=True)
-    if split_rows < full.shape[0]:
-        tail = full[split_rows:, :]
-        squares[1:2, :] = jnp.sum(tail * tail, 0, keepdims=True)
-
-
-def collect(meta, parts, split_rows=None):
-    rows = 8 * parts[0].shape[0]
-    outs = [shape((rows, LANES)), shape((8, LANES))]
+    row = lax.broadcasted_iota(jnp.int32, (rows, LANES), 0)
+    for place, part in zip(places_of(meta), parts):
+        square = part[...] * part[...]
+        if split_rows < 8 * rows:
+            is_split = row < split_rows - place * rows
+            sums[place, 1:2, :] = jnp.sum(jnp.where(is_split, 0.0, square), 0, keepdims=True)
+            square = jnp.where(is_split, square, 0.0)
+        sums[place, 0:1, :] = jnp.sum(square, 0, keepdims=True)
+    out[...] = jnp.zeros_like(out)
+    for kind in range(1 if split_rows == 8 * rows else 2):
+        total = before[0][kind : kind + 1, :] if before else None
+        for n in range(8):
+            term = sums[n, kind : kind + 1, :]
+            total = term if total is None else total + term
+        out[kind : kind + 1, :] = total
+
+
+def squares_of(meta, parts, split_rows=None, before=()):
+    out = shape((8, LANES))
     return pl.pallas_call(
-        functools.partial(collect_kernel, split_rows or rows),
+        functools.partial(squares_kernel, split_rows or 8 * parts[0].shape[0]),
         grid_spec=pltpu.PrefetchScalarGridSpec(
             num_scalar_prefetch=1,
             grid=(1,),
-            in_specs=[whole(p) for p in parts],
-            out_specs=[whole(o) for o in outs],
+            in_specs=[whole(p) for p in tuple(parts) + before],
+            out_specs=whole(out),
+            scratch_shapes=[pltpu.VMEM((8, 8, LANES), F32)],
         ),
-        out_shape=outs,
-        compiler_params=params(),
-        name="collect",
-    )(meta, *parts)
+        out_shape=out,
+        compiler_params=params(16),
+        name="squares",
+    )(meta, *parts, *before)
 
 
 def adam_kernel(count, meta, squares, *refs):
     moved = refs[:count]
-    a_full, b_full = refs[count : count + 2]
-    states = refs[count + 2 : count + 23]
-    norm_ref = refs[count + 23]
-    outs = refs[count + 24 : count + 45]
-    sums = refs[count + 45]
+    a_parts, b_parts = refs[count : count + 8], refs[count + 8 : count + 16]
+    refs = refs[count + 16 :]
+    states, norm_ref, targets = refs[:21], refs[21], refs[22:43]
+    sums, a_full, b_full, done = refs[43:47]
+    outs = refs[47:]
+    for parts, full in ((a_parts, a_full), (b_parts, b_full)):
+        rows = parts[0].shape[0]
+        for place, part in zip(places_of(meta), parts):
+            full[pl.ds(pl.multiple_of(place * rows, 8), rows), :] = part[...]
     sums[meta[0]] = squares[...]
     for r in range(1, count + 1):
         sums[meta[0] ^ r] = moved[r - 1][...]
@@ -738,24 +778,46 @@
     factor = jnp.minimum(1.0, clip_at / (grad_norm + 1e-06))
     width = states[5 * 3].shape[1]
     blocks = width // LANES
+    copies = []
 
     def update(index, where, grad, with_decay):
         first, second, weight = (states[3 * index + j][where] for j in range(3))
         for j, value in enumerate(adam_math(weight, first, second, grad, factor, with_decay)):
             outs[3 * index + j][where] = value
 
+    def give(index, where=None):
+        for j in range(3 * index, 3 * index + 3):
+            source, target = outs[j], targets[j]
+            if where is not None:
+                source, target = source.at[where], target.at[where]
+            copies.append(pltpu.make_async_copy(source, target, done.at[len(copies)]))
+            copies[-1].start()
+
+    rows = 4 * width
+    for b in range(blocks):
+        part = slice(b * width, (b + 1) * width)
+        update(2, (part, slice(None)), b_full[part, :], True)
+        give(2, part)
+    for b in range(blocks):
+        lanes = slice(b * LANES, (b + 1) * LANES)
+        update(3, (slice(None), lanes), b_full[rows + b * 4 * LANES : rows + (b + 1) * 4 * LANES, :], True)
+        give(3, (slice(None), lanes))
     for j in range(3):
         update(0, (j,), a_full[j * width : (j + 1) * width, :], True)
+        give(0, j)
     base = 3 * width
     for b in range(blocks):
         lanes = slice(b * LANES, (b + 1) * LANES)
         update(1, (slice(None), lanes), a_full[base + b * LANES : base + (b + 1) * LANES, :], True)
+    give(1)
     base += width
     update(4, (slice(None), slice(None)), a_full[base : base + 6, :], False)
+    give(4)
     base += 8
     for b in range(blocks):
         lanes = slice(b * LANES, (b + 1) * LANES)
         update(5, (slice(None), lanes), a_full[base + 8 * b : base + 8 * b + 6, :], False)
+    give(5)
     base += 8 * blocks
     tasks, kinds, _ = states[6 * 3].shape
     each = small_rows(tasks, kinds)
@@ -764,36 +826,40 @@
         for t in range(tasks):
             row = base + each * b + kinds * t
             update(6, (t, slice(None), lanes), a_full[row : row + kinds, :], True)
-    rows = 4 * width
-    update(2, (slice(None), slice(None)), b_full[:rows, :], True)
-    for b in range(blocks):
-        lanes = slice(b * LANES, (b + 1) * LANES)
-        update(3, (slice(None), lanes), b_full[rows + b * 4 * LANES : rows + (b + 1) * 4 * LANES, :], True)
-
-
-def run_adam(meta, squares, moved, a_full, b_full, states):
-    outs = [shape((1, 1))] + [shape(s.shape) for s in states]
-    args = (squares,) + tuple(moved) + (a_full, b_full) + tuple(states)
+    give(6)
+    for copy in copies:
+        copy.wait()
+
+
+def run_adam(meta, squares, moved, a_parts, b_parts, states):
+    held = pl.BlockSpec(memory_space=pltpu.HBM)
+    here = pl.BlockSpec(memory_space=pltpu.VMEM)
+    blocks = states[-4].shape[1] // LANES
+    args = (squares,) + tuple(moved) + tuple(a_parts) + tuple(b_parts)
     return pl.pallas_call(
         functools.partial(adam_kernel, len(moved)),
-        grid_spec=pltpu.PrefetchScalarGridSpec(
-            num_scalar_prefetch=1,
-            grid=(1,),
-            in_specs=[whole(a) for a in args],
-            out_specs=[whole(o) for o in outs],
-            scratch_shapes=[pltpu.VMEM((len(moved) + 1, 8, LANES), F32)],
-        ),
-        out_shape=outs,
-        compiler_params=params(),
+        in_specs=[pl.BlockSpec(memory_space=pltpu.SMEM)] + [here] * (len(args) + len(states)),
+        out_specs=[here] + [held] * len(states),
+        out_shape=[shape((1, 1))] + [shape(s.shape) for s in states],
+        scratch_shapes=[
+            pltpu.VMEM((len(moved) + 1, 8, LANES), F32),
+            pltpu.VMEM((8 * a_parts[0].shape[0], LANES), F32),
+            pltpu.VMEM((8 * b_parts[0].shape[0], LANES), F32),
+            pltpu.SemaphoreType.DMA((6 * blocks + 3 * 3 + 3 * 4,)),
+        ]
+        + [pltpu.VMEM(s.shape, F32) for s in states],
+        compiler_params=params(18),
         name="adam",
-    )(meta, *args)
+    )(meta, *args, *(s if n % 3 == 2 else in_vmem(s) for n, s in enumerate(states)))
 
 
 def shares(mesh, *args):
     fast = (
-        mesh.shape["batch"] == 4
+        mesh.shape["head"] == 4
+        and mesh.shape["batch"] == 4
         and mesh.shape["rep"] == 2
         and args[5].shape[2] == LANES
+        and args[0].shape[0] == 2 * BLOCK
         and mesh.shape["head"] * LANES == args[0].shape[1]
     )
     return (by_permutes if fast else by_gathers)(mesh, *args)
@@ -846,16 +912,21 @@
         return jnp.transpose(value, (0, 2, 1))
 
     up_flat, down_flat, classes = flat_up(up_weight), flat_down(down_weight), flat_class(class_weight)
-    a_send, b_send = pack(meta, qkv_weight, out_weight, split_bias, up_flat, down_flat, plane.batch * plane.rep)
+    a_send, b_send = pack(meta, qkv_weight, out_weight, split_bias, up_flat, down_flat)
     turns = range(1, plane.heads)
     a_first = [plane.along(a_send, r) for r in turns]
-    b_first = [plane.along(b_send, r) for r in turns]
-    a_moved = plane.spread(jnp.concatenate([v[:-8] for v in a_first], 0))
-    b_moved = plane.spread(jnp.concatenate(b_first, 0))
+    b_first = plane.round(b_send)
+    a_near = plane.spread(after(jnp.concatenate([v[:-8] for v in a_first], 0), b_first[0]))
+    b_first = plane.round_on(b_first)
+    a_corner = plane.corners(a_near)
+    b_near = plane.spread(after(jnp.concatenate(b_first, 0), a_near))
+    a_moved = plane.shared(a_near, a_corner)
 
     qkv, prob, context, pre_one, wqkv, wout = run_attention_forward(
         meta, lengths, tokens_in, norm_params, (qkv_weight, out_weight, split_bias), a_first, a_moved, False
     )
+    b_near = after(b_near, pre_one)
+    b_moved = plane.shared(b_near, plane.corners(b_near))
     output, back_one, norm_grad, class_grad, up_bias_grad, b_keep, b_give = run_feed(
         meta,
         labels,
@@ -870,13 +941,23 @@
         b_moved,
         False,
     )
+    b_parts = plane.quarters(b_keep, b_give, quarter)
+    back_one = after(back_one, b_parts)
     own, a_keep, a_give = run_own(
         meta, back_one, tokens_in, qkv, prob, context, wout, (norm_grad, class_grad, up_bias_grad), False
     )
-    input_grad = run_rest(meta, back_one, qkv, prob, wout, wqkv, own)
-    b_full, b_squares = collect(meta, plane.total(b_keep, b_give, quarter))
-    a_full, a_squares = collect(meta, plane.total(a_keep, a_give, quarter), 4 * width + 8)
-    squares = a_squares + b_squares
+    b_own = plane.scatter(b_parts, a_give)
+    b_crossed, b_near = plane.rejoin(b_own)
+    a_parts = plane.quarters(a_keep, a_give, quarter)
+    back_one = after(back_one, a_parts, b_crossed)
+    input_grad = run_rest(meta, back_one, qkv, prob, wout, wqkv, own, 0)
+    b_parts = plane.rejoin_on(b_own, b_crossed, after(b_near, input_grad))
+    a_own = plane.scatter(a_parts, input_grad)
+    a_crossed, a_near = plane.rejoin(a_own)
+    input_grad = run_rest(meta, after(back_one, a_crossed), qkv, prob, wout, wqkv, own, 1, input_grad)
+    a_parts = plane.rejoin_on(a_own, a_crossed, after(a_near, input_grad))
+    squares = squares_of(meta, a_parts, 4 * width + 8, (squares_of(meta, b_parts),))
+    moved = tuple(plane.along(squares, r) for r in turns)
     states = (
         (qkv_first, qkv_second, qkv_weight)
         + (out_first, out_second, out_weight)
@@ -886,11 +967,23 @@
         + (norm_first, norm_second, norm_params)
         + (flat_class(class_first), flat_class(class_second), classes)
     )
-    grad_norm, *new = run_adam(meta, squares, [plane.along(squares, r) for r in turns], a_full, b_full, states)
+    grad_norm, *new = run_adam(meta, squares, moved, a_parts, b_parts, states)
     new[6:9] = [v.reshape(up_weight.shape) for v in new[6:9]]
     new[9:12] = [v.reshape(down_weight.shape) for v in new[9:12]]
     new[18:21] = [jnp.transpose(v, (0, 2, 1)) for v in new[18:21]]
     return (output, input_grad, grad_norm[0, 0]) + tuple(new)
+
+
+def lower_kernel(source, target):
+    target[...] = source[...].astype(LOW)
+
+
+def lowered(value):
+    flat = value.reshape(-1, value.shape[-1])
+    out = pl.pallas_call(
+        lower_kernel, out_shape=shape(flat.shape, LOW), compiler_params=params(), name="lowered"
+    )(flat)
+    return out.reshape(value.shape)
 
 
 def by_gathers(
@@ -934,11 +1027,8 @@
     full_up = lax.all_gather(up_weight.reshape(width, hidden), "head", axis=0)
     full_down = lax.all_gather(down_weight.reshape(hidden, width), "head", axis=0)
     full_bias = lax.all_gather(split_bias, "head", axis=1, tiled=True)
-    full_qkv, full_out, full_up, full_down, full_bias = lax.optimization_barrier(
-        (full_qkv, full_out, full_up, full_down, full_bias)
-    )
-    wqkv = full_qkv.reshape(3, width, groups, LANES).transpose(2, 1, 0, 3).reshape(groups, width, 3 * LANES).astype(LOW)
-    wout = full_out.astype(LOW)
+    wqkv = full_qkv.reshape(3, width, groups, LANES).transpose(2, 1, 0, 3).reshape(groups, width, 3 * LANES)
+    wqkv, wout = lowered(wqkv), lowered(full_out)
     qv_bias = jnp.pad(full_bias[:2].reshape(2, groups, LANES).transpose(1, 0, 2), ((0, 0), (0, 6), (0, 0)))
     shards = width // cols
     up_bias = full_bias[2:].reshape(4, shards, cols).transpose(1, 0, 2).reshape(shards, 1, hidden)
@@ -956,14 +1046,16 @@
         out_grad,
         norm_params,
         classes,
-        (full_up.astype(LOW), full_down.astype(LOW), up_bias),
+        (lowered(full_up), lowered(full_down), up_bias),
         (),
         (),
         (),
         True,
     )
     own, qkv_grad, out_w_grad, split_grad = run_own(meta, back_one, tokens_in, qkv, prob, context, wout, (), True)
-    input_grad = run_rest(meta, back_one, qkv, prob, wout, wqkv, own)
+    input_grad = None
+    for block in range(tokens_in.shape[0] // BLOCK):
+        input_grad = run_rest(meta, back_one, qkv, prob, wout, wqkv, own, block, input_grad)
     start = here * cols % LANES
     qkv_grad = qkv_grad.reshape(width, 3, LANES).transpose(1, 0, 2)
     qkv_grad = lax.dynamic_slice_in_dim(qkv_grad, start, cols, 2)

time: 212 us -> 171 us (0.81)
  Pallas kernels: 77.7 us -> 59.9 us
  waiting for transfers between devices: 74.1 us -> 61.4 us
  local copies, waits for them, and re-layouts: 7.94 us -> 1.92 us
    ppermute x8, waiting for transfers between devices: 33.4 us -> 17.4 us  [other(): return lax.ppermute(value, 'rep', pairs(self.rep, 1))]
    pallas_call x1, Pallas kernels: 27.2 us -> 19.8 us  [run_feed(): pl.pallas_call(functools.partial(feed_kernel, len(first), given), grid_sp...]
    ppermute x0 -> x2, waiting for transfers between devices: none -> 7.15 us  [the longest x1 7.14 us: round_on(): return (near, far, last + lax.ppermute(far, 'head', [(1, 0), (2, 3)]))]
    pallas_call x4, Pallas kernels: 17.3 us -> 11 us  [the longest x1 7.71 us: run_adam(): pl.pallas_call(functools.partial(adam_kernel, len(moved)), in_specs=[pl.B...]
    ppermute x4, waiting for transfers between devices: 11.2 us -> 5.12 us  [corner(): lax.ppermute(value, ('batch', 'rep'), pairs(self.batch * self.rep, 2 * se...]
    ppermute x9 -> x8, starting transfers between devices: 19.1 us -> 13.6 us  [along(): return lax.ppermute(value, 'head', pairs(self.heads, bit))]
    unnamed x72 -> x68, local copies, waits for them, and re-layouts: 6.17 us -> 1.59 us
    pallas_call x1, Pallas kernels: 12.3 us -> 8.48 us  [run_attention_forward(): pl.pallas_call(functools.partial(attention_forward, len(first), given), g...]
  transfers between devices with their start and end apart: 49 -> 50, of which waited for: 18 -> 22; matrix products, arithmetic and copies ran while one was open for 3% -> 1% of each run, Pallas kernels for 16% -> 17%
where the time goes in v2:
time: 171 us
  waiting for transfers between devices  61.4 us (36%)
  Pallas kernels  59.9 us (35%)
  starting transfers between devices  42.9 us (25%)
  other arithmetic  3.29 us (2%)
  local copies, waits for them, and re-layouts  1.92 us (1%)
    ppermute x8, waiting for transfers between devices, along(): return lax.ppermute(value, 'head', pairs(self.heads, bit))  23 us
    pallas_call x1, Pallas kernels, run_feed(): pl.pallas_call(functools.partial(feed_kernel, len(first), given), grid_sp...  19.8 us
    ppermute x8, waiting for transfers between devices, other(): return lax.ppermute(value, 'rep', pairs(self.rep, 1))  17.4 us
    pallas_call x2, Pallas kernels, run_rest(): pl.pallas_call(rest_kernel, grid_spec=pltpu.PrefetchScalarGridSpec(num_sc...  13.7 us
    ppermute x8, starting transfers between devices, along(): return lax.ppermute(value, 'head', pairs(self.heads, bit))  13.6 us
    ppermute x8, starting transfers between devices, side(): return lax.ppermute(value, 'batch', pairs(self.batch, 2))  10.5 us
    ppermute x8, starting transfers between devices, other(): return lax.ppermute(value, 'rep', pairs(self.rep, 1))  8.51 us
    pallas_call x1, Pallas kernels, run_attention_forward(): pl.pallas_call(functools.partial(attention_forward, len(first), given), g...  8.48 us
  transfers between devices with their start and end apart: 50, of which 22 were waited for; matrix products, arithmetic and copies ran while one was open for 1% of the time, Pallas kernels for 17%

profile of v2, /device:TPU:0, one launch (start us, length us, event | category | flops | bytes accessed | tf_op | source)
XLA Modules:
  0.0 171.0 jit_solution(11369893376758511475)
XLA Ops:
  0.8 1.7 pack.1
  2.5 3.1 %collective-permute-start.3 = (f32[512,128]{1,0:T(8,128)S(1)}, f32[512,128]{1,0:T(8,128)S(1)}, u32[]{:S(2)}, u32[]{:S(2)}) collective-permute-start(f32[512,128]{1,0:T(8,128)S(1)} %get-tuple-element.85), channel_id=1, source_target_pairs={{0,8},{8,0},{16,24},{24,16},{1,9},{9,1},{17,25},{25,17},{2,10},{10... | collective-permute-start | bytes 786440 | tf_op jit(solution)/shard_map/ppermute | solution.py:124
  5.7 3.0 %collective-permute-start.1 = (f32[264,128]{1,0:T(8,128)S(1)}, f32[264,128]{1,0:T(8,128)S(1)}, u32[]{:S(2)}, u32[]{:S(2)}) collective-permute-start(f32[264,128]{1,0:T(8,128)S(1)} %get-tuple-element.84), channel_id=1, source_target_pairs={{0,16},{8,24},{16,0},{24,8},{1,17},{9,25},{17,1},{25,9},{2,18},{10... | collective-permute-start | bytes 405512 | tf_op jit(solution)/shard_map/ppermute | solution.py:124
  10.0 1.7 collective-permute-start.13
  11.7 10.5 %collective-permute-done.refs_5_.refs_7_ = f32[264,128]{1,0:T(8,128)S(1)} collective-permute-done((f32[264,128]{1,0:T(8,128)S(1)}, f32[264,128]{1,0:T(8,128)S(1)}, u32[]{:S(2)}, u32[]{:S(2)}) %collective-permute-start) | collective-permute-done | bytes 135200 | tf_op jit(solution)/shard_map/ppermute | solution.py:124
  22.2 1.8 %collective-permute-done.2.refs_7_.refs_9_ = f32[264,128]{1,0:T(8,128)S(1)} collective-permute-done((f32[264,128]{1,0:T(8,128)S(1)}, f32[264,128]{1,0:T(8,128)S(1)}, u32[]{:S(2)}, u32[]{:S(2)}) %collective-permute-start.2) | collective-permute-done | bytes 135200 | tf_op jit(solution)/shard_map/ppermute | solution.py:124
  24.1 1.6 collective-permute-start.4
  25.6 1.5 collective-permute-start.5
  27.8 5.4 %collective-permute-done.13.refs_11_ = f32[512,128]{1,0:T(8,128)S(1)} collective-permute-done((f32[512,128]{1,0:T(8,128)S(1)}, f32[512,128]{1,0:T(8,128)S(1)}, u32[]{:S(2)}, u32[]{:S(2)}) %collective-permute-start.13) | collective-permute-done | bytes 262176 | tf_op jit(solution)/shard_map/ppermute | solution.py:124
  34.6 7.1 %collective-permute-done.15 = f32[512,128]{1,0:T(8,128)S(1)} collective-permute-done((f32[512,128]{1,0:T(8,128)S(1)}, f32[512,128]{1,0:T(8,128)S(1)}, u32[]{:S(2)}, u32[]{:S(2)}) %collective-permute-start.15) | collective-permute-done | bytes 262176 | tf_op jit(solution)/shard_map/ppermute | solution.py:131
  43.1 1.6 collective-permute-start.7
  46.1 3.5 %collective-permute-done.6.refs_10_ = f32[384,128]{1,0:T(8,128)S(1)} collective-permute-done((f32[384,128]{1,0:T(8,128)S(1)}, f32[384,128]{1,0:T(8,128)S(1)}, u32[]{:S(2)}, u32[]{:S(2)}) %collective-permute-start.6) | collective-permute-done | bytes 196640 | tf_op jit(solution)/shard_map/ppermute | solution.py:118
  51.5 1.5 collective-permute-done.12.refs_16_
  53.1 8.5 %attention_forward.1 = (bf16[4,1024,384]{2,1,0:T(8,128)(2,1)}, f32[4,8,256,128]{3,2,1,0:T(8,128)}, bf16[1024,512]{1,0:T(8,128)(2,1)}, f32[1024,512]{1,0:T(8,128)...) custom-call(s32[5]{0:T(128)S(1)} %stack.20.meta, s32[8]{0:T(128)S(1)} %copy-done.24, ...), custom_call_target="tpu_custom_call" | custom-call | flops 2684354560 | bytes 16777216 | tf_op jit(solution)/shard_map/attention_forward/pallas_call | solution.py:343
  63.3 1.8 %collective-permute-start.19 = (f32[768,128]{1,0:T(8,128)S(1)}, f32[768,128]{1,0:T(8,128)S(1)}, u32[]{:S(2)}, u32[]{:S(2)}) collective-permute-start(f32[768,128]{1,0:T(8,128)S(1)} %slice.27), channel_id=1, source_target_pairs={{0,4},{2,6},{4,0},{6,2},{1,5},{3,7},{5,1},{7,3},{8,12},{10,14},{12... | collective-permute-start | bytes 1179656 | tf_op jit(solution)/shard_map/ppermute | solution.py:115
  65.6 8.0 %collective-permute-done.18.refs_15_ = f32[768,128]{1,0:T(8,128)S(1)} collective-permute-done((f32[768,128]{1,0:T(8,128)S(1)}, f32[768,128]{1,0:T(8,128)S(1)}, u32[]{:S(2)}, u32[]{:S(2)}) %collective-permute-start.18) | collective-permute-done | bytes 393248 | tf_op jit(solution)/shard_map/ppermute | solution.py:118
  76.1 19.8 %feed_both.1 = (f32[1024,512]{1,0:T(8,128)}, f32[1024,512]{1,0:T(8,128)}, f32[8,512]{1,0:T(8,128)S(1)}, f32[9,3,512]{2,1,0:T(4,128)S(1)}, f32[8,512]{1,0:T(8,128...) custom-call(s32[5]{0:T(128)S(1)} %stack.20.meta, s32[8]{0:T(128)S(1)} %copy-done.25, s32[8]{0:T(128)S(1)} %copy-done.26, ...), custom_call_target="tpu_custom_call" | custom-call | flops 38654705664 | bytes 20971520 | tf_op jit(solution)/shard_map/feed_both/pallas_call | solution.py:509
  96.6 2.9 %collective-permute-done.25 = f32[2048,128]{1,0:T(8,128)} collective-permute-done((f32[2048,128]{1,0:T(8,128)}, f32[2048,128]{1,0:T(8,128)}, u32[]{:S(2)}, u32[]{:S(2)}) %collective-permute-start.25) | collective-permute-done | bytes 1048608 | tf_op jit(solution)/shard_map/ppermute | solution.py:112
  99.5 1.8 %add.66 = f32[2048,128]{1,0:T(8,128)S(1)} add(f32[2048,128]{1,0:T(8,128)} %get-tuple-element.94, f32[2048,128]{1,0:T(8,128)} %collective-permute-done.25) | non-fusion elementwise | flops 262144 | bytes 3145728 | tf_op jit(solution)/shard_map/add | solution.py:146
  101.4 1.6 collective-permute-start.27
  105.0 6.9 %attention_own.1 = (bf16[1024,384]{1,0:T(8,128)(2,1)}, f32[1120,128]{1,0:T(8,128)}, f32[1120,128]{1,0:T(8,128)}) custom-call(s32[5]{0:T(128)S(1)} %stack.20.meta, f32[1024,512]{1,0:T(8,128)} %get-tuple-element.115.back_ref, bf16[1024,512]{1,0:T(8,128)(2,1)S(1)} %copy-done.23, bf16[4,1024,384]{2,1,0:T(8,128)(2,1)} %get-tuple-element.97.qkv, ...), custom_call_target="tpu_custom_call" | custom-call | flops 4294967296 | bytes 8388608 | tf_op jit(solution)/shard_map/attention_own/pallas_call | solution.py:650
  111.9 4.8 %collective-permute-done.28 = f32[512,128]{1,0:T(8,128)S(1)} collective-permute-done((f32[512,128]{1,0:T(8,128)S(1)}, f32[512,128]{1,0:T(8,128)S(1)}, u32[]{:S(2)}, u32[]{:S(2)}) %collective-permute-start.28) | collective-permute-done | bytes 262176 | tf_op jit(solution)/shard_map/ppermute | solution.py:118
  120.0 1.5 collective-permute-start.31
  123.6 6.7 %attention_rest.2.refs_0_ = f32[1024,512]{1,0:T(8,128)} custom-call(s32[5]{0:T(128)S(1)} %stack.20.meta, f32[1024,512]{1,0:T(8,128)} %get-tuple-element.115.back_ref, bf16[4,1024,384]{2,1,0:T(8,128)(2,1)} %get-tuple-element.97.qkv, f32[4,8,256,128]{3,2,1,0:T(8,128)} %get-tuple-element.98.prob, bf16[512,512]{1,0:T(8,128)(2,1)S(1)} %copy-done.31, ...), custom_call_target="tpu_custom_call" | custom-call | flops 8589934592 | bytes 8388608 | tf_op jit(solution)/shard_map/attention_rest/pallas_call | solution.py:692
  130.3 1.7 %collective-permute-start.43 = (f32[512,128]{1,0:T(8,128)S(1)}, f32[512,128]{1,0:T(8,128)S(1)}, u32[]{:S(2)}, u32[]{:S(2)}) collective-permute-start(f32[512,128]{1,0:T(8,128)S(1)} %add_add_fusion.refs_0_.refs_11_), channel_id=1, source_target_pairs={{0,5},{1,4},{2,7},{3,6},{4,1},{5,0},{6,3},{7,2},{8,13},{9,12},{10,... | collective-permute-start | bytes 786440 | tf_op jit(solution)/shard_map/ppermute | solution.py:121
  134.2 4.4 %collective-permute-done.43.refs_3_.refs_14_ = f32[512,128]{1,0:T(8,128)S(1)} collective-permute-done((f32[512,128]{1,0:T(8,128)S(1)}, f32[512,128]{1,0:T(8,128)S(1)}, u32[]{:S(2)}, u32[]{:S(2)}) %collective-permute-start.43) | collective-permute-done | bytes 262176 | tf_op jit(solution)/shard_map/ppermute | solution.py:121
  141.5 1.7 collective-permute-start.37
  143.3 7.0 %attention_rest.3 = f32[1024,512]{1,0:T(8,128)} custom-call(s32[5]{0:T(128)S(1)} %stack.20.meta, f32[1024,512]{1,0:T(8,128)} %get-tuple-element.115.back_ref, bf16[4,1024,384]{2,1,0:T(8,128)(2,1)} %get-tuple-element.97.qkv, f32[4,8,256,128]{3,2,1,0:T(8,128)} %get-tuple-element.98.prob, ...), custom_call_target="tpu_custom_call", output_to_operand_aliasing={{}: (7, {})} | custom-call | flops 8589934592 | bytes 8388608 | tf_op jit(solution)/shard_map/attention_rest/pallas_call | solution.py:692
  153.3 4.3 %collective-permute-start.48 = (f32[8,128]{1,0:T(8,128)S(1)}, f32[8,128]{1,0:T(8,128)S(1)}, u32[]{:S(2)}, u32[]{:S(2)}) collective-permute-start(f32[8,128]{1,0:T(8,128)S(1)} %squares.3), channel_id=1, source_target_pairs={{0,16},{8,24},{16,0},{24,8},{1,17},{9,25},{17,1},{25,9},{2,18},{10... | collective-permute-start | bytes 12296 | tf_op jit(solution)/shard_map/ppermute | solution.py:124
  157.6 1.6 collective-permute-done.48.refs_1_
  159.2 3.8 %collective-permute-done.49.refs_2_ = f32[8,128]{1,0:T(8,128)S(1)} collective-permute-done((f32[8,128]{1,0:T(8,128)S(1)}, f32[8,128]{1,0:T(8,128)S(1)}, u32[]{:S(2)}, u32[]{:S(2)}) %collective-permute-start.49) | collective-permute-done | bytes 4128 | tf_op jit(solution)/shard_map/ppermute | solution.py:124
  163.2 7.7 %adam.1 = (f32[1,1]{1,0:T(1,128)}, f32[3,512,128]{2,1,0:T(8,128)}, f32[3,512,128]{2,1,0:T(8,128)}, f32[3,512,128]{2,1,0:T(8,128)}, f32[128,512]{1,0:T(8,128)}, /...) custom-call(s32[5]{0:T(128)S(1)} %stack.20.meta, ...), custom_call_target="tpu_custom_call" | custom-call | tf_op jit(solution)/shard_map/adam/pallas_call | solution.py:839
  (162 shorter events, 29.3 us)
Async XLA Ops:
  2.5 21.6 %collective-permute-start.3 = (f32[512,128]{1,0:T(8,128)S(1)}, f32[512,128]{1,0:T(8,128)S(1)}, u32[]{:S(2)}, u32[]{:S(2)}) collective-permute-start(f32[512,128]{1,0:T(8,128)S(1)} %get-tuple-element.85), channel_id=1, source_target_pairs={{0,8},{8,0},{16,24},{24,16},{1,9},{9,1},{17,25},{25,17},{2,10},{10... | collective-permute-start | bytes 786440 | tf_op jit(solution)/shard_map/ppermute | solution.py:124
  5.6 16.5 %collective-permute-start = (f32[264,128]{1,0:T(8,128)S(1)}, f32[264,128]{1,0:T(8,128)S(1)}, u32[]{:S(2)}, u32[]{:S(2)}) collective-permute-start(f32[264,128]{1,0:T(8,128)S(1)} %get-tuple-element.84), channel_id=1, source_target_pairs={{0,8},{8,0},{16,24},{24,16},{1,9},{9,1},{17,25},{25,17},{2,10},{10... | collective-permute-start | bytes 405512 | tf_op jit(solution)/shard_map/ppermute | solution.py:124
  5.7 16.5 %collective-permute-start.1 = (f32[264,128]{1,0:T(8,128)S(1)}, f32[264,128]{1,0:T(8,128)S(1)}, u32[]{:S(2)}, u32[]{:S(2)}) collective-permute-start(f32[264,128]{1,0:T(8,128)S(1)} %get-tuple-element.84), channel_id=1, source_target_pairs={{0,16},{8,24},{16,0},{24,8},{1,17},{9,25},{17,1},{25,9},{2,18},{10... | collective-permute-start | bytes 405512 | tf_op jit(solution)/shard_map/ppermute | solution.py:124
  8.6 15.4 %collective-permute-start.2 = (f32[264,128]{1,0:T(8,128)S(1)}, f32[264,128]{1,0:T(8,128)S(1)}, u32[]{:S(2)}, u32[]{:S(2)}) collective-permute-start(f32[264,128]{1,0:T(8,128)S(1)} %get-tuple-element.84), channel_id=1, source_target_pairs={{0,24},{8,16},{16,8},{24,0},{1,25},{9,17},{17,9},{25,1},{2,26},{10... | collective-permute-start | bytes 405512 | tf_op jit(solution)/shard_map/ppermute | solution.py:124
  10.0 23.2 %collective-permute-start.13 = (f32[512,128]{1,0:T(8,128)S(1)}, f32[512,128]{1,0:T(8,128)S(1)}, u32[]{:S(2)}, u32[]{:S(2)}) collective-permute-start(f32[512,128]{1,0:T(8,128)S(1)} %get-tuple-element.85), channel_id=1, source_target_pairs={{0,16},{8,24},{16,0},{24,8},{1,17},{9,25},{17,1},{25,9},{2,18},{10... | collective-permute-start | bytes 786440 | tf_op jit(solution)/shard_map/ppermute | solution.py:124
  24.1 17.7 %collective-permute-start.4 = (f32[768,128]{1,0:T(8,128)S(1)}, f32[768,128]{1,0:T(8,128)S(1)}, u32[]{:S(2)}, u32[]{:S(2)}) collective-permute-start(f32[768,128]{1,0:T(8,128)S(1)} %pad_maximum_fusion.1), channel_id=1, source_target_pairs={{0,4},{2,6},{4,0},{6,2},{1,5},{3,7},{5,1},{7,3},{8,12},{10,14},{12... | collective-permute-start | bytes 1179656 | tf_op jit(solution)/shard_map/ppermute | solution.py:115
  25.6 17.5 %collective-permute-start.5 = (f32[768,128]{1,0:T(8,128)S(1)}, f32[768,128]{1,0:T(8,128)S(1)}, u32[]{:S(2)}, u32[]{:S(2)}) collective-permute-start(f32[768,128]{1,0:T(8,128)S(1)} %pad_maximum_fusion.1), channel_id=1, source_target_pairs={{0,1},{1,0},{2,3},{3,2},{4,5},{5,4},{6,7},{7,6},{8,9},{9,8},{10,11... | collective-permute-start | bytes 1179656 | tf_op jit(solution)/shard_map/ppermute | solution.py:118
  33.2 8.5 %collective-permute-start.15 = (f32[512,128]{1,0:T(8,128)S(1)}, f32[512,128]{1,0:T(8,128)S(1)}, u32[]{:S(2)}, u32[]{:S(2)}) collective-permute-start(f32[512,128]{1,0:T(8,128)S(1)} %collective-permute-done.13.refs_11_), channel_id=1, source_target_pairs={{8,0},{16,24},{9,1},{17,25},{10,2},{18,26},{11,3},{19,27},{12,4},{... | collective-permute-start | bytes 786440 | tf_op jit(solution)/shard_map/ppermute | solution.py:131
  34.5 15.2 %collective-permute-start.8 = (f32[768,128]{1,0:T(8,128)S(1)}, f32[768,128]{1,0:T(8,128)S(1)}, u32[]{:S(2)}, u32[]{:S(2)}) collective-permute-start(f32[768,128]{1,0:T(8,128)S(1)} %pad_maximum_fusion.1), channel_id=1, source_target_pairs={{0,2},{2,0},{4,6},{6,4},{1,3},{3,1},{5,7},{7,5},{8,10},{10,8},{12,... | collective-permute-start | bytes 1179656 | tf_op jit(solution)/shard_map/ppermute | solution.py:112
  43.1 7.9 %collective-permute-start.7 = (f32[384,128]{1,0:T(8,128)S(1)}, f32[384,128]{1,0:T(8,128)S(1)}, u32[]{:S(2)}, u32[]{:S(2)}) collective-permute-start(f32[384,128]{1,0:T(8,128)S(1)} %slice.32), channel_id=1, source_target_pairs={{0,4},{2,6},{4,0},{6,2},{1,5},{3,7},{5,1},{7,3},{8,12},{10,14},{12... | collective-permute-start | bytes 589832 | tf_op jit(solution)/shard_map/ppermute | solution.py:115
  44.8 18.1 %collective-permute-start.16 = (f32[1536,128]{1,0:T(8,128)S(1)}, f32[1536,128]{1,0:T(8,128)S(1)}, u32[]{:S(2)}, u32[]{:S(2)}) collective-permute-start(f32[1536,128]{1,0:T(8,128)S(1)} %pad_maximum_fusion), channel_id=1, source_target_pairs={{0,4},{2,6},{4,0},{6,2},{1,5},{3,7},{5,1},{7,3},{8,12},{10,14},{12... | collective-permute-start | bytes 2359304 | tf_op jit(solution)/shard_map/ppermute | solution.py:115
  45.4 17.5 %collective-permute-start.17 = (f32[1536,128]{1,0:T(8,128)S(1)}, f32[1536,128]{1,0:T(8,128)S(1)}, u32[]{:S(2)}, u32[]{:S(2)}) collective-permute-start(f32[1536,128]{1,0:T(8,128)S(1)} %pad_maximum_fusion), channel_id=1, source_target_pairs={{0,1},{1,0},{2,3},{3,2},{4,5},{5,4},{6,7},{7,6},{8,9},{9,8},{10,11... | collective-permute-start | bytes 2359304 | tf_op jit(solution)/shard_map/ppermute | solution.py:118
  62.9 10.7 %collective-permute-start.18 = (f32[768,128]{1,0:T(8,128)S(1)}, f32[768,128]{1,0:T(8,128)S(1)}, u32[]{:S(2)}, u32[]{:S(2)}) collective-permute-start(f32[768,128]{1,0:T(8,128)S(1)} %slice.26), channel_id=1, source_target_pairs={{0,1},{1,0},{2,3},{3,2},{4,5},{5,4},{6,7},{7,6},{8,9},{9,8},{10,11... | collective-permute-start | bytes 1179656 | tf_op jit(solution)/shard_map/ppermute | solution.py:118
  63.3 11.0 %collective-permute-start.19 = (f32[768,128]{1,0:T(8,128)S(1)}, f32[768,128]{1,0:T(8,128)S(1)}, u32[]{:S(2)}, u32[]{:S(2)}) collective-permute-start(f32[768,128]{1,0:T(8,128)S(1)} %slice.27), channel_id=1, source_target_pairs={{0,4},{2,6},{4,0},{6,2},{1,5},{3,7},{5,1},{7,3},{8,12},{10,14},{12... | collective-permute-start | bytes 1179656 | tf_op jit(solution)/shard_map/ppermute | solution.py:115
  65.1 10.9 %collective-permute-start.20 = (f32[1536,128]{1,0:T(8,128)S(1)}, f32[1536,128]{1,0:T(8,128)S(1)}, u32[]{:S(2)}, u32[]{:S(2)}) collective-permute-start(f32[1536,128]{1,0:T(8,128)S(1)} %pad_maximum_fusion), channel_id=1, source_target_pairs={{0,2},{2,0},{4,6},{6,4},{1,3},{3,1},{5,7},{7,5},{8,10},{10,8},{12,... | collective-permute-start | bytes 2359304 | tf_op jit(solution)/shard_map/ppermute | solution.py:112
  65.1 10.9 %collective-permute-start.21 = (f32[1536,128]{1,0:T(8,128)S(1)}, f32[1536,128]{1,0:T(8,128)S(1)}, u32[]{:S(2)}, u32[]{:S(2)}) collective-permute-start(f32[1536,128]{1,0:T(8,128)S(1)} %collective-permute-done.16.refs_13_), channel_id=1, source_target_pairs={{0,2},{2,0},{4,6},{6,4},{1,3},{3,1},{5,7},{7,5},{8,10},{10,8},{12,... | collective-permute-start | bytes 2359304 | tf_op jit(solution)/shard_map/ppermute | solution.py:112
  65.6 10.4 %collective-permute-start.22 = (f32[1536,128]{1,0:T(8,128)S(1)}, f32[1536,128]{1,0:T(8,128)S(1)}, u32[]{:S(2)}, u32[]{:S(2)}) collective-permute-start(f32[1536,128]{1,0:T(8,128)S(1)} %collective-permute-done.17.refs_14_), channel_id=1, source_target_pairs={{0,2},{2,0},{4,6},{6,4},{1,3},{3,1},{5,7},{7,5},{8,10},{10,8},{12,... | collective-permute-start | bytes 2359304 | tf_op jit(solution)/shard_map/ppermute | solution.py:112
  101.4 10.5 %collective-permute-start.27 = (f32[512,128]{1,0:T(8,128)S(1)}, f32[512,128]{1,0:T(8,128)S(1)}, u32[]{:S(2)}, u32[]{:S(2)}) collective-permute-start(f32[512,128]{1,0:T(8,128)S(1)} %get-tuple-element.145), channel_id=1, source_target_pairs={{0,4},{2,6},{4,0},{6,2},{1,5},{3,7},{5,1},{7,3},{8,12},{10,14},{12... | collective-permute-start | bytes 786440 | tf_op jit(solution)/shard_map/ppermute | solution.py:115
  102.9 13.7 %collective-permute-start.28 = (f32[512,128]{1,0:T(8,128)S(1)}, f32[512,128]{1,0:T(8,128)S(1)}, u32[]{:S(2)}, u32[]{:S(2)}) collective-permute-start(f32[512,128]{1,0:T(8,128)S(1)} %get-tuple-element.146), channel_id=1, source_target_pairs={{0,1},{1,0},{2,3},{3,2},{4,5},{5,4},{6,7},{7,6},{8,9},{9,8},{10,11... | collective-permute-start | bytes 786440 | tf_op jit(solution)/shard_map/ppermute | solution.py:118
  104.1 12.5 %collective-permute-start.29 = (f32[512,128]{1,0:T(8,128)S(1)}, f32[512,128]{1,0:T(8,128)S(1)}, u32[]{:S(2)}, u32[]{:S(2)}) collective-permute-start(f32[512,128]{1,0:T(8,128)S(1)} %get-tuple-element.144), channel_id=1, source_target_pairs={{0,5},{1,4},{2,7},{3,6},{4,1},{5,0},{6,3},{7,2},{8,13},{9,12},{10,... | collective-permute-start | bytes 786440 | tf_op jit(solution)/shard_map/ppermute | solution.py:121
  116.8 17.4 %collective-permute-start.41 = (f32[512,128]{1,0:T(8,128)S(1)}, f32[512,128]{1,0:T(8,128)S(1)}, u32[]{:S(2)}, u32[]{:S(2)}) collective-permute-start(f32[512,128]{1,0:T(8,128)S(1)} %add_add_fusion.refs_0_.refs_11_), channel_id=1, source_target_pairs={{0,1},{1,0},{2,3},{3,2},{4,5},{5,4},{6,7},{7,6},{8,9},{9,8},{10,11... | collective-permute-start | bytes 786440 | tf_op jit(solution)/shard_map/ppermute | solution.py:118
  118.1 16.1 %collective-permute-start.42 = (f32[512,128]{1,0:T(8,128)S(1)}, f32[512,128]{1,0:T(8,128)S(1)}, u32[]{:S(2)}, u32[]{:S(2)}) collective-permute-start(f32[512,128]{1,0:T(8,128)S(1)} %add_add_fusion.refs_0_.refs_11_), channel_id=1, source_target_pairs={{0,4},{2,6},{4,0},{6,2},{1,5},{3,7},{5,1},{7,3},{8,12},{10,14},{12... | collective-permute-start | bytes 786440 | tf_op jit(solution)/shard_map/ppermute | solution.py:115
  120.0 10.3 %collective-permute-start.31 = (f32[280,128]{1,0:T(8,128)S(1)}, f32[280,128]{1,0:T(8,128)S(1)}, u32[]{:S(2)}, u32[]{:S(2)}) collective-permute-start(f32[280,128]{1,0:T(8,128)S(1)} %get-tuple-element.149), channel_id=1, source_target_pairs={{0,4},{2,6},{4,0},{6,2},{1,5},{3,7},{5,1},{7,3},{8,12},{10,14},{12... | collective-permute-start | bytes 430088 | tf_op jit(solution)/shard_map/ppermute | solution.py:115
  121.6 10.5 %collective-permute-start.32 = (f32[280,128]{1,0:T(8,128)S(1)}, f32[280,128]{1,0:T(8,128)S(1)}, u32[]{:S(2)}, u32[]{:S(2)}) collective-permute-start(f32[280,128]{1,0:T(8,128)S(1)} %get-tuple-element.150), channel_id=1, source_target_pairs={{0,1},{1,0},{2,3},{3,2},{4,5},{5,4},{6,7},{7,6},{8,9},{9,8},{10,11... | collective-permute-start | bytes 430088 | tf_op jit(solution)/shard_map/ppermute | solution.py:118
  122.4 10.4 %collective-permute-start.33 = (f32[280,128]{1,0:T(8,128)S(1)}, f32[280,128]{1,0:T(8,128)S(1)}, u32[]{:S(2)}, u32[]{:S(2)}) collective-permute-start(f32[280,128]{1,0:T(8,128)S(1)} %get-tuple-element.148), channel_id=1, source_target_pairs={{0,5},{1,4},{2,7},{3,6},{4,1},{5,0},{6,3},{7,2},{8,13},{9,12},{10,... | collective-permute-start | bytes 430088 | tf_op jit(solution)/shard_map/ppermute | solution.py:121
  130.3 8.2 %collective-permute-start.43 = (f32[512,128]{1,0:T(8,128)S(1)}, f32[512,128]{1,0:T(8,128)S(1)}, u32[]{:S(2)}, u32[]{:S(2)}) collective-permute-start(f32[512,128]{1,0:T(8,128)S(1)} %add_add_fusion.refs_0_.refs_11_), channel_id=1, source_target_pairs={{0,5},{1,4},{2,7},{3,6},{4,1},{5,0},{6,3},{7,2},{8,13},{9,12},{10,... | collective-permute-start | bytes 786440 | tf_op jit(solution)/shard_map/ppermute | solution.py:121
  133.0 8.6 %collective-permute-start.35 = (f32[280,128]{1,0:T(8,128)S(1)}, f32[280,128]{1,0:T(8,128)S(1)}, u32[]{:S(2)}, u32[]{:S(2)}) collective-permute-start(f32[280,128]{1,0:T(8,128)S(1)} %add_add_fusion.1.refs_0_.refs_3_), channel_id=1, source_target_pairs={{0,1},{1,0},{2,3},{3,2},{4,5},{5,4},{6,7},{7,6},{8,9},{9,8},{10,11... | collective-permute-start | bytes 430088 | tf_op jit(solution)/shard_map/ppermute | solution.py:118
  138.6 12.4 %collective-permute-start.44 = (f32[512,128]{1,0:T(8,128)S(1)}, f32[512,128]{1,0:T(8,128)S(1)}, u32[]{:S(2)}, u32[]{:S(2)}) collective-permute-start(f32[512,128]{1,0:T(8,128)S(1)} %collective-permute-done.41.refs_1_.refs_12_), channel_id=1, source_target_pairs={{0,2},{2,0},{4,6},{6,4},{1,3},{3,1},{5,7},{7,5},{8,10},{10,8},{12,... | collective-permute-start | bytes 786440 | tf_op jit(solution)/shard_map/ppermute | solution.py:112
  138.6 12.5 %collective-permute-start.45 = (f32[512,128]{1,0:T(8,128)S(1)}, f32[512,128]{1,0:T(8,128)S(1)}, u32[]{:S(2)}, u32[]{:S(2)}) collective-permute-start(f32[512,128]{1,0:T(8,128)S(1)} %collective-permute-done.42.refs_2_.refs_13_), channel_id=1, source_target_pairs={{0,2},{2,0},{4,6},{6,4},{1,3},{3,1},{5,7},{7,5},{8,10},{10,8},{12,... | collective-permute-start | bytes 786440 | tf_op jit(solution)/shard_map/ppermute | solution.py:112
  139.1 12.0 %collective-permute-start.46 = (f32[512,128]{1,0:T(8,128)S(1)}, f32[512,128]{1,0:T(8,128)S(1)}, u32[]{:S(2)}, u32[]{:S(2)}) collective-permute-start(f32[512,128]{1,0:T(8,128)S(1)} %collective-permute-done.43.refs_3_.refs_14_), channel_id=1, source_target_pairs={{0,2},{2,0},{4,6},{6,4},{1,3},{3,1},{5,7},{7,5},{8,10},{10,8},{12,... | collective-permute-start | bytes 786440 | tf_op jit(solution)/shard_map/ppermute | solution.py:112
  139.1 11.3 %collective-permute-start.36 = (f32[280,128]{1,0:T(8,128)S(1)}, f32[280,128]{1,0:T(8,128)S(1)}, u32[]{:S(2)}, u32[]{:S(2)}) collective-permute-start(f32[280,128]{1,0:T(8,128)S(1)} %add_add_fusion.1.refs_0_.refs_3_), channel_id=1, source_target_pairs={{0,4},{2,6},{4,0},{6,2},{1,5},{3,7},{5,1},{7,3},{8,12},{10,14},{12... | collective-permute-start | bytes 430088 | tf_op jit(solution)/shard_map/ppermute | solution.py:115
  141.5 8.9 %collective-permute-start.37 = (f32[280,128]{1,0:T(8,128)S(1)}, f32[280,128]{1,0:T(8,128)S(1)}, u32[]{:S(2)}, u32[]{:S(2)}) collective-permute-start(f32[280,128]{1,0:T(8,128)S(1)} %add_add_fusion.1.refs_0_.refs_3_), channel_id=1, source_target_pairs={{0,5},{1,4},{2,7},{3,6},{4,1},{5,0},{6,3},{7,2},{8,13},{9,12},{10,... | collective-permute-start | bytes 430088 | tf_op jit(solution)/shard_map/ppermute | solution.py:121
  (52 other events, 697.0 us)

commit v3 on v2

--- a/solution.py
+++ b/solution.py
@@ -709,7 +709,7 @@
         out_shape=shape((rows, width)),
         input_output_aliases={7: 0} if held else {},
         compiler_params=params(28),
-        cost_estimate=pl.CostEstimate(flops=8 << 30, bytes_accessed=8 << 20, transcendentals=0),
+        cost_estimate=pl.CostEstimate(flops=68719476736, bytes_accessed=1 << 10, transcendentals=0),
         name="attention_rest",
     )(meta, in_hbm(back), in_hbm(qkv), in_hbm(prob), wout, wqkv, in_hbm(own), *held)
 
@@ -718,17 +718,33 @@
     return [(meta[2] ^ half) * 4 + (meta[4] ^ bits) for half in range(2) for bits in range(4)]
 
 
-def squares_kernel(split_rows, meta, *refs):
-    parts, before, out, sums = refs[:8], refs[8:-2], refs[-2], refs[-1]
-    rows = parts[0].shape[0]
-    row = lax.broadcasted_iota(jnp.int32, (rows, LANES), 0)
-    for place, part in zip(places_of(meta), parts):
-        square = part[...] * part[...]
+def halves_of(refs):
+    each = len(refs) // 2
+    parts = []
+    for half in range(2):
+        own = refs[half * each : (half + 1) * each]
+        few = own[0].shape[0] // 2
+        parts += [(ref.at[:few], ref.at[few:]) for ref in own[: 4 if each == 4 else 3]]
+        parts += [tuple(own[3:])] if each == 5 else []
+    return parts
+
+
+def squares_kernel(split_rows, count, meta, *refs):
+    parts, before, out, sums = refs[:count], refs[count:-2], refs[-2], refs[-1]
+    rows = 2 * halves_of(parts)[0][0].shape[0]
+    row = lax.broadcasted_iota(jnp.int32, (rows // 2, LANES), 0)
+    for place, pieces in zip(places_of(meta), halves_of(parts)):
+        split = shared = 0.0
+        for n, piece in enumerate(pieces):
+            square = piece[...] * piece[...]
+            if split_rows < 8 * rows:
+                is_split = row < split_rows - place * rows - n * (rows // 2)
+                shared = shared + jnp.sum(jnp.where(is_split, 0.0, square), 0, keepdims=True)
+                square = jnp.where(is_split, square, 0.0)
+            split = split + jnp.sum(square, 0, keepdims=True)
+        sums[place, 0:1, :] = split
         if split_rows < 8 * rows:
-            is_split = row < split_rows - place * rows
-            sums[place, 1:2, :] = jnp.sum(jnp.where(is_split, 0.0, square), 0, keepdims=True)
-            square = jnp.where(is_split, square, 0.0)
-        sums[place, 0:1, :] = jnp.sum(square, 0, keepdims=True)
+            sums[place, 1:2, :] = shared
     out[...] = jnp.zeros_like(out)
     for kind in range(1 if split_rows == 8 * rows else 2):
         total = before[0][kind : kind + 1, :] if before else None
@@ -741,7 +757,7 @@
 def squares_of(meta, parts, split_rows=None, before=()):
     out = shape((8, LANES))
     return pl.pallas_call(
-        functools.partial(squares_kernel, split_rows or 8 * parts[0].shape[0]),
+        functools.partial(squares_kernel, split_rows or 8 * parts[0].shape[0], len(parts)),
         grid_spec=pltpu.PrefetchScalarGridSpec(
             num_scalar_prefetch=1,
             grid=(1,),
@@ -757,15 +773,19 @@
 
 def adam_kernel(count, meta, squares, *refs):
     moved = refs[:count]
-    a_parts, b_parts = refs[count : count + 8], refs[count + 8 : count + 16]
-    refs = refs[count + 16 :]
-    states, norm_ref, targets = refs[:21], refs[21], refs[22:43]
-    sums, a_full, b_full, done = refs[43:47]
-    outs = refs[47:]
-    for parts, full in ((a_parts, a_full), (b_parts, b_full)):
-        rows = parts[0].shape[0]
-        for place, part in zip(places_of(meta), parts):
-            full[pl.ds(pl.multiple_of(place * rows, 8), rows), :] = part[...]
+    a_parts, b_parts = refs[count : count + 8], refs[count + 8 : count + 18]
+    refs = refs[count + 18 :]
+    states, norm_ref, targets = list(refs[:21]), refs[21], refs[22:43]
+    sums, a_full, fetched, done = refs[43:47]
+    outs, weights = refs[47:68], refs[68:]
+    fetch = [pltpu.make_async_copy(states[3 * n + 2], weights[n], fetched.at[n]) for n in range(4)]
+    for copy in fetch:
+        copy.start()
+    for n in range(4):
+        states[3 * n + 2] = weights[n]
+    rows = a_parts[0].shape[0]
+    for place, part in zip(places_of(meta), a_parts):
+        a_full[pl.ds(pl.multiple_of(place * rows, 8), rows), :] = part[...]
     sums[meta[0]] = squares[...]
     for r in range(1, count + 1):
         sums[meta[0] ^ r] = moved[r - 1][...]
@@ -793,30 +813,41 @@
             copies.append(pltpu.make_async_copy(source, target, done.at[len(copies)]))
             copies[-1].start()
 
-    rows = 4 * width
-    for b in range(blocks):
-        part = slice(b * width, (b + 1) * width)
-        update(2, (part, slice(None)), b_full[part, :], True)
-        give(2, part)
-    for b in range(blocks):
-        lanes = slice(b * LANES, (b + 1) * LANES)
-        update(3, (slice(None), lanes), b_full[rows + b * 4 * LANES : rows + (b + 1) * 4 * LANES, :], True)
-        give(3, (slice(None), lanes))
+    pieces = halves_of(b_parts)
+    few = width // 2
+    lower = meta[2] == 0
+    every = slice(None)
+    fetch[2].wait()
+    for bits in range(4):
+        place = meta[4] ^ bits
+        for n in range(2):
+            grad = jnp.where(lower, pieces[bits][n][...], pieces[4 + bits][n][...])
+            update(2, (at(place * width + n * few, few), every), grad, True)
+        give(2, (at(place * width, width), every))
+    fetch[3].wait()
+    for bits in range(4):
+        lanes = at((meta[4] ^ bits) * LANES, LANES)
+        for n in range(2):
+            grad = jnp.where(lower, pieces[4 + bits][n][...], pieces[bits][n][...])
+            update(3, (slice(n * few, (n + 1) * few), lanes), grad, True)
+        give(3, (every, lanes))
+    fetch[0].wait()
     for j in range(3):
         update(0, (j,), a_full[j * width : (j + 1) * width, :], True)
         give(0, j)
+    fetch[1].wait()
     base = 3 * width
     for b in range(blocks):
         lanes = slice(b * LANES, (b + 1) * LANES)
-        update(1, (slice(None), lanes), a_full[base + b * LANES : base + (b + 1) * LANES, :], True)
+        update(1, (every, lanes), a_full[base + b * LANES : base + (b + 1) * LANES, :], True)
     give(1)
     base += width
-    update(4, (slice(None), slice(None)), a_full[base : base + 6, :], False)
+    update(4, (every, every), a_full[base : base + 6, :], False)
     give(4)
     base += 8
     for b in range(blocks):
         lanes = slice(b * LANES, (b + 1) * LANES)
-        update(5, (slice(None), lanes), a_full[base + 8 * b : base + 8 * b + 6, :], False)
+        update(5, (every, lanes), a_full[base + 8 * b : base + 8 * b + 6, :], False)
     give(5)
     base += 8 * blocks
     tasks, kinds, _ = states[6 * 3].shape
@@ -825,7 +856,7 @@
         lanes = slice(b * LANES, (b + 1) * LANES)
         for t in range(tasks):
             row = base + each * b + kinds * t
-            update(6, (t, slice(None), lanes), a_full[row : row + kinds, :], True)
+            update(6, (t, every, lanes), a_full[row : row + kinds, :], True)
     give(6)
     for copy in copies:
         copy.wait()
@@ -836,21 +867,25 @@
     here = pl.BlockSpec(memory_space=pltpu.VMEM)
     blocks = states[-4].shape[1] // LANES
     args = (squares,) + tuple(moved) + tuple(a_parts) + tuple(b_parts)
+    late = [n < 12 and n % 3 == 2 for n in range(len(states))]
     return pl.pallas_call(
         functools.partial(adam_kernel, len(moved)),
-        in_specs=[pl.BlockSpec(memory_space=pltpu.SMEM)] + [here] * (len(args) + len(states)),
+        in_specs=[pl.BlockSpec(memory_space=pltpu.SMEM)]
+        + [here] * len(args)
+        + [held if later else here for later in late],
         out_specs=[here] + [held] * len(states),
         out_shape=[shape((1, 1))] + [shape(s.shape) for s in states],
         scratch_shapes=[
             pltpu.VMEM((len(moved) + 1, 8, LANES), F32),
             pltpu.VMEM((8 * a_parts[0].shape[0], LANES), F32),
-            pltpu.VMEM((8 * b_parts[0].shape[0], LANES), F32),
+            pltpu.SemaphoreType.DMA((4,)),
             pltpu.SemaphoreType.DMA((6 * blocks + 3 * 3 + 3 * 4,)),
         ]
-        + [pltpu.VMEM(s.shape, F32) for s in states],
-        compiler_params=params(18),
+        + [pltpu.VMEM(s.shape, F32) for s in states]
+        + [pltpu.VMEM(s.shape, F32) for s, later in zip(states, late) if later],
+        compiler_params=params(24),
         name="adam",
-    )(meta, *args, *(s if n % 3 == 2 else in_vmem(s) for n, s in enumerate(states)))
+    )(meta, *args, *(in_hbm(s) if later else s if n % 3 == 2 else in_vmem(s) for n, (s, later) in enumerate(zip(states, late))))
 
 
 def shares(mesh, *args):
@@ -947,15 +982,18 @@
         meta, back_one, tokens_in, qkv, prob, context, wout, (norm_grad, class_grad, up_bias_grad), False
     )
     b_own = plane.scatter(b_parts, a_give)
-    b_crossed, b_near = plane.rejoin(b_own)
+    b_crossed, b_near = plane.core(b_own), plane.spread(b_own)
     a_parts = plane.quarters(a_keep, a_give, quarter)
     back_one = after(back_one, a_parts, b_crossed)
     input_grad = run_rest(meta, back_one, qkv, prob, wout, wqkv, own, 0)
-    b_parts = plane.rejoin_on(b_own, b_crossed, after(b_near, input_grad))
     a_own = plane.scatter(a_parts, input_grad)
+    b_near = after(b_near, input_grad)
+    b_corner = plane.corners(b_near)
     a_crossed, a_near = plane.rejoin(a_own)
     input_grad = run_rest(meta, after(back_one, a_crossed), qkv, prob, wout, wqkv, own, 1, input_grad)
-    a_parts = plane.rejoin_on(a_own, a_crossed, after(a_near, input_grad))
+    b_near, b_corner, a_near = after((b_near, b_corner, a_near), input_grad)
+    b_parts = plane.rejoin_on(b_own, b_crossed, (b_near[2], b_near[1]) + b_corner)
+    a_parts = plane.rejoin_on(a_own, a_crossed, a_near)
     squares = squares_of(meta, a_parts, 4 * width + 8, (squares_of(meta, b_parts),))
     moved = tuple(plane.along(squares, r) for r in turns)
     states = (

time: 171 us -> 166 us (0.971)
  waiting for transfers between devices: 61.4 us -> 57.7 us
    ppermute x4 -> x3, waiting for transfers between devices: 5.12 us -> 2.2 us  [corner(): lax.ppermute(value, ('batch', 'rep'), pairs(self.batch * self.rep, 2 * se...]
    ppermute x8 -> x9, waiting for transfers between devices: 17.4 us -> 15.4 us  [other(): return lax.ppermute(value, 'rep', pairs(self.rep, 1))]
    ppermute x4 -> x3, starting transfers between devices: 5.43 us -> 3.75 us  [corner(): lax.ppermute(value, ('batch', 'rep'), pairs(self.batch * self.rep, 2 * se...]
    ppermute x8 -> x9, starting transfers between devices: 10.5 us -> 11.9 us  [side(): return lax.ppermute(value, 'batch', pairs(self.batch, 2))]
    ppermute x20 -> x21, starting transfers between devices: 2.93 us -> 3.46 us  [core(): return lax.ppermute(value, 'batch', pairs(self.batch, 1))]
    ppermute x20 -> x21, waiting for transfers between devices: 6.76 us -> 7.09 us  [core(): return lax.ppermute(value, 'batch', pairs(self.batch, 1))]
    ppermute x8 -> x9, starting transfers between devices: 8.51 us -> 8.63 us  [other(): return lax.ppermute(value, 'rep', pairs(self.rep, 1))]
  transfers between devices with their start and end apart: 50 -> 52, of which waited for: 22 -> 22; matrix products, arithmetic and copies ran while one was open for 1% -> 1% of each run, Pallas kernels for 17% -> 18%
where the time goes in v3:
time: 166 us
  Pallas kernels  60.1 us (36%)
  waiting for transfers between devices  57.7 us (35%)
  starting transfers between devices  43.3 us (26%)
  other arithmetic  3.01 us (2%)
    ppermute x8, waiting for transfers between devices, along(): return lax.ppermute(value, 'head', pairs(self.heads, bit))  23 us
    pallas_call x1, Pallas kernels, run_feed(): pl.pallas_call(functools.partial(feed_kernel, len(first), given), grid_sp...  19.9 us
    ppermute x9, waiting for transfers between devices, other(): return lax.ppermute(value, 'rep', pairs(self.rep, 1))  15.4 us
    pallas_call x2, Pallas kernels, run_rest(): pl.pallas_call(rest_kernel, grid_spec=pltpu.PrefetchScalarGridSpec(num_sc...  13.9 us
    ppermute x8, starting transfers between devices, along(): return lax.ppermute(value, 'head', pairs(self.heads, bit))  13.6 us
    ppermute x9, starting transfers between devices, side(): return lax.ppermute(value, 'batch', pairs(self.batch, 2))  11.9 us
    ppermute x9, starting transfers between devices, other(): return lax.ppermute(value, 'rep', pairs(self.rep, 1))  8.63 us
    pallas_call x1, Pallas kernels, run_attention_forward(): pl.pallas_call(functools.partial(attention_forward, len(first), given), g...  8.47 us
  transfers between devices with their start and end apart: 52, of which 22 were waited for; matrix products, arithmetic and copies ran while one was open for 1% of the time, Pallas kernels for 18%

profile of v3, /device:TPU:0, one launch (start us, length us, event | category | flops | bytes accessed | tf_op | source)
XLA Modules:
  0.0 166.1 jit_solution(15324805459700611668)
XLA Ops:
  0.8 1.7 %pack.1 = (f32[264,128]{1,0:T(8,128)S(1)}, f32[512,128]{1,0:T(8,128)S(1)}) custom-call(s32[5]{0:T(128)S(1)} %stack.20.meta, f32[3,512,128]{2,1,0:T(8,128)} %refs_23_.1, f32[128,512]{1,0:T(8,128)} %refs_26_.1, f32[6,128]{1,0:T(8,128)} %refs_35_.1, f32[2048,128]{1,0:T(8,128)} %bitcast.23, f32[512,512]{1,0:T(8,128)} %bitcast.26), custom_call_target="tpu_custom_call" | custom-call | tf_op jit(solution)/shard_map/pack/pallas_call | solution.py:198
  2.5 3.1 %collective-permute-start.3 = (f32[512,128]{1,0:T(8,128)S(1)}, f32[512,128]{1,0:T(8,128)S(1)}, u32[]{:S(2)}, u32[]{:S(2)}) collective-permute-start(f32[512,128]{1,0:T(8,128)S(1)} %get-tuple-element.88), channel_id=1, source_target_pairs={{0,8},{8,0},{16,24},{24,16},{1,9},{9,1},{17,25},{25,17},{2,10},{10... | collective-permute-start | bytes 786440 | tf_op jit(solution)/shard_map/ppermute | solution.py:124
  5.7 3.0 %collective-permute-start.1 = (f32[264,128]{1,0:T(8,128)S(1)}, f32[264,128]{1,0:T(8,128)S(1)}, u32[]{:S(2)}, u32[]{:S(2)}) collective-permute-start(f32[264,128]{1,0:T(8,128)S(1)} %get-tuple-element.87), channel_id=1, source_target_pairs={{0,16},{8,24},{16,0},{24,8},{1,17},{9,25},{17,1},{25,9},{2,18},{10... | collective-permute-start | bytes 405512 | tf_op jit(solution)/shard_map/ppermute | solution.py:124
  10.0 1.7 %collective-permute-start.13 = (f32[512,128]{1,0:T(8,128)S(1)}, f32[512,128]{1,0:T(8,128)S(1)}, u32[]{:S(2)}, u32[]{:S(2)}) collective-permute-start(f32[512,128]{1,0:T(8,128)S(1)} %get-tuple-element.88), channel_id=1, source_target_pairs={{0,16},{8,24},{16,0},{24,8},{1,17},{9,25},{17,1},{25,9},{2,18},{10... | collective-permute-start | bytes 786440 | tf_op jit(solution)/shard_map/ppermute | solution.py:124
  11.7 10.5 %collective-permute-done.refs_5_.refs_7_ = f32[264,128]{1,0:T(8,128)S(1)} collective-permute-done((f32[264,128]{1,0:T(8,128)S(1)}, f32[264,128]{1,0:T(8,128)S(1)}, u32[]{:S(2)}, u32[]{:S(2)}) %collective-permute-start) | collective-permute-done | bytes 135200 | tf_op jit(solution)/shard_map/ppermute | solution.py:124
  22.2 1.8 %collective-permute-done.2.refs_7_.refs_9_ = f32[264,128]{1,0:T(8,128)S(1)} collective-permute-done((f32[264,128]{1,0:T(8,128)S(1)}, f32[264,128]{1,0:T(8,128)S(1)}, u32[]{:S(2)}, u32[]{:S(2)}) %collective-permute-start.2) | collective-permute-done | bytes 135200 | tf_op jit(solution)/shard_map/ppermute | solution.py:124
  24.1 1.6 collective-permute-start.4
  25.6 1.5 collective-permute-start.5
  27.8 5.4 %collective-permute-done.13.refs_11_ = f32[512,128]{1,0:T(8,128)S(1)} collective-permute-done((f32[512,128]{1,0:T(8,128)S(1)}, f32[512,128]{1,0:T(8,128)S(1)}, u32[]{:S(2)}, u32[]{:S(2)}) %collective-permute-start.13) | collective-permute-done | bytes 262176 | tf_op jit(solution)/shard_map/ppermute | solution.py:124
  34.6 7.1 %collective-permute-done.15 = f32[512,128]{1,0:T(8,128)S(1)} collective-permute-done((f32[512,128]{1,0:T(8,128)S(1)}, f32[512,128]{1,0:T(8,128)S(1)}, u32[]{:S(2)}, u32[]{:S(2)}) %collective-permute-start.15) | collective-permute-done | bytes 262176 | tf_op jit(solution)/shard_map/ppermute | solution.py:131
  43.1 1.6 collective-permute-start.7
  46.1 3.5 %collective-permute-done.6.refs_10_ = f32[384,128]{1,0:T(8,128)S(1)} collective-permute-done((f32[384,128]{1,0:T(8,128)S(1)}, f32[384,128]{1,0:T(8,128)S(1)}, u32[]{:S(2)}, u32[]{:S(2)}) %collective-permute-start.6) | collective-permute-done | bytes 196640 | tf_op jit(solution)/shard_map/ppermute | solution.py:118
  51.5 1.5 collective-permute-done.12.refs_16_
  53.1 8.5 %attention_forward.1 = (bf16[4,1024,384]{2,1,0:T(8,128)(2,1)}, f32[4,8,256,128]{3,2,1,0:T(8,128)}, bf16[1024,512]{1,0:T(8,128)(2,1)}, f32[1024,512]{1,0:T(8,128)...) custom-call(s32[5]{0:T(128)S(1)} %stack.20.meta, s32[8]{0:T(128)S(1)} %copy-done.25, ...), custom_call_target="tpu_custom_call" | custom-call | flops 2684354560 | bytes 16777216 | tf_op jit(solution)/shard_map/attention_forward/pallas_call | solution.py:343
  63.3 1.8 %collective-permute-start.19 = (f32[768,128]{1,0:T(8,128)S(1)}, f32[768,128]{1,0:T(8,128)S(1)}, u32[]{:S(2)}, u32[]{:S(2)}) collective-permute-start(f32[768,128]{1,0:T(8,128)S(1)} %slice.33), channel_id=1, source_target_pairs={{0,4},{2,6},{4,0},{6,2},{1,5},{3,7},{5,1},{7,3},{8,12},{10,14},{12... | collective-permute-start | bytes 1179656 | tf_op jit(solution)/shard_map/ppermute | solution.py:115
  65.6 7.2 %collective-permute-done.18.refs_15_ = f32[768,128]{1,0:T(8,128)S(1)} collective-permute-done((f32[768,128]{1,0:T(8,128)S(1)}, f32[768,128]{1,0:T(8,128)S(1)}, u32[]{:S(2)}, u32[]{:S(2)}) %collective-permute-start.18) | collective-permute-done | bytes 393248 | tf_op jit(solution)/shard_map/ppermute | solution.py:118
  75.3 19.9 %feed_both.1 = (f32[1024,512]{1,0:T(8,128)}, f32[1024,512]{1,0:T(8,128)}, f32[8,512]{1,0:T(8,128)S(1)}, f32[9,3,512]{2,1,0:T(4,128)S(1)}, f32[8,512]{1,0:T(8,128...) custom-call(s32[5]{0:T(128)S(1)} %stack.20.meta, s32[8]{0:T(128)S(1)} %copy-done.26, s32[8]{0:T(128)S(1)} %copy-done.27, ...), custom_call_target="tpu_custom_call" | custom-call | flops 38654705664 | bytes 20971520 | tf_op jit(solution)/shard_map/feed_both/pallas_call | solution.py:509
  95.3 2.9 %collective-permute-done.25 = f32[2048,128]{1,0:T(8,128)} collective-permute-done((f32[2048,128]{1,0:T(8,128)}, f32[2048,128]{1,0:T(8,128)}, u32[]{:S(2)}, u32[]{:S(2)}) %collective-permute-start.25) | collective-permute-done | bytes 1048608 | tf_op jit(solution)/shard_map/ppermute | solution.py:112
  98.2 1.6 add.66
  99.9 1.6 collective-permute-start.27
  103.5 6.9 %attention_own.1 = (bf16[1024,384]{1,0:T(8,128)(2,1)}, f32[1120,128]{1,0:T(8,128)}, f32[1120,128]{1,0:T(8,128)}) custom-call(s32[5]{0:T(128)S(1)} %stack.20.meta, f32[1024,512]{1,0:T(8,128)} %get-tuple-element.118.back_ref, bf16[1024,512]{1,0:T(8,128)(2,1)S(1)} %copy-done.24, bf16[4,1024,384]{2,1,0:T(8,128)(2,1)} %get-tuple-element.100.qkv, ...), custom_call_target="tpu_custom_call" | custom-call | flops 4294967296 | bytes 8388608 | tf_op jit(solution)/shard_map/attention_own/pallas_call | solution.py:650
  110.5 4.6 %collective-permute-done.28 = f32[512,128]{1,0:T(8,128)S(1)} collective-permute-done((f32[512,128]{1,0:T(8,128)S(1)}, f32[512,128]{1,0:T(8,128)S(1)}, u32[]{:S(2)}, u32[]{:S(2)}) %collective-permute-start.28) | collective-permute-done | bytes 262176 | tf_op jit(solution)/shard_map/ppermute | solution.py:118
  118.4 1.5 collective-permute-start.31
  121.9 6.8 %attention_rest.2.refs_0_ = f32[1024,512]{1,0:T(8,128)} custom-call(s32[5]{0:T(128)S(1)} %stack.20.meta, f32[1024,512]{1,0:T(8,128)} %get-tuple-element.118.back_ref, bf16[4,1024,384]{2,1,0:T(8,128)(2,1)} %get-tuple-element.100.qkv, f32[4,8,256,128]{3,2,1,0:T(8,128)} %get-tuple-element.101.prob, bf16[512,512]{1,0:T(8,128)(2,1)S(1)} %copy-done.29, ...), custom_call_target="tpu_custom_call" | custom-call | flops 68719476736 | bytes 1024 | tf_op jit(solution)/shard_map/attention_rest/pallas_call | solution.py:692
  128.7 2.1 %collective-permute-done.33 = f32[280,128]{1,0:T(8,128)S(1)} collective-permute-done((f32[280,128]{1,0:T(8,128)S(1)}, f32[280,128]{1,0:T(8,128)S(1)}, u32[]{:S(2)}, u32[]{:S(2)}) %collective-permute-start.33) | collective-permute-done | bytes 143392 | tf_op jit(solution)/shard_map/ppermute | solution.py:121
  131.9 1.5 collective-permute-start.38
  135.2 1.8 %collective-permute-start.41 = (f32[280,128]{1,0:T(8,128)S(1)}, f32[280,128]{1,0:T(8,128)S(1)}, u32[]{:S(2)}, u32[]{:S(2)}) collective-permute-start(f32[280,128]{1,0:T(8,128)S(1)} %add_add_fusion.1.refs_0_.refs_3_), channel_id=1, source_target_pairs={{0,5},{1,4},{2,7},{3,6},{4,1},{5,0},{6,3},{7,2},{8,13},{9,12},{10,... | collective-permute-start | bytes 430088 | tf_op jit(solution)/shard_map/ppermute | solution.py:121
  137.0 7.1 %attention_rest.3 = f32[1024,512]{1,0:T(8,128)} custom-call(s32[5]{0:T(128)S(1)} %stack.20.meta, f32[1024,512]{1,0:T(8,128)} %get-tuple-element.118.back_ref, bf16[4,1024,384]{2,1,0:T(8,128)(2,1)} %get-tuple-element.100.qkv, f32[4,8,256,128]{3,2,1,0:T(8,128)} %get-tuple-element.101.prob, ...), custom_call_target="tpu_custom_call", output_to_operand_aliasing={{}: (7, {})} | custom-call | flops 68719476736 | bytes 1024 | tf_op jit(solution)/shard_map/attention_rest/pallas_call | solution.py:692
  148.4 4.3 %collective-permute-start.50 = (f32[8,128]{1,0:T(8,128)S(1)}, f32[8,128]{1,0:T(8,128)S(1)}, u32[]{:S(2)}, u32[]{:S(2)}) collective-permute-start(f32[8,128]{1,0:T(8,128)S(1)} %squares.3), channel_id=1, source_target_pairs={{0,16},{8,24},{16,0},{24,8},{1,17},{9,25},{17,1},{25,9},{2,18},{10... | collective-permute-start | bytes 12296 | tf_op jit(solution)/shard_map/ppermute | solution.py:124
  152.8 1.6 collective-permute-done.50.refs_1_
  154.4 3.8 %collective-permute-done.51.refs_2_ = f32[8,128]{1,0:T(8,128)S(1)} collective-permute-done((f32[8,128]{1,0:T(8,128)S(1)}, f32[8,128]{1,0:T(8,128)S(1)}, u32[]{:S(2)}, u32[]{:S(2)}) %collective-permute-start.51) | collective-permute-done | bytes 4128 | tf_op jit(solution)/shard_map/ppermute | solution.py:124
  158.3 7.7 %adam.1 = (f32[1,1]{1,0:T(1,128)}, f32[3,512,128]{2,1,0:T(8,128)}, f32[3,512,128]{2,1,0:T(8,128)}, f32[3,512,128]{2,1,0:T(8,128)}, f32[128,512]{1,0:T(8,128)}, /...) custom-call(s32[5]{0:T(128)S(1)} %stack.20.meta, ...), custom_call_target="tpu_custom_call" | custom-call | tf_op jit(solution)/shard_map/adam/pallas_call | solution.py:871
  (160 shorter events, 27.6 us)
Async XLA Ops:
  2.5 21.6 %collective-permute-start.3 = (f32[512,128]{1,0:T(8,128)S(1)}, f32[512,128]{1,0:T(8,128)S(1)}, u32[]{:S(2)}, u32[]{:S(2)}) collective-permute-start(f32[512,128]{1,0:T(8,128)S(1)} %get-tuple-element.88), channel_id=1, source_target_pairs={{0,8},{8,0},{16,24},{24,16},{1,9},{9,1},{17,25},{25,17},{2,10},{10... | collective-permute-start | bytes 786440 | tf_op jit(solution)/shard_map/ppermute | solution.py:124
  5.6 16.5 %collective-permute-start = (f32[264,128]{1,0:T(8,128)S(1)}, f32[264,128]{1,0:T(8,128)S(1)}, u32[]{:S(2)}, u32[]{:S(2)}) collective-permute-start(f32[264,128]{1,0:T(8,128)S(1)} %get-tuple-element.87), channel_id=1, source_target_pairs={{0,8},{8,0},{16,24},{24,16},{1,9},{9,1},{17,25},{25,17},{2,10},{10... | collective-permute-start | bytes 405512 | tf_op jit(solution)/shard_map/ppermute | solution.py:124
  5.7 16.5 %collective-permute-start.1 = (f32[264,128]{1,0:T(8,128)S(1)}, f32[264,128]{1,0:T(8,128)S(1)}, u32[]{:S(2)}, u32[]{:S(2)}) collective-permute-start(f32[264,128]{1,0:T(8,128)S(1)} %get-tuple-element.87), channel_id=1, source_target_pairs={{0,16},{8,24},{16,0},{24,8},{1,17},{9,25},{17,1},{25,9},{2,18},{10... | collective-permute-start | bytes 405512 | tf_op jit(solution)/shard_map/ppermute | solution.py:124
  8.6 15.4 %collective-permute-start.2 = (f32[264,128]{1,0:T(8,128)S(1)}, f32[264,128]{1,0:T(8,128)S(1)}, u32[]{:S(2)}, u32[]{:S(2)}) collective-permute-start(f32[264,128]{1,0:T(8,128)S(1)} %get-tuple-element.87), channel_id=1, source_target_pairs={{0,24},{8,16},{16,8},{24,0},{1,25},{9,17},{17,9},{25,1},{2,26},{10... | collective-permute-start | bytes 405512 | tf_op jit(solution)/shard_map/ppermute | solution.py:124
  10.0 23.2 %collective-permute-start.13 = (f32[512,128]{1,0:T(8,128)S(1)}, f32[512,128]{1,0:T(8,128)S(1)}, u32[]{:S(2)}, u32[]{:S(2)}) collective-permute-start(f32[512,128]{1,0:T(8,128)S(1)} %get-tuple-element.88), channel_id=1, source_target_pairs={{0,16},{8,24},{16,0},{24,8},{1,17},{9,25},{17,1},{25,9},{2,18},{10... | collective-permute-start | bytes 786440 | tf_op jit(solution)/shard_map/ppermute | solution.py:124
  24.1 17.7 %collective-permute-start.4 = (f32[768,128]{1,0:T(8,128)S(1)}, f32[768,128]{1,0:T(8,128)S(1)}, u32[]{:S(2)}, u32[]{:S(2)}) collective-permute-start(f32[768,128]{1,0:T(8,128)S(1)} %pad_maximum_fusion.1), channel_id=1, source_target_pairs={{0,4},{2,6},{4,0},{6,2},{1,5},{3,7},{5,1},{7,3},{8,12},{10,14},{12... | collective-permute-start | bytes 1179656 | tf_op jit(solution)/shard_map/ppermute | solution.py:115
  25.6 17.5 %collective-permute-start.5 = (f32[768,128]{1,0:T(8,128)S(1)}, f32[768,128]{1,0:T(8,128)S(1)}, u32[]{:S(2)}, u32[]{:S(2)}) collective-permute-start(f32[768,128]{1,0:T(8,128)S(1)} %pad_maximum_fusion.1), channel_id=1, source_target_pairs={{0,1},{1,0},{2,3},{3,2},{4,5},{5,4},{6,7},{7,6},{8,9},{9,8},{10,11... | collective-permute-start | bytes 1179656 | tf_op jit(solution)/shard_map/ppermute | solution.py:118
  27.1 7.4 %collective-permute-start.14 = (f32[512,128]{1,0:T(8,128)S(1)}, f32[512,128]{1,0:T(8,128)S(1)}, u32[]{:S(2)}, u32[]{:S(2)}) collective-permute-start(f32[512,128]{1,0:T(8,128)S(1)} %get-tuple-element.88), channel_id=1, source_target_pairs={{8,16},{16,8},{9,17},{17,9},{10,18},{18,10},{11,19},{19,11},{12,20... | collective-permute-start | bytes 786440 | tf_op jit(solution)/shard_map/ppermute | solution.py:127
  33.2 8.5 %collective-permute-start.15 = (f32[512,128]{1,0:T(8,128)S(1)}, f32[512,128]{1,0:T(8,128)S(1)}, u32[]{:S(2)}, u32[]{:S(2)}) collective-permute-start(f32[512,128]{1,0:T(8,128)S(1)} %collective-permute-done.13.refs_11_), channel_id=1, source_target_pairs={{8,0},{16,24},{9,1},{17,25},{10,2},{18,26},{11,3},{19,27},{12,4},{... | collective-permute-start | bytes 786440 | tf_op jit(solution)/shard_map/ppermute | solution.py:131
  34.5 15.2 %collective-permute-start.8 = (f32[768,128]{1,0:T(8,128)S(1)}, f32[768,128]{1,0:T(8,128)S(1)}, u32[]{:S(2)}, u32[]{:S(2)}) collective-permute-start(f32[768,128]{1,0:T(8,128)S(1)} %pad_maximum_fusion.1), channel_id=1, source_target_pairs={{0,2},{2,0},{4,6},{6,4},{1,3},{3,1},{5,7},{7,5},{8,10},{10,8},{12,... | collective-permute-start | bytes 1179656 | tf_op jit(solution)/shard_map/ppermute | solution.py:112
  41.8 7.9 %collective-permute-start.6 = (f32[384,128]{1,0:T(8,128)S(1)}, f32[384,128]{1,0:T(8,128)S(1)}, u32[]{:S(2)}, u32[]{:S(2)}) collective-permute-start(f32[384,128]{1,0:T(8,128)S(1)} %slice.39), channel_id=1, source_target_pairs={{0,1},{1,0},{2,3},{3,2},{4,5},{5,4},{6,7},{7,6},{8,9},{9,8},{10,11... | collective-permute-start | bytes 589832 | tf_op jit(solution)/shard_map/ppermute | solution.py:118
  43.1 7.9 %collective-permute-start.7 = (f32[384,128]{1,0:T(8,128)S(1)}, f32[384,128]{1,0:T(8,128)S(1)}, u32[]{:S(2)}, u32[]{:S(2)}) collective-permute-start(f32[384,128]{1,0:T(8,128)S(1)} %slice.40), channel_id=1, source_target_pairs={{0,4},{2,6},{4,0},{6,2},{1,5},{3,7},{5,1},{7,3},{8,12},{10,14},{12... | collective-permute-start | bytes 589832 | tf_op jit(solution)/shard_map/ppermute | solution.py:115
  44.8 18.1 %collective-permute-start.16 = (f32[1536,128]{1,0:T(8,128)S(1)}, f32[1536,128]{1,0:T(8,128)S(1)}, u32[]{:S(2)}, u32[]{:S(2)}) collective-permute-start(f32[1536,128]{1,0:T(8,128)S(1)} %pad_maximum_fusion), channel_id=1, source_target_pairs={{0,4},{2,6},{4,0},{6,2},{1,5},{3,7},{5,1},{7,3},{8,12},{10,14},{12... | collective-permute-start | bytes 2359304 | tf_op jit(solution)/shard_map/ppermute | solution.py:115
  45.4 17.5 %collective-permute-start.17 = (f32[1536,128]{1,0:T(8,128)S(1)}, f32[1536,128]{1,0:T(8,128)S(1)}, u32[]{:S(2)}, u32[]{:S(2)}) collective-permute-start(f32[1536,128]{1,0:T(8,128)S(1)} %pad_maximum_fusion), channel_id=1, source_target_pairs={{0,1},{1,0},{2,3},{3,2},{4,5},{5,4},{6,7},{7,6},{8,9},{9,8},{10,11... | collective-permute-start | bytes 2359304 | tf_op jit(solution)/shard_map/ppermute | solution.py:118
  62.9 9.9 %collective-permute-start.18 = (f32[768,128]{1,0:T(8,128)S(1)}, f32[768,128]{1,0:T(8,128)S(1)}, u32[]{:S(2)}, u32[]{:S(2)}) collective-permute-start(f32[768,128]{1,0:T(8,128)S(1)} %slice.32), channel_id=1, source_target_pairs={{0,1},{1,0},{2,3},{3,2},{4,5},{5,4},{6,7},{7,6},{8,9},{9,8},{10,11... | collective-permute-start | bytes 1179656 | tf_op jit(solution)/shard_map/ppermute | solution.py:118
  63.3 10.2 %collective-permute-start.19 = (f32[768,128]{1,0:T(8,128)S(1)}, f32[768,128]{1,0:T(8,128)S(1)}, u32[]{:S(2)}, u32[]{:S(2)}) collective-permute-start(f32[768,128]{1,0:T(8,128)S(1)} %slice.33), channel_id=1, source_target_pairs={{0,4},{2,6},{4,0},{6,2},{1,5},{3,7},{5,1},{7,3},{8,12},{10,14},{12... | collective-permute-start | bytes 1179656 | tf_op jit(solution)/shard_map/ppermute | solution.py:115
  65.1 10.1 %collective-permute-start.20 = (f32[1536,128]{1,0:T(8,128)S(1)}, f32[1536,128]{1,0:T(8,128)S(1)}, u32[]{:S(2)}, u32[]{:S(2)}) collective-permute-start(f32[1536,128]{1,0:T(8,128)S(1)} %pad_maximum_fusion), channel_id=1, source_target_pairs={{0,2},{2,0},{4,6},{6,4},{1,3},{3,1},{5,7},{7,5},{8,10},{10,8},{12,... | collective-permute-start | bytes 2359304 | tf_op jit(solution)/shard_map/ppermute | solution.py:112
  65.1 10.1 %collective-permute-start.21 = (f32[1536,128]{1,0:T(8,128)S(1)}, f32[1536,128]{1,0:T(8,128)S(1)}, u32[]{:S(2)}, u32[]{:S(2)}) collective-permute-start(f32[1536,128]{1,0:T(8,128)S(1)} %collective-permute-done.16.refs_13_), channel_id=1, source_target_pairs={{0,2},{2,0},{4,6},{6,4},{1,3},{3,1},{5,7},{7,5},{8,10},{10,8},{12,... | collective-permute-start | bytes 2359304 | tf_op jit(solution)/shard_map/ppermute | solution.py:112
  65.6 9.6 %collective-permute-start.22 = (f32[1536,128]{1,0:T(8,128)S(1)}, f32[1536,128]{1,0:T(8,128)S(1)}, u32[]{:S(2)}, u32[]{:S(2)}) collective-permute-start(f32[1536,128]{1,0:T(8,128)S(1)} %collective-permute-done.17.refs_14_), channel_id=1, source_target_pairs={{0,2},{2,0},{4,6},{6,4},{1,3},{3,1},{5,7},{7,5},{8,10},{10,8},{12,... | collective-permute-start | bytes 2359304 | tf_op jit(solution)/shard_map/ppermute | solution.py:112
  99.9 10.6 %collective-permute-start.27 = (f32[512,128]{1,0:T(8,128)S(1)}, f32[512,128]{1,0:T(8,128)S(1)}, u32[]{:S(2)}, u32[]{:S(2)}) collective-permute-start(f32[512,128]{1,0:T(8,128)S(1)} %get-tuple-element.151), channel_id=1, source_target_pairs={{0,4},{2,6},{4,0},{6,2},{1,5},{3,7},{5,1},{7,3},{8,12},{10,14},{12... | collective-permute-start | bytes 786440 | tf_op jit(solution)/shard_map/ppermute | solution.py:115
  101.5 13.7 %collective-permute-start.28 = (f32[512,128]{1,0:T(8,128)S(1)}, f32[512,128]{1,0:T(8,128)S(1)}, u32[]{:S(2)}, u32[]{:S(2)}) collective-permute-start(f32[512,128]{1,0:T(8,128)S(1)} %get-tuple-element.152), channel_id=1, source_target_pairs={{0,1},{1,0},{2,3},{3,2},{4,5},{5,4},{6,7},{7,6},{8,9},{9,8},{10,11... | collective-permute-start | bytes 786440 | tf_op jit(solution)/shard_map/ppermute | solution.py:118
  102.7 12.5 %collective-permute-start.29 = (f32[512,128]{1,0:T(8,128)S(1)}, f32[512,128]{1,0:T(8,128)S(1)}, u32[]{:S(2)}, u32[]{:S(2)}) collective-permute-start(f32[512,128]{1,0:T(8,128)S(1)} %get-tuple-element.150), channel_id=1, source_target_pairs={{0,5},{1,4},{2,7},{3,6},{4,1},{5,0},{6,3},{7,2},{8,13},{9,12},{10,... | collective-permute-start | bytes 786440 | tf_op jit(solution)/shard_map/ppermute | solution.py:121
  115.3 15.6 %collective-permute-start.35 = (f32[512,128]{1,0:T(8,128)S(1)}, f32[512,128]{1,0:T(8,128)S(1)}, u32[]{:S(2)}, u32[]{:S(2)}) collective-permute-start(f32[512,128]{1,0:T(8,128)S(1)} %add_add_fusion.refs_0_.refs_11_), channel_id=1, source_target_pairs={{0,4},{2,6},{4,0},{6,2},{1,5},{3,7},{5,1},{7,3},{8,12},{10,14},{12... | collective-permute-start | bytes 786440 | tf_op jit(solution)/shard_map/ppermute | solution.py:115
  116.3 14.6 %collective-permute-start.36 = (f32[512,128]{1,0:T(8,128)S(1)}, f32[512,128]{1,0:T(8,128)S(1)}, u32[]{:S(2)}, u32[]{:S(2)}) collective-permute-start(f32[512,128]{1,0:T(8,128)S(1)} %add_add_fusion.refs_0_.refs_11_), channel_id=1, source_target_pairs={{0,1},{1,0},{2,3},{3,2},{4,5},{5,4},{6,7},{7,6},{8,9},{9,8},{10,11... | collective-permute-start | bytes 786440 | tf_op jit(solution)/shard_map/ppermute | solution.py:118
  118.4 10.3 %collective-permute-start.31 = (f32[280,128]{1,0:T(8,128)S(1)}, f32[280,128]{1,0:T(8,128)S(1)}, u32[]{:S(2)}, u32[]{:S(2)}) collective-permute-start(f32[280,128]{1,0:T(8,128)S(1)} %get-tuple-element.155), channel_id=1, source_target_pairs={{0,4},{2,6},{4,0},{6,2},{1,5},{3,7},{5,1},{7,3},{8,12},{10,14},{12... | collective-permute-start | bytes 430088 | tf_op jit(solution)/shard_map/ppermute | solution.py:115
  119.9 8.8 %collective-permute-start.32 = (f32[280,128]{1,0:T(8,128)S(1)}, f32[280,128]{1,0:T(8,128)S(1)}, u32[]{:S(2)}, u32[]{:S(2)}) collective-permute-start(f32[280,128]{1,0:T(8,128)S(1)} %get-tuple-element.156), channel_id=1, source_target_pairs={{0,1},{1,0},{2,3},{3,2},{4,5},{5,4},{6,7},{7,6},{8,9},{9,8},{10,11... | collective-permute-start | bytes 430088 | tf_op jit(solution)/shard_map/ppermute | solution.py:118
  120.7 10.0 %collective-permute-start.33 = (f32[280,128]{1,0:T(8,128)S(1)}, f32[280,128]{1,0:T(8,128)S(1)}, u32[]{:S(2)}, u32[]{:S(2)}) collective-permute-start(f32[280,128]{1,0:T(8,128)S(1)} %get-tuple-element.154), channel_id=1, source_target_pairs={{0,5},{1,4},{2,7},{3,6},{4,1},{5,0},{6,3},{7,2},{8,13},{9,12},{10,... | collective-permute-start | bytes 430088 | tf_op jit(solution)/shard_map/ppermute | solution.py:121
  131.0 13.2 %collective-permute-start.37 = (f32[256,128]{1,0:T(8,128)S(1)}, f32[256,128]{1,0:T(8,128)S(1)}, u32[]{:S(2)}, u32[]{:S(2)}) collective-permute-start(f32[256,128]{1,0:T(8,128)S(1)} %slice.34), channel_id=1, source_target_pairs={{0,1},{1,0},{2,3},{3,2},{4,5},{5,4},{6,7},{7,6},{8,9},{9,8},{10,11... | collective-permute-start | bytes 393224 | tf_op jit(solution)/shard_map/ppermute | solution.py:118
  131.9 12.3 %collective-permute-start.38 = (f32[256,128]{1,0:T(8,128)S(1)}, f32[256,128]{1,0:T(8,128)S(1)}, u32[]{:S(2)}, u32[]{:S(2)}) collective-permute-start(f32[256,128]{1,0:T(8,128)S(1)} %slice.35), channel_id=1, source_target_pairs={{0,4},{2,6},{4,0},{6,2},{1,5},{3,7},{5,1},{7,3},{8,12},{10,14},{12... | collective-permute-start | bytes 393224 | tf_op jit(solution)/shard_map/ppermute | solution.py:115
  133.4 10.8 %collective-permute-start.39 = (f32[280,128]{1,0:T(8,128)S(1)}, f32[280,128]{1,0:T(8,128)S(1)}, u32[]{:S(2)}, u32[]{:S(2)}) collective-permute-start(f32[280,128]{1,0:T(8,128)S(1)} %add_add_fusion.1.refs_0_.refs_3_), channel_id=1, source_target_pairs={{0,1},{1,0},{2,3},{3,2},{4,5},{5,4},{6,7},{7,6},{8,9},{9,8},{10,11... | collective-permute-start | bytes 430088 | tf_op jit(solution)/shard_map/ppermute | solution.py:118
  134.3 9.9 %collective-permute-start.40 = (f32[280,128]{1,0:T(8,128)S(1)}, f32[280,128]{1,0:T(8,128)S(1)}, u32[]{:S(2)}, u32[]{:S(2)}) collective-permute-start(f32[280,128]{1,0:T(8,128)S(1)} %add_add_fusion.1.refs_0_.refs_3_), channel_id=1, source_target_pairs={{0,4},{2,6},{4,0},{6,2},{1,5},{3,7},{5,1},{7,3},{8,12},{10,14},{12... | collective-permute-start | bytes 430088 | tf_op jit(solution)/shard_map/ppermute | solution.py:115
  135.2 9.2 %collective-permute-start.41 = (f32[280,128]{1,0:T(8,128)S(1)}, f32[280,128]{1,0:T(8,128)S(1)}, u32[]{:S(2)}, u32[]{:S(2)}) collective-permute-start(f32[280,128]{1,0:T(8,128)S(1)} %add_add_fusion.1.refs_0_.refs_3_), channel_id=1, source_target_pairs={{0,5},{1,4},{2,7},{3,6},{4,1},{5,0},{6,3},{7,2},{8,13},{9,12},{10,... | collective-permute-start | bytes 430088 | tf_op jit(solution)/shard_map/ppermute | solution.py:121
  (50 other events, 762.4 us)

commit v4 on v2

--- a/solution.py
+++ b/solution.py
@@ -36,6 +36,10 @@
 def whole(array):
     rank = len(array.shape)
     return pl.BlockSpec(array.shape, lambda *_: (0,) * rank, pipeline_mode=pl.Buffered(1))
+
+
+def resident(array):
+    return pl.BlockSpec(memory_space=pltpu.VMEM)
 
 
 def params(mib=52):
@@ -320,12 +324,12 @@
     seqs = BLOCK // LANES
     heads = LANES // HEAD_DIM
     args = (tokens, norm) + tuple(weights) + tuple(first) + tuple(moved)
-    in_specs = [pl.BlockSpec((BLOCK, width), lambda i, *_: (i, 0))] + [whole(a) for a in args[1:]]
+    in_specs = [pl.BlockSpec((BLOCK, width), lambda i, *_: (i, 0))] + [(whole if given else resident)(a) for a in args[1:]]
     out_shape = [
         pltpu.HBM((groups, rows, 3 * LANES), LOW),
         pltpu.HBM((groups, rows // LANES, heads * LANES, LANES), F32),
         pltpu.HBM((rows, width), LOW),
-        pltpu.HBM((rows, width), F32),
+        (shape if given else pltpu.VMEM)((rows, width), F32),
     ]
     out_specs = [
         pl.BlockSpec((groups, BLOCK, 3 * LANES), lambda i, *_: (0, i, 0)),
@@ -335,7 +339,7 @@
     ]
     scratch = []
     if not given:
-        extra = [shape((groups, width, 3 * LANES), LOW), shape((width, width), LOW)]
+        extra = [pltpu.HBM((groups, width, 3 * LANES), LOW), pltpu.HBM((width, width), LOW)]
         out_shape += extra
         out_specs += [whole(e) for e in extra]
         scratch = [pltpu.VMEM((groups, 8, LANES), F32)]
@@ -486,7 +490,7 @@
         shards, hidden = len(first) + 1, 4 * LANES
     args = (pre_one, out_grad, norm, classes) + tuple(weights) + tuple(biases) + tuple(first) + tuple(moved)
     by_rows = pl.BlockSpec((BLOCK, width), lambda i, *_: (i, 0))
-    in_specs = [by_rows, by_rows] + [whole(a) for a in args[2:]]
+    in_specs = [by_rows, by_rows] + [(whole if given else resident)(a) for a in args[2:]]
     fixed = [shape((8, width)), shape(classes.shape), shape((8, hidden))]
     scratch = [
         pltpu.VMEM((shards, BLOCK, hidden), LOW),
@@ -497,7 +501,7 @@
         fixed += [shape((width, hidden)), shape((hidden, width))]
     else:
         half = hidden * width // LANES
-        fixed += [pltpu.HBM((half, LANES), F32), pltpu.HBM((half, LANES), F32)]
+        fixed += [pltpu.VMEM((half, LANES), F32), pltpu.VMEM((half, LANES), F32)]
         scratch += [
             pltpu.VMEM((shards, width, hidden), LOW),
             pltpu.VMEM((shards, hidden, width), LOW),
@@ -516,7 +520,7 @@
             scratch_shapes=scratch,
         ),
         out_shape=[pltpu.HBM((rows, width), F32), pltpu.HBM((rows, width), F32)] + fixed,
-        compiler_params=params(44),
+        compiler_params=params(36),
         cost_estimate=pl.CostEstimate(flops=4 * flops, bytes_accessed=20 << 20, transcendentals=0),
         name="feed_both",
     )(meta, labels, tasks, *args)
@@ -645,7 +649,7 @@
         fixed = sums
     else:
         count = packed_rows(width, *smalls[1].shape[:2])
-        fixed = [pltpu.HBM((count // 2, LANES), F32)] * 2
+        fixed = [pltpu.VMEM((count // 2, LANES), F32)] * 2
         scratch = [pltpu.VMEM(s.shape, F32) for s in sums] + [pltpu.VMEM((count, LANES), F32)]
     return pl.pallas_call(
         functools.partial(own_kernel, given),
@@ -660,7 +664,7 @@
         compiler_params=params(28),
         cost_estimate=pl.CostEstimate(flops=4 << 30, bytes_accessed=8 << 20, transcendentals=0),
         name="attention_own",
-    )(meta, in_hbm(back), tokens, in_hbm(qkv), in_hbm(prob), in_hbm(context), wout, *smalls)
+    )(meta, in_hbm(back), tokens, in_hbm(qkv), in_hbm(prob), in_hbm(context), in_hbm(wout), *smalls)
 
 
 def rest_kernel(meta, back_ref, qkv, prob, wout, wqkv, own, *refs):
@@ -709,63 +713,112 @@
         out_shape=shape((rows, width)),
         input_output_aliases={7: 0} if held else {},
         compiler_params=params(28),
-        cost_estimate=pl.CostEstimate(flops=8 << 30, bytes_accessed=8 << 20, transcendentals=0),
+        cost_estimate=pl.CostEstimate(flops=68719476736, bytes_accessed=1 << 10, transcendentals=0),
         name="attention_rest",
-    )(meta, in_hbm(back), in_hbm(qkv), in_hbm(prob), wout, wqkv, in_hbm(own), *held)
+    )(meta, in_hbm(back), in_hbm(qkv), in_hbm(prob), in_hbm(wout), in_hbm(wqkv), in_hbm(own), *held)
 
 
 def places_of(meta):
     return [(meta[2] ^ half) * 4 + (meta[4] ^ bits) for half in range(2) for bits in range(4)]
 
 
-def squares_kernel(split_rows, meta, *refs):
-    parts, before, out, sums = refs[:8], refs[8:-2], refs[-2], refs[-1]
-    rows = parts[0].shape[0]
-    row = lax.broadcasted_iota(jnp.int32, (rows, LANES), 0)
-    for place, part in zip(places_of(meta), parts):
-        square = part[...] * part[...]
-        if split_rows < 8 * rows:
-            is_split = row < split_rows - place * rows
-            sums[place, 1:2, :] = jnp.sum(jnp.where(is_split, 0.0, square), 0, keepdims=True)
-            square = jnp.where(is_split, square, 0.0)
-        sums[place, 0:1, :] = jnp.sum(square, 0, keepdims=True)
-    out[...] = jnp.zeros_like(out)
-    for kind in range(1 if split_rows == 8 * rows else 2):
-        total = before[0][kind : kind + 1, :] if before else None
-        for n in range(8):
-            term = sums[n, kind : kind + 1, :]
-            total = term if total is None else total + term
-        out[kind : kind + 1, :] = total
-
-
-def squares_of(meta, parts, split_rows=None, before=()):
+def halves_of(refs):
+    each = len(refs) // 2
+    parts = []
+    for half in range(2):
+        own = refs[half * each : (half + 1) * each]
+        few = own[0].shape[0] // 2
+        parts += [(ref.at[:few], ref.at[few:]) for ref in own[: 4 if each == 4 else 3]]
+        parts += [tuple(own[3:])] if each == 5 else []
+    return parts
+
+
+def squares_kernel(split_rows, count, meta, *refs):
+    out, sums = refs[-2:]
+    sums[...] = jnp.zeros_like(sums)
+    places = places_of(meta)
+    for base, parts, limit in ((0, refs[:count], split_rows), (8, refs[count:-2], None)):
+        halves = halves_of(parts)
+        few = halves[0][0].shape[0]
+        row = lax.broadcasted_iota(jnp.int32, (few, LANES), 0)
+        for place, pieces in zip(places, halves):
+            split = shared = 0.0
+            for n, piece in enumerate(pieces):
+                square = piece[...] * piece[...]
+                if limit is not None:
+                    is_split = row < limit - (2 * place + n) * few
+                    shared = shared + jnp.sum(jnp.where(is_split, 0.0, square), 0, keepdims=True)
+                    square = jnp.where(is_split, square, 0.0)
+                split = split + jnp.sum(square, 0, keepdims=True)
+            sums[base + place, 0:1, :] = split
+            if limit is not None:
+                sums[base + place, 1:2, :] = shared
+    total = sums[0]
+    for n in range(1, 16):
+        total = total + sums[n]
+    out[...] = total
+
+
+def squares_of(meta, a_parts, b_parts, split_rows):
     out = shape((8, LANES))
+    parts = tuple(a_parts) + tuple(b_parts)
     return pl.pallas_call(
-        functools.partial(squares_kernel, split_rows or 8 * parts[0].shape[0]),
+        functools.partial(squares_kernel, split_rows, len(a_parts)),
         grid_spec=pltpu.PrefetchScalarGridSpec(
             num_scalar_prefetch=1,
             grid=(1,),
-            in_specs=[whole(p) for p in tuple(parts) + before],
+            in_specs=[whole(p) for p in parts],
             out_specs=whole(out),
-            scratch_shapes=[pltpu.VMEM((8, 8, LANES), F32)],
+            scratch_shapes=[pltpu.VMEM((16, 8, LANES), F32)],
         ),
         out_shape=out,
         compiler_params=params(16),
         name="squares",
-    )(meta, *parts, *before)
+    )(meta, *parts)
+
+
+def ready_kernel(count, meta, *refs):
+    a_parts, b_parts, weights = refs[:count], refs[count:-11], refs[-11:-7]
+    a_full, b_full = refs[-7:-5]
+    held, fetched = refs[-5:-1], refs[-1]
+    fetch = [pltpu.make_async_copy(weights[n], held[n], fetched.at[n]) for n in range(4)]
+    for copy in fetch:
+        copy.start()
+    for parts, full in ((a_parts, a_full), (b_parts, b_full)):
+        for place, pieces in zip(places_of(meta), halves_of(parts)):
+            few = pieces[0].shape[0]
+            for n, piece in enumerate(pieces):
+                full[pl.ds(pl.multiple_of((2 * place + n) * few, 4), few), :] = piece[...]
+    for copy in fetch:
+        copy.wait()
+
+
+def run_ready(meta, a_parts, b_parts, weights):
+    here = pl.BlockSpec(memory_space=pltpu.VMEM)
+    parts = tuple(a_parts) + tuple(b_parts)
+    outs = [pltpu.VMEM((8 * p[0].shape[0], LANES), F32) for p in (a_parts, b_parts)]
+    outs += [pltpu.VMEM(w.shape, F32) for w in weights]
+    return pl.pallas_call(
+        functools.partial(ready_kernel, len(a_parts)),
+        in_specs=[pl.BlockSpec(memory_space=pltpu.SMEM)]
+        + [here] * len(parts)
+        + [pl.BlockSpec(memory_space=pltpu.HBM)] * len(weights),
+        out_specs=[here] * len(outs),
+        out_shape=outs,
+        scratch_shapes=[pltpu.SemaphoreType.DMA((4,))],
+        compiler_params=params(16),
+        cost_estimate=pl.CostEstimate(flops=64 << 30, bytes_accessed=1 << 10, transcendentals=0),
+        name="ready",
+    )(meta, *parts, *(in_hbm(w) for w in weights))
 
 
 def adam_kernel(count, meta, squares, *refs):
     moved = refs[:count]
-    a_parts, b_parts = refs[count : count + 8], refs[count + 8 : count + 16]
-    refs = refs[count + 16 :]
+    a_full, b_full = refs[count : count + 2]
+    refs = refs[count + 2 :]
     states, norm_ref, targets = refs[:21], refs[21], refs[22:43]
-    sums, a_full, b_full, done = refs[43:47]
-    outs = refs[47:]
-    for parts, full in ((a_parts, a_full), (b_parts, b_full)):
-        rows = parts[0].shape[0]
-        for place, part in zip(places_of(meta), parts):
-            full[pl.ds(pl.multiple_of(place * rows, 8), rows), :] = part[...]
+    sums, done = refs[43:45]
+    outs = refs[45:]
     sums[meta[0]] = squares[...]
     for r in range(1, count + 1):
         sums[meta[0] ^ r] = moved[r - 1][...]
@@ -798,10 +851,12 @@
         part = slice(b * width, (b + 1) * width)
         update(2, (part, slice(None)), b_full[part, :], True)
         give(2, part)
-    for b in range(blocks):
-        lanes = slice(b * LANES, (b + 1) * LANES)
-        update(3, (slice(None), lanes), b_full[rows + b * 4 * LANES : rows + (b + 1) * 4 * LANES, :], True)
-        give(3, (slice(None), lanes))
+    for r in range(blocks):
+        part = slice(r * LANES, (r + 1) * LANES)
+        for b in range(blocks):
+            start = rows + b * width + r * LANES
+            update(3, (part, slice(b * LANES, (b + 1) * LANES)), b_full[start : start + LANES, :], True)
+        give(3, part)
     for j in range(3):
         update(0, (j,), a_full[j * width : (j + 1) * width, :], True)
         give(0, j)
@@ -831,11 +886,11 @@
         copy.wait()
 
 
-def run_adam(meta, squares, moved, a_parts, b_parts, states):
+def run_adam(meta, squares, moved, a_full, b_full, states):
     held = pl.BlockSpec(memory_space=pltpu.HBM)
     here = pl.BlockSpec(memory_space=pltpu.VMEM)
     blocks = states[-4].shape[1] // LANES
-    args = (squares,) + tuple(moved) + tuple(a_parts) + tuple(b_parts)
+    args = (squares,) + tuple(moved) + (in_vmem(a_full), in_vmem(b_full))
     return pl.pallas_call(
         functools.partial(adam_kernel, len(moved)),
         in_specs=[pl.BlockSpec(memory_space=pltpu.SMEM)] + [here] * (len(args) + len(states)),
@@ -843,14 +898,12 @@
         out_shape=[shape((1, 1))] + [shape(s.shape) for s in states],
         scratch_shapes=[
             pltpu.VMEM((len(moved) + 1, 8, LANES), F32),
-            pltpu.VMEM((8 * a_parts[0].shape[0], LANES), F32),
-            pltpu.VMEM((8 * b_parts[0].shape[0], LANES), F32),
             pltpu.SemaphoreType.DMA((6 * blocks + 3 * 3 + 3 * 4,)),
         ]
         + [pltpu.VMEM(s.shape, F32) for s in states],
         compiler_params=params(18),
         name="adam",
-    )(meta, *args, *(s if n % 3 == 2 else in_vmem(s) for n, s in enumerate(states)))
+    )(meta, *args, *(in_vmem(s) if n < 12 or n % 3 < 2 else s for n, s in enumerate(states)))
 
 
 def shares(mesh, *args):
@@ -914,7 +967,7 @@
     up_flat, down_flat, classes = flat_up(up_weight), flat_down(down_weight), flat_class(class_weight)
     a_send, b_send = pack(meta, qkv_weight, out_weight, split_bias, up_flat, down_flat)
     turns = range(1, plane.heads)
-    a_first = [plane.along(a_send, r) for r in turns]
+    a_first = plane.round_on(plane.round(a_send))
     b_first = plane.round(b_send)
     a_near = plane.spread(after(jnp.concatenate([v[:-8] for v in a_first], 0), b_first[0]))
     b_first = plane.round_on(b_first)
@@ -931,7 +984,7 @@
         meta,
         labels,
         task_id,
-        pre_one,
+        in_vmem(pre_one),
         out_grad,
         norm_params,
         classes,
@@ -947,27 +1000,33 @@
         meta, back_one, tokens_in, qkv, prob, context, wout, (norm_grad, class_grad, up_bias_grad), False
     )
     b_own = plane.scatter(b_parts, a_give)
-    b_crossed, b_near = plane.rejoin(b_own)
+    b_crossed, b_near = plane.core(b_own), plane.spread(b_own)
     a_parts = plane.quarters(a_keep, a_give, quarter)
     back_one = after(back_one, a_parts, b_crossed)
     input_grad = run_rest(meta, back_one, qkv, prob, wout, wqkv, own, 0)
-    b_parts = plane.rejoin_on(b_own, b_crossed, after(b_near, input_grad))
     a_own = plane.scatter(a_parts, input_grad)
+    b_near = after(b_near, input_grad)
+    b_corner = plane.corners(b_near)
     a_crossed, a_near = plane.rejoin(a_own)
     input_grad = run_rest(meta, after(back_one, a_crossed), qkv, prob, wout, wqkv, own, 1, input_grad)
-    a_parts = plane.rejoin_on(a_own, a_crossed, after(a_near, input_grad))
-    squares = squares_of(meta, a_parts, 4 * width + 8, (squares_of(meta, b_parts),))
-    moved = tuple(plane.along(squares, r) for r in turns)
+    b_near, b_corner, a_near = after((b_near, b_corner, a_near), input_grad)
+    b_parts = plane.rejoin_on(b_own, b_crossed, (b_near[2], b_near[1]) + b_corner)
+    a_parts = plane.rejoin_on(a_own, a_crossed, a_near)
+    squares = squares_of(meta, a_parts, b_parts, 4 * width + 8)
+    a_full, b_full, *held = run_ready(
+        meta, after(a_parts, squares), b_parts, (qkv_weight, out_weight, up_flat, down_flat)
+    )
+    moved = after(tuple(plane.along(squares, r) for r in turns), b_full)
     states = (
-        (qkv_first, qkv_second, qkv_weight)
-        + (out_first, out_second, out_weight)
-        + (flat_up(up_first), flat_up(up_second), up_flat)
-        + (flat_down(down_first), flat_down(down_second), down_flat)
+        (qkv_first, qkv_second, held[0])
+        + (out_first, out_second, held[1])
+        + (flat_up(up_first), flat_up(up_second), held[2])
+        + (flat_down(down_first), flat_down(down_second), held[3])
         + (split_first, split_second, split_bias)
         + (norm_first, norm_second, norm_params)
         + (flat_class(class_first), flat_class(class_second), classes)
     )
-    grad_norm, *new = run_adam(meta, squares, moved, a_parts, b_parts, states)
+    grad_norm, *new = run_adam(meta, squares, moved, a_full, b_full, states)
     new[6:9] = [v.reshape(up_weight.shape) for v in new[6:9]]
     new[9:12] = [v.reshape(down_weight.shape) for v in new[9:12]]
     new[18:21] = [jnp.transpose(v, (0, 2, 1)) for v in new[18:21]]

time: 171 us -> 160 us (0.936)
  waiting for transfers between devices: 61.4 us -> 49 us
  starting transfers between devices: 42.9 us -> 47.3 us
    ppermute x8 -> x7, waiting for transfers between devices: 23 us -> 11 us  [along(): return lax.ppermute(value, 'head', pairs(self.heads, bit))]
    ppermute x8 -> x9, waiting for transfers between devices: 17.4 us -> 14.2 us  [other(): return lax.ppermute(value, 'rep', pairs(self.rep, 1))]
    ppermute x4 -> x3, waiting for transfers between devices: 5.12 us -> 2.55 us  [corner(): lax.ppermute(value, ('batch', 'rep'), pairs(self.batch * self.rep, 2 * se...]
    ppermute x8 -> x9, waiting for transfers between devices: 2.05 us -> 4.58 us  [side(): return lax.ppermute(value, 'batch', pairs(self.batch, 2))]
    pallas_call x1, Pallas kernels: 19.8 us -> 17.7 us  [run_feed(): pl.pallas_call(functools.partial(feed_kernel, len(first), given), grid_sp...]
    ppermute x1 -> x2, waiting for transfers between devices: 7.14 us -> 9.19 us  [round_on(): return (near, far, last + lax.ppermute(far, 'head', [(1, 0), (2, 3)]))]
    pallas_call x2, Pallas kernels: 1.6 us -> 3.47 us  [the longest x1 2.45 us: run_ready(): pl.pallas_call(functools.partial(ready_kernel, len(a_parts)), in_specs=[p...]
    ppermute x8 -> x7, starting transfers between devices: 13.6 us -> 15.4 us  [along(): return lax.ppermute(value, 'head', pairs(self.heads, bit))]
  transfers between devices with their start and end apart: 50 -> 53, of which waited for: 22 -> 21; matrix products, arithmetic and copies ran while one was open for 1% -> 0% of each run, Pallas kernels for 17% -> 21%
where the time goes in v4:
time: 160 us
  Pallas kernels  60 us (38%)
  waiting for transfers between devices  49 us (31%)
  starting transfers between devices  47.3 us (30%)
  other arithmetic  1.65 us (1%)
  between operations  1.64 us (1%)
    pallas_call x1, Pallas kernels, run_feed(): pl.pallas_call(functools.partial(feed_kernel, len(first), given), grid_sp...  17.7 us
    ppermute x7, starting transfers between devices, along(): return lax.ppermute(value, 'head', pairs(self.heads, bit))  15.4 us
    pallas_call x2, Pallas kernels, run_rest(): pl.pallas_call(rest_kernel, grid_spec=pltpu.PrefetchScalarGridSpec(num_sc...  14.9 us
    ppermute x9, waiting for transfers between devices, other(): return lax.ppermute(value, 'rep', pairs(self.rep, 1))  14.2 us
    ppermute x9, starting transfers between devices, side(): return lax.ppermute(value, 'batch', pairs(self.batch, 2))  12.1 us
    ppermute x7, waiting for transfers between devices, along(): return lax.ppermute(value, 'head', pairs(self.heads, bit))  11 us
    ppermute x2, waiting for transfers between devices, round_on(): return (near, far, last + lax.ppermute(far, 'head', [(1, 0), (2, 3)]))  9.19 us
    pallas_call x1, Pallas kernels, run_attention_forward(): pl.pallas_call(functools.partial(attention_forward, len(first), given), g...  8.77 us
  transfers between devices with their start and end apart: 53, of which 21 were waited for; matrix products, arithmetic and copies ran while one was open for 0% of the time, Pallas kernels for 21%

profile of v4, /device:TPU:0, one launch (start us, length us, event | category | flops | bytes accessed | tf_op | source)
XLA Modules:
  0.0 160.0 jit_solution(841912391190547622)
XLA Ops:
  0.8 1.7 %pack.1 = (f32[264,128]{1,0:T(8,128)S(1)}, f32[512,128]{1,0:T(8,128)S(1)}) custom-call(s32[5]{0:T(128)S(1)} %stack.20.meta, f32[3,512,128]{2,1,0:T(8,128)} %refs_18_.2, f32[128,512]{1,0:T(8,128)} %refs_19_.2, f32[6,128]{1,0:T(8,128)} %refs_19_.3, f32[2048,128]{1,0:T(8,128)} %bitcast.27, f32[512,512]{1,0:T(8,128)} %bitcast.30), custom_call_target="tpu_custom_call" | custom-call | tf_op jit(solution)/shard_map/pack/pallas_call | solution.py:202
  2.5 4.1 %collective-permute-start.1 = (f32[264,128]{1,0:T(8,128)S(1)}, f32[264,128]{1,0:T(8,128)S(1)}, u32[]{:S(2)}, u32[]{:S(2)}) collective-permute-start(f32[264,128]{1,0:T(8,128)S(1)} %get-tuple-element.104), channel_id=1, source_target_pairs={{0,16},{8,24},{16,0},{24,8},{1,17},{9,25},{17,1},{25,9},{2,18},{10... | collective-permute-start | bytes 405512 | tf_op jit(solution)/shard_map/ppermute | solution.py:128
  6.6 1.6 collective-permute-start.4
  9.3 3.9 %collective-permute-done.1.refs_6_.refs_8_ = f32[264,128]{1,0:T(8,128)S(1)} collective-permute-done((f32[264,128]{1,0:T(8,128)S(1)}, f32[264,128]{1,0:T(8,128)S(1)}, u32[]{:S(2)}, u32[]{:S(2)}) %collective-permute-start.1) | collective-permute-done | bytes 135200 | tf_op jit(solution)/shard_map/ppermute | solution.py:128
  14.5 4.8 %collective-permute-start.14 = (f32[512,128]{1,0:T(8,128)S(1)}, f32[512,128]{1,0:T(8,128)S(1)}, u32[]{:S(2)}, u32[]{:S(2)}) collective-permute-start(f32[512,128]{1,0:T(8,128)S(1)} %get-tuple-element.105), channel_id=1, source_target_pairs={{0,16},{8,24},{16,0},{24,8},{1,17},{9,25},{17,1},{25,9},{2,18},{10... | collective-permute-start | bytes 786440 | tf_op jit(solution)/shard_map/ppermute | solution.py:128
  19.3 1.7 %collective-permute-done.refs_5_.refs_7_ = f32[264,128]{1,0:T(8,128)S(1)} collective-permute-done((f32[264,128]{1,0:T(8,128)S(1)}, f32[264,128]{1,0:T(8,128)S(1)}, u32[]{:S(2)}, u32[]{:S(2)}) %collective-permute-start) | collective-permute-done | bytes 135200 | tf_op jit(solution)/shard_map/ppermute | solution.py:128
  22.6 1.6 %collective-permute-start.5 = (f32[768,128]{1,0:T(8,128)S(1)}, f32[768,128]{1,0:T(8,128)S(1)}, u32[]{:S(2)}, u32[]{:S(2)}) collective-permute-start(f32[768,128]{1,0:T(8,128)S(1)} %pad_maximum_fusion.1), channel_id=1, source_target_pairs={{0,4},{2,6},{4,0},{6,2},{1,5},{3,7},{5,1},{7,3},{8,12},{10,14},{12... | collective-permute-start | bytes 1179656 | tf_op jit(solution)/shard_map/ppermute | solution.py:119
  24.2 1.5 collective-permute-start.6
  26.4 4.8 %collective-permute-done.14.refs_11_ = f32[512,128]{1,0:T(8,128)S(1)} collective-permute-done((f32[512,128]{1,0:T(8,128)S(1)}, f32[512,128]{1,0:T(8,128)S(1)}, u32[]{:S(2)}, u32[]{:S(2)}) %collective-permute-start.14) | collective-permute-done | bytes 262176 | tf_op jit(solution)/shard_map/ppermute | solution.py:128
  32.5 7.8 %collective-permute-done.16 = f32[512,128]{1,0:T(8,128)S(1)} collective-permute-done((f32[512,128]{1,0:T(8,128)S(1)}, f32[512,128]{1,0:T(8,128)S(1)}, u32[]{:S(2)}, u32[]{:S(2)}) %collective-permute-start.16) | collective-permute-done | bytes 262176 | tf_op jit(solution)/shard_map/ppermute | solution.py:135
  40.3 1.6 collective-permute-start.7
  41.9 1.6 collective-permute-start.8
  44.7 3.3 %collective-permute-done.7.refs_10_ = f32[384,128]{1,0:T(8,128)S(1)} collective-permute-done((f32[384,128]{1,0:T(8,128)S(1)}, f32[384,128]{1,0:T(8,128)S(1)}, u32[]{:S(2)}, u32[]{:S(2)}) %collective-permute-start.7) | collective-permute-done | bytes 196640 | tf_op jit(solution)/shard_map/ppermute | solution.py:122
  51.9 8.8 %attention_forward.1 = (bf16[4,1024,384]{2,1,0:T(8,128)(2,1)}, f32[4,8,256,128]{3,2,1,0:T(8,128)}, bf16[1024,512]{1,0:T(8,128)(2,1)}, f32[1024,512]{1,0:T(8,128)...) custom-call(s32[5]{0:T(128)S(1)} %stack.20.meta, s32[8]{0:T(128)S(1)} %copy-done.26, ...), custom_call_target="tpu_custom_call" | custom-call | flops 2684354560 | bytes 16777216 | tf_op jit(solution)/shard_map/attention_forward/pallas_call | solution.py:347
  60.7 2.8 %collective-permute-done.17.refs_13_ = f32[1536,128]{1,0:T(8,128)S(1)} collective-permute-done((f32[1536,128]{1,0:T(8,128)S(1)}, f32[1536,128]{1,0:T(8,128)S(1)}, u32[]{:S(2)}, u32[]{:S(2)}) %collective-permute-start.17) | collective-permute-done | bytes 786464 | tf_op jit(solution)/shard_map/ppermute | solution.py:119
  64.1 1.6 collective-permute-start.20
  66.2 6.0 %collective-permute-done.19.refs_15_ = f32[768,128]{1,0:T(8,128)S(1)} collective-permute-done((f32[768,128]{1,0:T(8,128)S(1)}, f32[768,128]{1,0:T(8,128)S(1)}, u32[]{:S(2)}, u32[]{:S(2)}) %collective-permute-start.19) | collective-permute-done | bytes 393248 | tf_op jit(solution)/shard_map/ppermute | solution.py:122
  74.5 17.7 %feed_both.1 = (f32[1024,512]{1,0:T(8,128)}, f32[1024,512]{1,0:T(8,128)}, f32[8,512]{1,0:T(8,128)S(1)}, f32[9,3,512]{2,1,0:T(4,128)S(1)}, f32[8,512]{1,0:T(8,128...) custom-call(s32[5]{0:T(128)S(1)} %stack.20.meta, s32[8]{0:T(128)S(1)} %copy-done.27, s32[8]{0:T(128)S(1)} %copy-done.28, ...), custom_call_target="tpu_custom_call" | custom-call | flops 38654705664 | bytes 20971520 | tf_op jit(solution)/shard_map/feed_both/pallas_call | solution.py:513
  92.3 2.7 %collective-permute-done.26 = f32[2048,128]{1,0:T(8,128)} collective-permute-done((f32[2048,128]{1,0:T(8,128)S(1)}, f32[2048,128]{1,0:T(8,128)}, u32[]{:S(2)}, u32[]{:S(2)}) %collective-permute-start.26) | collective-permute-done | bytes 1048608 | tf_op jit(solution)/shard_map/ppermute | solution.py:116
  96.5 1.5 collective-permute-start.28
  100.0 6.7 %attention_own.1 = (bf16[1024,384]{1,0:T(8,128)(2,1)}, f32[1120,128]{1,0:T(8,128)S(1)}, f32[1120,128]{1,0:T(8,128)S(1)}) custom-call(s32[5]{0:T(128)S(1)} %stack.20.meta, f32[1024,512]{1,0:T(8,128)} %get-tuple-element.135.back_ref, bf16[1024,512]{1,0:T(8,128)(2,1)S(1)} %copy-done.25, bf16[4,1024,384]{2,1,0:T(8,128)(2,1)} %get-tuple-element.117.qkv, ...), custom_call_target="tpu_custom_call" | custom-call | flops 4294967296 | bytes 8388608 | tf_op jit(solution)/shard_map/attention_own/pallas_call | solution.py:654
  106.7 5.0 %collective-permute-done.29 = f32[512,128]{1,0:T(8,128)S(1)} collective-permute-done((f32[512,128]{1,0:T(8,128)S(1)}, f32[512,128]{1,0:T(8,128)S(1)}, u32[]{:S(2)}, u32[]{:S(2)}) %collective-permute-start.29) | collective-permute-done | bytes 262176 | tf_op jit(solution)/shard_map/ppermute | solution.py:122
  113.9 1.6 collective-permute-start.32
  117.4 7.4 %attention_rest.2.refs_0_ = f32[1024,512]{1,0:T(8,128)} custom-call(s32[5]{0:T(128)S(1)} %stack.20.meta, f32[1024,512]{1,0:T(8,128)} %get-tuple-element.135.back_ref, bf16[4,1024,384]{2,1,0:T(8,128)(2,1)} %get-tuple-element.117.qkv, f32[4,8,256,128]{3,2,1,0:T(8,128)} %get-tuple-element.118.prob, bf16[512,512]{1,0:T(8,128)(2,1)} %get-tuple-element.120.wout, ...), custom_call_target="tpu_custom_call" | custom-call | flops 68719476736 | bytes 1024 | tf_op jit(solution)/shard_map/attention_rest/pallas_call | solution.py:696
  124.9 2.5 %collective-permute-done.34 = f32[280,128]{1,0:T(8,128)S(1)} collective-permute-done((f32[280,128]{1,0:T(8,128)S(1)}, f32[280,128]{1,0:T(8,128)S(1)}, u32[]{:S(2)}, u32[]{:S(2)}) %collective-permute-start.34) | collective-permute-done | bytes 143392 | tf_op jit(solution)/shard_map/ppermute | solution.py:125
  128.5 1.6 collective-permute-start.39
  131.8 1.8 %collective-permute-start.42 = (f32[280,128]{1,0:T(8,128)S(1)}, f32[280,128]{1,0:T(8,128)S(1)}, u32[]{:S(2)}, u32[]{:S(2)}) collective-permute-start(f32[280,128]{1,0:T(8,128)S(1)} %add_add_fusion.1.refs_0_), channel_id=1, source_target_pairs={{0,5},{1,4},{2,7},{3,6},{4,1},{5,0},{6,3},{7,2},{8,13},{9,12},{10,... | collective-permute-start | bytes 430088 | tf_op jit(solution)/shard_map/ppermute | solution.py:125
  133.6 7.4 %attention_rest.3 = f32[1024,512]{1,0:T(8,128)} custom-call(s32[5]{0:T(128)S(1)} %stack.20.meta, f32[1024,512]{1,0:T(8,128)} %get-tuple-element.135.back_ref, bf16[4,1024,384]{2,1,0:T(8,128)(2,1)} %get-tuple-element.117.qkv, f32[4,8,256,128]{3,2,1,0:T(8,128)} %get-tuple-element.118.prob, ...), custom_call_target="tpu_custom_call", output_to_operand_aliasing={{}: (7, {})} | custom-call | flops 68719476736 | bytes 1024 | tf_op jit(solution)/shard_map/attention_rest/pallas_call | solution.py:696
  145.4 2.1 %collective-permute-start.51 = (f32[8,128]{1,0:T(8,128)S(1)}, f32[8,128]{1,0:T(8,128)S(1)}, u32[]{:S(2)}, u32[]{:S(2)}) collective-permute-start(f32[8,128]{1,0:T(8,128)S(1)} %squares.1), channel_id=1, source_target_pairs={{0,16},{8,24},{16,0},{24,8},{1,17},{9,25},{17,1},{25,9},{2,18},{10... | collective-permute-start | bytes 12296 | tf_op jit(solution)/shard_map/ppermute | solution.py:128
  147.6 2.2 %collective-permute-start.52 = (f32[8,128]{1,0:T(8,128)S(1)}, f32[8,128]{1,0:T(8,128)S(1)}, u32[]{:S(2)}, u32[]{:S(2)}) collective-permute-start(f32[8,128]{1,0:T(8,128)S(1)} %squares.1), channel_id=1, source_target_pairs={{0,24},{8,16},{16,8},{24,0},{1,25},{9,17},{17,9},{25,1},{2,26},{10... | collective-permute-start | bytes 12296 | tf_op jit(solution)/shard_map/ppermute | solution.py:128
  149.8 2.4 %ready.1 = (f32[2240,128]{1,0:T(8,128)S(1)}, f32[4096,128]{1,0:T(8,128)S(1)}, f32[3,512,128]{2,1,0:T(8,128)S(1)}, f32[128,512]{1,0:T(8,128)S(1)}, f32[2048,128]{1,0:T(8,128)S(1)}, /*index=5*/f32[512,512]{1,0:T(8,128)S(1)}) custom-call(s32[5]{0:T(128)S(1)} %stack.20.meta, f32[280,128]{1,0:T(8,128)S(1)} %add_add_fusion.1.refs_0_, ...), custom_call_target="tpu_custom_call" | custom-call | flops 68719476736 | bytes 1024 | tf_op jit(solution)/shard_map/ready/pallas_call | solution.py:801
  153.1 6.7 %adam.1 = (f32[1,1]{1,0:T(1,128)}, f32[3,512,128]{2,1,0:T(8,128)}, f32[3,512,128]{2,1,0:T(8,128)}, f32[3,512,128]{2,1,0:T(8,128)}, f32[128,512]{1,0:T(8,128)}, /...) custom-call(s32[5]{0:T(128)S(1)} %stack.20.meta, ...), custom_call_target="tpu_custom_call" | custom-call | tf_op jit(solution)/shard_map/adam/pallas_call | solution.py:894
  (161 shorter events, 30.0 us)
Async XLA Ops:
  2.5 10.7 %collective-permute-start.1 = (f32[264,128]{1,0:T(8,128)S(1)}, f32[264,128]{1,0:T(8,128)S(1)}, u32[]{:S(2)}, u32[]{:S(2)}) collective-permute-start(f32[264,128]{1,0:T(8,128)S(1)} %get-tuple-element.104), channel_id=1, source_target_pairs={{0,16},{8,24},{16,0},{24,8},{1,17},{9,25},{17,1},{25,9},{2,18},{10... | collective-permute-start | bytes 405512 | tf_op jit(solution)/shard_map/ppermute | solution.py:128
  6.6 16.0 %collective-permute-start.4 = (f32[512,128]{1,0:T(8,128)S(1)}, f32[512,128]{1,0:T(8,128)S(1)}, u32[]{:S(2)}, u32[]{:S(2)}) collective-permute-start(f32[512,128]{1,0:T(8,128)S(1)} %get-tuple-element.105), channel_id=1, source_target_pairs={{0,8},{8,0},{16,24},{24,16},{1,9},{9,1},{17,25},{25,17},{2,10},{10... | collective-permute-start | bytes 786440 | tf_op jit(solution)/shard_map/ppermute | solution.py:128
  8.2 12.8 %collective-permute-start = (f32[264,128]{1,0:T(8,128)S(1)}, f32[264,128]{1,0:T(8,128)S(1)}, u32[]{:S(2)}, u32[]{:S(2)}) collective-permute-start(f32[264,128]{1,0:T(8,128)S(1)} %get-tuple-element.104), channel_id=1, source_target_pairs={{0,8},{8,0},{16,24},{24,16},{1,9},{9,1},{17,25},{25,17},{2,10},{10... | collective-permute-start | bytes 405512 | tf_op jit(solution)/shard_map/ppermute | solution.py:128
  8.6 12.4 %collective-permute-start.2 = (f32[264,128]{1,0:T(8,128)S(1)}, f32[264,128]{1,0:T(8,128)S(1)}, u32[]{:S(2)}, u32[]{:S(2)}) collective-permute-start(f32[264,128]{1,0:T(8,128)S(1)} %get-tuple-element.104), channel_id=1, source_target_pairs={{8,16},{16,8},{9,17},{17,9},{10,18},{18,10},{11,19},{19,11},{12,20... | collective-permute-start | bytes 405512 | tf_op jit(solution)/shard_map/ppermute | solution.py:131
  13.2 9.2 %collective-permute-start.3 = (f32[264,128]{1,0:T(8,128)S(1)}, f32[264,128]{1,0:T(8,128)S(1)}, u32[]{:S(2)}, u32[]{:S(2)}) collective-permute-start(f32[264,128]{1,0:T(8,128)S(1)} %collective-permute-done.1.refs_6_.refs_8_), channel_id=1, source_target_pairs={{8,0},{16,24},{9,1},{17,25},{10,2},{18,26},{11,3},{19,27},{12,4},{... | collective-permute-start | bytes 405512 | tf_op jit(solution)/shard_map/ppermute | solution.py:135
  14.5 16.7 %collective-permute-start.14 = (f32[512,128]{1,0:T(8,128)S(1)}, f32[512,128]{1,0:T(8,128)S(1)}, u32[]{:S(2)}, u32[]{:S(2)}) collective-permute-start(f32[512,128]{1,0:T(8,128)S(1)} %get-tuple-element.105), channel_id=1, source_target_pairs={{0,16},{8,24},{16,0},{24,8},{1,17},{9,25},{17,1},{25,9},{2,18},{10... | collective-permute-start | bytes 786440 | tf_op jit(solution)/shard_map/ppermute | solution.py:128
  22.6 17.7 %collective-permute-start.5 = (f32[768,128]{1,0:T(8,128)S(1)}, f32[768,128]{1,0:T(8,128)S(1)}, u32[]{:S(2)}, u32[]{:S(2)}) collective-permute-start(f32[768,128]{1,0:T(8,128)S(1)} %pad_maximum_fusion.1), channel_id=1, source_target_pairs={{0,4},{2,6},{4,0},{6,2},{1,5},{3,7},{5,1},{7,3},{8,12},{10,14},{12... | collective-permute-start | bytes 1179656 | tf_op jit(solution)/shard_map/ppermute | solution.py:119
  24.2 17.7 %collective-permute-start.6 = (f32[768,128]{1,0:T(8,128)S(1)}, f32[768,128]{1,0:T(8,128)S(1)}, u32[]{:S(2)}, u32[]{:S(2)}) collective-permute-start(f32[768,128]{1,0:T(8,128)S(1)} %pad_maximum_fusion.1), channel_id=1, source_target_pairs={{0,1},{1,0},{2,3},{3,2},{4,5},{5,4},{6,7},{7,6},{8,9},{9,8},{10,11... | collective-permute-start | bytes 1179656 | tf_op jit(solution)/shard_map/ppermute | solution.py:122
  31.1 9.1 %collective-permute-start.16 = (f32[512,128]{1,0:T(8,128)S(1)}, f32[512,128]{1,0:T(8,128)S(1)}, u32[]{:S(2)}, u32[]{:S(2)}) collective-permute-start(f32[512,128]{1,0:T(8,128)S(1)} %collective-permute-done.14.refs_11_), channel_id=1, source_target_pairs={{8,0},{16,24},{9,1},{17,25},{10,2},{18,26},{11,3},{19,27},{12,4},{... | collective-permute-start | bytes 786440 | tf_op jit(solution)/shard_map/ppermute | solution.py:135
  32.4 15.6 %collective-permute-start.9 = (f32[768,128]{1,0:T(8,128)S(1)}, f32[768,128]{1,0:T(8,128)S(1)}, u32[]{:S(2)}, u32[]{:S(2)}) collective-permute-start(f32[768,128]{1,0:T(8,128)S(1)} %pad_maximum_fusion.1), channel_id=1, source_target_pairs={{0,2},{2,0},{4,6},{6,4},{1,3},{3,1},{5,7},{7,5},{8,10},{10,8},{12,... | collective-permute-start | bytes 1179656 | tf_op jit(solution)/shard_map/ppermute | solution.py:116
  40.3 7.7 %collective-permute-start.7 = (f32[384,128]{1,0:T(8,128)S(1)}, f32[384,128]{1,0:T(8,128)S(1)}, u32[]{:S(2)}, u32[]{:S(2)}) collective-permute-start(f32[384,128]{1,0:T(8,128)S(1)} %slice.39), channel_id=1, source_target_pairs={{0,1},{1,0},{2,3},{3,2},{4,5},{5,4},{6,7},{7,6},{8,9},{9,8},{10,11... | collective-permute-start | bytes 589832 | tf_op jit(solution)/shard_map/ppermute | solution.py:122
  41.9 7.9 %collective-permute-start.8 = (f32[384,128]{1,0:T(8,128)S(1)}, f32[384,128]{1,0:T(8,128)S(1)}, u32[]{:S(2)}, u32[]{:S(2)}) collective-permute-start(f32[384,128]{1,0:T(8,128)S(1)} %slice.40), channel_id=1, source_target_pairs={{0,4},{2,6},{4,0},{6,2},{1,5},{3,7},{5,1},{7,3},{8,12},{10,14},{12... | collective-permute-start | bytes 589832 | tf_op jit(solution)/shard_map/ppermute | solution.py:119
  43.6 19.9 %collective-permute-start.17 = (f32[1536,128]{1,0:T(8,128)S(1)}, f32[1536,128]{1,0:T(8,128)S(1)}, u32[]{:S(2)}, u32[]{:S(2)}) collective-permute-start(f32[1536,128]{1,0:T(8,128)S(1)} %pad_maximum_fusion), channel_id=1, source_target_pairs={{0,4},{2,6},{4,0},{6,2},{1,5},{3,7},{5,1},{7,3},{8,12},{10,14},{12... | collective-permute-start | bytes 2359304 | tf_op jit(solution)/shard_map/ppermute | solution.py:119
  44.2 19.3 %collective-permute-start.18 = (f32[1536,128]{1,0:T(8,128)S(1)}, f32[1536,128]{1,0:T(8,128)S(1)}, u32[]{:S(2)}, u32[]{:S(2)}) collective-permute-start(f32[1536,128]{1,0:T(8,128)S(1)} %pad_maximum_fusion), channel_id=1, source_target_pairs={{0,1},{1,0},{2,3},{3,2},{4,5},{5,4},{6,7},{7,6},{8,9},{9,8},{10,11... | collective-permute-start | bytes 2359304 | tf_op jit(solution)/shard_map/ppermute | solution.py:122
  63.5 8.6 %collective-permute-start.19 = (f32[768,128]{1,0:T(8,128)S(1)}, f32[768,128]{1,0:T(8,128)S(1)}, u32[]{:S(2)}, u32[]{:S(2)}) collective-permute-start(f32[768,128]{1,0:T(8,128)S(1)} %slice.32), channel_id=1, source_target_pairs={{0,1},{1,0},{2,3},{3,2},{4,5},{5,4},{6,7},{7,6},{8,9},{9,8},{10,11... | collective-permute-start | bytes 1179656 | tf_op jit(solution)/shard_map/ppermute | solution.py:122
  64.1 8.5 %collective-permute-start.20 = (f32[768,128]{1,0:T(8,128)S(1)}, f32[768,128]{1,0:T(8,128)S(1)}, u32[]{:S(2)}, u32[]{:S(2)}) collective-permute-start(f32[768,128]{1,0:T(8,128)S(1)} %slice.33), channel_id=1, source_target_pairs={{0,4},{2,6},{4,0},{6,2},{1,5},{3,7},{5,1},{7,3},{8,12},{10,14},{12... | collective-permute-start | bytes 1179656 | tf_op jit(solution)/shard_map/ppermute | solution.py:119
  65.7 8.8 %collective-permute-start.21 = (f32[1536,128]{1,0:T(8,128)S(1)}, f32[1536,128]{1,0:T(8,128)S(1)}, u32[]{:S(2)}, u32[]{:S(2)}) collective-permute-start(f32[1536,128]{1,0:T(8,128)S(1)} %pad_maximum_fusion), channel_id=1, source_target_pairs={{0,2},{2,0},{4,6},{6,4},{1,3},{3,1},{5,7},{7,5},{8,10},{10,8},{12,... | collective-permute-start | bytes 2359304 | tf_op jit(solution)/shard_map/ppermute | solution.py:116
  65.7 8.8 %collective-permute-start.22 = (f32[1536,128]{1,0:T(8,128)S(1)}, f32[1536,128]{1,0:T(8,128)S(1)}, u32[]{:S(2)}, u32[]{:S(2)}) collective-permute-start(f32[1536,128]{1,0:T(8,128)S(1)} %collective-permute-done.17.refs_13_), channel_id=1, source_target_pairs={{0,2},{2,0},{4,6},{6,4},{1,3},{3,1},{5,7},{7,5},{8,10},{10,8},{12,... | collective-permute-start | bytes 2359304 | tf_op jit(solution)/shard_map/ppermute | solution.py:116
  66.2 8.3 %collective-permute-start.23 = (f32[1536,128]{1,0:T(8,128)S(1)}, f32[1536,128]{1,0:T(8,128)S(1)}, u32[]{:S(2)}, u32[]{:S(2)}) collective-permute-start(f32[1536,128]{1,0:T(8,128)S(1)} %collective-permute-done.18.refs_14_), channel_id=1, source_target_pairs={{0,2},{2,0},{4,6},{6,4},{1,3},{3,1},{5,7},{7,5},{8,10},{10,8},{12,... | collective-permute-start | bytes 2359304 | tf_op jit(solution)/shard_map/ppermute | solution.py:116
  96.5 10.3 %collective-permute-start.28 = (f32[512,128]{1,0:T(8,128)S(1)}, f32[512,128]{1,0:T(8,128)S(1)}, u32[]{:S(2)}, u32[]{:S(2)}) collective-permute-start(f32[512,128]{1,0:T(8,128)S(1)} %get-tuple-element.185), channel_id=1, source_target_pairs={{0,4},{2,6},{4,0},{6,2},{1,5},{3,7},{5,1},{7,3},{8,12},{10,14},{12... | collective-permute-start | bytes 786440 | tf_op jit(solution)/shard_map/ppermute | solution.py:119
  98.0 13.7 %collective-permute-start.29 = (f32[512,128]{1,0:T(8,128)S(1)}, f32[512,128]{1,0:T(8,128)S(1)}, u32[]{:S(2)}, u32[]{:S(2)}) collective-permute-start(f32[512,128]{1,0:T(8,128)S(1)} %get-tuple-element.186), channel_id=1, source_target_pairs={{0,1},{1,0},{2,3},{3,2},{4,5},{5,4},{6,7},{7,6},{8,9},{9,8},{10,11... | collective-permute-start | bytes 786440 | tf_op jit(solution)/shard_map/ppermute | solution.py:122
  99.3 12.4 %collective-permute-start.30 = (f32[512,128]{1,0:T(8,128)S(1)}, f32[512,128]{1,0:T(8,128)S(1)}, u32[]{:S(2)}, u32[]{:S(2)}) collective-permute-start(f32[512,128]{1,0:T(8,128)S(1)} %get-tuple-element.184), channel_id=1, source_target_pairs={{0,5},{1,4},{2,7},{3,6},{4,1},{5,0},{6,3},{7,2},{8,13},{9,12},{10,... | collective-permute-start | bytes 786440 | tf_op jit(solution)/shard_map/ppermute | solution.py:125
  111.9 15.7 %collective-permute-start.36 = (f32[512,128]{1,0:T(8,128)S(1)}, f32[512,128]{1,0:T(8,128)S(1)}, u32[]{:S(2)}, u32[]{:S(2)}) collective-permute-start(f32[512,128]{1,0:T(8,128)S(1)} %add_add_fusion.refs_8_), channel_id=1, source_target_pairs={{0,4},{2,6},{4,0},{6,2},{1,5},{3,7},{5,1},{7,3},{8,12},{10,14},{12... | collective-permute-start | bytes 786440 | tf_op jit(solution)/shard_map/ppermute | solution.py:119
  112.9 14.6 %collective-permute-start.37 = (f32[512,128]{1,0:T(8,128)S(1)}, f32[512,128]{1,0:T(8,128)S(1)}, u32[]{:S(2)}, u32[]{:S(2)}) collective-permute-start(f32[512,128]{1,0:T(8,128)S(1)} %add_add_fusion.refs_8_), channel_id=1, source_target_pairs={{0,1},{1,0},{2,3},{3,2},{4,5},{5,4},{6,7},{7,6},{8,9},{9,8},{10,11... | collective-permute-start | bytes 786440 | tf_op jit(solution)/shard_map/ppermute | solution.py:122
  113.9 11.0 %collective-permute-start.32 = (f32[280,128]{1,0:T(8,128)S(1)}, f32[280,128]{1,0:T(8,128)S(1)}, u32[]{:S(2)}, u32[]{:S(2)}) collective-permute-start(f32[280,128]{1,0:T(8,128)S(1)} %get-tuple-element.189), channel_id=1, source_target_pairs={{0,4},{2,6},{4,0},{6,2},{1,5},{3,7},{5,1},{7,3},{8,12},{10,14},{12... | collective-permute-start | bytes 430088 | tf_op jit(solution)/shard_map/ppermute | solution.py:119
  115.5 9.4 %collective-permute-start.33 = (f32[280,128]{1,0:T(8,128)S(1)}, f32[280,128]{1,0:T(8,128)S(1)}, u32[]{:S(2)}, u32[]{:S(2)}) collective-permute-start(f32[280,128]{1,0:T(8,128)S(1)} %get-tuple-element.190), channel_id=1, source_target_pairs={{0,1},{1,0},{2,3},{3,2},{4,5},{5,4},{6,7},{7,6},{8,9},{9,8},{10,11... | collective-permute-start | bytes 430088 | tf_op jit(solution)/shard_map/ppermute | solution.py:122
  116.2 11.2 %collective-permute-start.34 = (f32[280,128]{1,0:T(8,128)S(1)}, f32[280,128]{1,0:T(8,128)S(1)}, u32[]{:S(2)}, u32[]{:S(2)}) collective-permute-start(f32[280,128]{1,0:T(8,128)S(1)} %get-tuple-element.188), channel_id=1, source_target_pairs={{0,5},{1,4},{2,7},{3,6},{4,1},{5,0},{6,3},{7,2},{8,13},{9,12},{10,... | collective-permute-start | bytes 430088 | tf_op jit(solution)/shard_map/ppermute | solution.py:125
  127.6 13.4 %collective-permute-start.38 = (f32[256,128]{1,0:T(8,128)S(1)}, f32[256,128]{1,0:T(8,128)S(1)}, u32[]{:S(2)}, u32[]{:S(2)}) collective-permute-start(f32[256,128]{1,0:T(8,128)S(1)} %slice.34), channel_id=1, source_target_pairs={{0,1},{1,0},{2,3},{3,2},{4,5},{5,4},{6,7},{7,6},{8,9},{9,8},{10,11... | collective-permute-start | bytes 393224 | tf_op jit(solution)/shard_map/ppermute | solution.py:122
  128.5 12.5 %collective-permute-start.39 = (f32[256,128]{1,0:T(8,128)S(1)}, f32[256,128]{1,0:T(8,128)S(1)}, u32[]{:S(2)}, u32[]{:S(2)}) collective-permute-start(f32[256,128]{1,0:T(8,128)S(1)} %slice.35), channel_id=1, source_target_pairs={{0,4},{2,6},{4,0},{6,2},{1,5},{3,7},{5,1},{7,3},{8,12},{10,14},{12... | collective-permute-start | bytes 393224 | tf_op jit(solution)/shard_map/ppermute | solution.py:119
  130.1 10.9 %collective-permute-start.40 = (f32[280,128]{1,0:T(8,128)S(1)}, f32[280,128]{1,0:T(8,128)S(1)}, u32[]{:S(2)}, u32[]{:S(2)}) collective-permute-start(f32[280,128]{1,0:T(8,128)S(1)} %add_add_fusion.1.refs_0_), channel_id=1, source_target_pairs={{0,1},{1,0},{2,3},{3,2},{4,5},{5,4},{6,7},{7,6},{8,9},{9,8},{10,11... | collective-permute-start | bytes 430088 | tf_op jit(solution)/shard_map/ppermute | solution.py:122
  130.8 10.2 %collective-permute-start.41 = (f32[280,128]{1,0:T(8,128)S(1)}, f32[280,128]{1,0:T(8,128)S(1)}, u32[]{:S(2)}, u32[]{:S(2)}) collective-permute-start(f32[280,128]{1,0:T(8,128)S(1)} %add_add_fusion.1.refs_0_), channel_id=1, source_target_pairs={{0,4},{2,6},{4,0},{6,2},{1,5},{3,7},{5,1},{7,3},{8,12},{10,14},{12... | collective-permute-start | bytes 430088 | tf_op jit(solution)/shard_map/ppermute | solution.py:119
  131.8 9.2 %collective-permute-start.42 = (f32[280,128]{1,0:T(8,128)S(1)}, f32[280,128]{1,0:T(8,128)S(1)}, u32[]{:S(2)}, u32[]{:S(2)}) collective-permute-start(f32[280,128]{1,0:T(8,128)S(1)} %add_add_fusion.1.refs_0_), channel_id=1, source_target_pairs={{0,5},{1,4},{2,7},{3,6},{4,1},{5,0},{6,3},{7,2},{8,13},{9,12},{10,... | collective-permute-start | bytes 430088 | tf_op jit(solution)/shard_map/ppermute | solution.py:125
  (50 other events, 564.6 us)

commit v5 on v4

--- a/solution.py
+++ b/solution.py
@@ -195,8 +195,8 @@
     places = 8
     width = out.shape[1]
     outs = [
-        shape((4 * width // places + 8, LANES)),
-        shape(((up.shape[0] + down.shape[0] * width // LANES) // places, LANES)),
+        pltpu.VMEM((4 * width // places + 8, LANES), F32),
+        pltpu.VMEM(((up.shape[0] + down.shape[0] * width // LANES) // places, LANES), F32),
     ]
     held = pl.BlockSpec(memory_space=pltpu.HBM)
     return pl.pallas_call(
@@ -205,7 +205,7 @@
             num_scalar_prefetch=1,
             grid=(1,),
             in_specs=[held] * 5,
-            out_specs=[held] * 2,
+            out_specs=[pl.BlockSpec(memory_space=pltpu.VMEM)] * 2,
             scratch_shapes=[pltpu.SemaphoreType.DMA((5 + 2 * (width // LANES),))],
         ),
         out_shape=outs,
@@ -339,7 +339,7 @@
     ]
     scratch = []
     if not given:
-        extra = [pltpu.HBM((groups, width, 3 * LANES), LOW), pltpu.HBM((width, width), LOW)]
+        extra = [pltpu.VMEM((groups, width, 3 * LANES), LOW), pltpu.VMEM((width, width), LOW)]
         out_shape += extra
         out_specs += [whole(e) for e in extra]
         scratch = [pltpu.VMEM((groups, 8, LANES), F32)]
@@ -662,9 +662,9 @@
         ),
         out_shape=out_shape + fixed,
         compiler_params=params(28),
-        cost_estimate=pl.CostEstimate(flops=4 << 30, bytes_accessed=8 << 20, transcendentals=0),
+        cost_estimate=pl.CostEstimate(flops=1073741824, bytes_accessed=1 << 10, transcendentals=0),
         name="attention_own",
-    )(meta, in_hbm(back), tokens, in_hbm(qkv), in_hbm(prob), in_hbm(context), in_hbm(wout), *smalls)
+    )(meta, in_hbm(back), tokens, in_hbm(qkv), in_hbm(prob), in_hbm(context), wout, *smalls)
 
 
 def rest_kernel(meta, back_ref, qkv, prob, wout, wqkv, own, *refs):
@@ -702,8 +702,8 @@
                 by_rows,
                 pl.BlockSpec((groups, few, 3 * LANES), lambda i, m: (0, 2 * block + i, 0)),
                 pl.BlockSpec((groups, seqs, heads * LANES, LANES), lambda i, m: (0, 2 * block + i, 0, 0)),
-                whole(wout),
-                whole(wqkv),
+                resident(wout),
+                resident(wqkv),
                 pl.BlockSpec((few, 3 * LANES), lambda i, m: (2 * block + i, 0)),
             ]
             + [pl.BlockSpec(memory_space=pl.ANY)] * len(held),
@@ -715,7 +715,7 @@
         compiler_params=params(28),
         cost_estimate=pl.CostEstimate(flops=68719476736, bytes_accessed=1 << 10, transcendentals=0),
         name="attention_rest",
-    )(meta, in_hbm(back), in_hbm(qkv), in_hbm(prob), in_hbm(wout), in_hbm(wqkv), in_hbm(own), *held)
+    )(meta, in_hbm(back), in_hbm(qkv), in_hbm(prob), wout, wqkv, in_hbm(own), *held)
 
 
 def places_of(meta):

time: 160 us -> 159 us (level)
  Pallas kernels: 60 us -> 58.2 us
  transfers between devices with their start and end apart: 53 -> 53, of which waited for: 21 -> 22; matrix products, arithmetic and copies ran while one was open for 0% -> 0% of each run, Pallas kernels for 21% -> 19%
where the time goes in v5:
time: 159 us
  Pallas kernels  58.2 us (37%)
  waiting for transfers between devices  50.2 us (32%)
  starting transfers between devices  47.6 us (30%)
  between operations  1.67 us (1%)
    pallas_call x1, Pallas kernels, run_feed(): pl.pallas_call(functools.partial(feed_kernel, len(first), given), grid_sp...  18.1 us
    ppermute x7, starting transfers between devices, along(): return lax.ppermute(value, 'head', pairs(self.heads, bit))  15.4 us
    ppermute x9, waiting for transfers between devices, other(): return lax.ppermute(value, 'rep', pairs(self.rep, 1))  15 us
    pallas_call x2, Pallas kernels, run_rest(): pl.pallas_call(rest_kernel, grid_spec=pltpu.PrefetchScalarGridSpec(num_sc...  13.5 us
    ppermute x9, starting transfers between devices, side(): return lax.ppermute(value, 'batch', pairs(self.batch, 2))  12 us
    ppermute x7, waiting for transfers between devices, along(): return lax.ppermute(value, 'head', pairs(self.heads, bit))  10.3 us
    ppermute x2, waiting for transfers between devices, round_on(): return (near, far, last + lax.ppermute(far, 'head', [(1, 0), (2, 3)]))  9.19 us
    ppermute x9, starting transfers between devices, other(): return lax.ppermute(value, 'rep', pairs(self.rep, 1))  8.69 us
  transfers between devices with their start and end apart: 53, of which 22 were waited for; matrix products, arithmetic and copies ran while one was open for 0% of the time, Pallas kernels for 19%

profile of v5, /device:TPU:0, one launch (start us, length us, event | category | flops | bytes accessed | tf_op | source)
XLA Modules:
  0.0 158.5 jit_solution(4387485312653822972)
XLA Ops:
  0.8 1.7 %pack.1 = (f32[264,128]{1,0:T(8,128)S(1)}, f32[512,128]{1,0:T(8,128)S(1)}) custom-call(s32[5]{0:T(128)S(1)} %stack.20.meta, f32[3,512,128]{2,1,0:T(8,128)} %refs_18_.2, f32[128,512]{1,0:T(8,128)} %refs_19_.2, f32[6,128]{1,0:T(8,128)} %refs_19_.3, f32[2048,128]{1,0:T(8,128)} %bitcast.27, f32[512,512]{1,0:T(8,128)} %bitcast.30), custom_call_target="tpu_custom_call" | custom-call | tf_op jit(solution)/shard_map/pack/pallas_call | solution.py:202
  2.5 4.1 %collective-permute-start.1 = (f32[264,128]{1,0:T(8,128)S(1)}, f32[264,128]{1,0:T(8,128)S(1)}, u32[]{:S(2)}, u32[]{:S(2)}) collective-permute-start(f32[264,128]{1,0:T(8,128)S(1)} %get-tuple-element.104), channel_id=1, source_target_pairs={{0,16},{8,24},{16,0},{24,8},{1,17},{9,25},{17,1},{25,9},{2,18},{10... | collective-permute-start | bytes 405512 | tf_op jit(solution)/shard_map/ppermute | solution.py:128
  6.6 1.6 collective-permute-start.4
  9.3 3.9 %collective-permute-done.1.refs_6_.refs_8_ = f32[264,128]{1,0:T(8,128)S(1)} collective-permute-done((f32[264,128]{1,0:T(8,128)S(1)}, f32[264,128]{1,0:T(8,128)S(1)}, u32[]{:S(2)}, u32[]{:S(2)}) %collective-permute-start.1) | collective-permute-done | bytes 135200 | tf_op jit(solution)/shard_map/ppermute | solution.py:128
  14.5 4.8 %collective-permute-start.14 = (f32[512,128]{1,0:T(8,128)S(1)}, f32[512,128]{1,0:T(8,128)S(1)}, u32[]{:S(2)}, u32[]{:S(2)}) collective-permute-start(f32[512,128]{1,0:T(8,128)S(1)} %get-tuple-element.105), channel_id=1, source_target_pairs={{0,16},{8,24},{16,0},{24,8},{1,17},{9,25},{17,1},{25,9},{2,18},{10... | collective-permute-start | bytes 786440 | tf_op jit(solution)/shard_map/ppermute | solution.py:128
  19.3 1.7 %collective-permute-done.refs_5_.refs_7_ = f32[264,128]{1,0:T(8,128)S(1)} collective-permute-done((f32[264,128]{1,0:T(8,128)S(1)}, f32[264,128]{1,0:T(8,128)S(1)}, u32[]{:S(2)}, u32[]{:S(2)}) %collective-permute-start) | collective-permute-done | bytes 135200 | tf_op jit(solution)/shard_map/ppermute | solution.py:128
  22.6 1.6 %collective-permute-start.5 = (f32[768,128]{1,0:T(8,128)S(1)}, f32[768,128]{1,0:T(8,128)S(1)}, u32[]{:S(2)}, u32[]{:S(2)}) collective-permute-start(f32[768,128]{1,0:T(8,128)S(1)} %pad_maximum_fusion.1), channel_id=1, source_target_pairs={{0,4},{2,6},{4,0},{6,2},{1,5},{3,7},{5,1},{7,3},{8,12},{10,14},{12... | collective-permute-start | bytes 1179656 | tf_op jit(solution)/shard_map/ppermute | solution.py:119
  24.2 1.5 collective-permute-start.6
  26.4 4.8 %collective-permute-done.14.refs_11_ = f32[512,128]{1,0:T(8,128)S(1)} collective-permute-done((f32[512,128]{1,0:T(8,128)S(1)}, f32[512,128]{1,0:T(8,128)S(1)}, u32[]{:S(2)}, u32[]{:S(2)}) %collective-permute-start.14) | collective-permute-done | bytes 262176 | tf_op jit(solution)/shard_map/ppermute | solution.py:128
  32.5 7.8 %collective-permute-done.16 = f32[512,128]{1,0:T(8,128)S(1)} collective-permute-done((f32[512,128]{1,0:T(8,128)S(1)}, f32[512,128]{1,0:T(8,128)S(1)}, u32[]{:S(2)}, u32[]{:S(2)}) %collective-permute-start.16) | collective-permute-done | bytes 262176 | tf_op jit(solution)/shard_map/ppermute | solution.py:135
  40.3 1.6 %collective-permute-start.7 = (f32[384,128]{1,0:T(8,128)S(1)}, f32[384,128]{1,0:T(8,128)S(1)}, u32[]{:S(2)}, u32[]{:S(2)}) collective-permute-start(f32[384,128]{1,0:T(8,128)S(1)} %slice.39), channel_id=1, source_target_pairs={{0,1},{1,0},{2,3},{3,2},{4,5},{5,4},{6,7},{7,6},{8,9},{9,8},{10,11... | collective-permute-start | bytes 589832 | tf_op jit(solution)/shard_map/ppermute | solution.py:122
  41.9 1.6 collective-permute-start.8
  44.7 3.3 %collective-permute-done.7.refs_10_ = f32[384,128]{1,0:T(8,128)S(1)} collective-permute-done((f32[384,128]{1,0:T(8,128)S(1)}, f32[384,128]{1,0:T(8,128)S(1)}, u32[]{:S(2)}, u32[]{:S(2)}) %collective-permute-start.7) | collective-permute-done | bytes 196640 | tf_op jit(solution)/shard_map/ppermute | solution.py:122
  50.4 1.5 collective-permute-done.13.refs_16_
  51.9 8.1 %attention_forward.1 = (bf16[4,1024,384]{2,1,0:T(8,128)(2,1)}, f32[4,8,256,128]{3,2,1,0:T(8,128)}, bf16[1024,512]{1,0:T(8,128)(2,1)}, f32[1024,512]{1,0:T(8,128)...) custom-call(s32[5]{0:T(128)S(1)} %stack.20.meta, s32[8]{0:T(128)S(1)} %copy-done.29, ...), custom_call_target="tpu_custom_call" | custom-call | flops 2684354560 | bytes 16777216 | tf_op jit(solution)/shard_map/attention_forward/pallas_call | solution.py:347
  60.0 3.5 %collective-permute-done.17.refs_13_ = f32[1536,128]{1,0:T(8,128)S(1)} collective-permute-done((f32[1536,128]{1,0:T(8,128)S(1)}, f32[1536,128]{1,0:T(8,128)S(1)}, u32[]{:S(2)}, u32[]{:S(2)}) %collective-permute-start.17) | collective-permute-done | bytes 786464 | tf_op jit(solution)/shard_map/ppermute | solution.py:119
  64.1 1.6 collective-permute-start.20
  66.2 6.0 %collective-permute-done.19.refs_15_ = f32[768,128]{1,0:T(8,128)S(1)} collective-permute-done((f32[768,128]{1,0:T(8,128)S(1)}, f32[768,128]{1,0:T(8,128)S(1)}, u32[]{:S(2)}, u32[]{:S(2)}) %collective-permute-start.19) | collective-permute-done | bytes 393248 | tf_op jit(solution)/shard_map/ppermute | solution.py:122
  74.5 18.1 %feed_both.1 = (f32[1024,512]{1,0:T(8,128)}, f32[1024,512]{1,0:T(8,128)}, f32[8,512]{1,0:T(8,128)S(1)}, f32[9,3,512]{2,1,0:T(4,128)S(1)}, f32[8,512]{1,0:T(8,128...) custom-call(s32[5]{0:T(128)S(1)} %stack.20.meta, s32[8]{0:T(128)S(1)} %copy-done.30, s32[8]{0:T(128)S(1)} %copy-done.31, ...), custom_call_target="tpu_custom_call" | custom-call | flops 38654705664 | bytes 20971520 | tf_op jit(solution)/shard_map/feed_both/pallas_call | solution.py:513
  92.8 2.8 %collective-permute-done.26 = f32[2048,128]{1,0:T(8,128)S(1)} collective-permute-done((f32[2048,128]{1,0:T(8,128)}, f32[2048,128]{1,0:T(8,128)S(1)}, u32[]{:S(2)}, u32[]{:S(2)}) %collective-permute-start.26) | collective-permute-done | bytes 1048608 | tf_op jit(solution)/shard_map/ppermute | solution.py:116
  95.8 1.6 collective-permute-start.28
  99.3 6.6 %attention_own.1 = (bf16[1024,384]{1,0:T(8,128)(2,1)}, f32[1120,128]{1,0:T(8,128)S(1)}, f32[1120,128]{1,0:T(8,128)S(1)}) custom-call(s32[5]{0:T(128)S(1)} %stack.20.meta, f32[1024,512]{1,0:T(8,128)} %get-tuple-element.135.back_ref, bf16[1024,512]{1,0:T(8,128)(2,1)S(1)} %copy-done.7, bf16[4,1024,384]{2,1,0:T(8,128)(2,1)} %get-tuple-element.117.qkv, ...), custom_call_target="tpu_custom_call" | custom-call | flops 1073741824 | bytes 1024 | tf_op jit(solution)/shard_map/attention_own/pallas_call | solution.py:654
  105.9 5.1 %collective-permute-done.29 = f32[512,128]{1,0:T(8,128)S(1)} collective-permute-done((f32[512,128]{1,0:T(8,128)S(1)}, f32[512,128]{1,0:T(8,128)S(1)}, u32[]{:S(2)}, u32[]{:S(2)}) %collective-permute-start.29) | collective-permute-done | bytes 262176 | tf_op jit(solution)/shard_map/ppermute | solution.py:122
  113.2 1.6 collective-permute-start.32
  116.8 6.8 %attention_rest.2.refs_0_ = f32[1024,512]{1,0:T(8,128)} custom-call(s32[5]{0:T(128)S(1)} %stack.20.meta, f32[1024,512]{1,0:T(8,128)} %get-tuple-element.135.back_ref, bf16[4,1024,384]{2,1,0:T(8,128)(2,1)} %get-tuple-element.117.qkv, f32[4,8,256,128]{3,2,1,0:T(8,128)} %get-tuple-element.118.prob, bf16[512,512]{1,0:T(8,128)(2,1)S(1)} %copy-done.12, ...), custom_call_target="tpu_custom_call" | custom-call | flops 68719476736 | bytes 1024 | tf_op jit(solution)/shard_map/attention_rest/pallas_call | solution.py:696
  124.2 2.5 %collective-permute-done.34 = f32[280,128]{1,0:T(8,128)S(1)} collective-permute-done((f32[280,128]{1,0:T(8,128)S(1)}, f32[280,128]{1,0:T(8,128)S(1)}, u32[]{:S(2)}, u32[]{:S(2)}) %collective-permute-start.34) | collective-permute-done | bytes 143392 | tf_op jit(solution)/shard_map/ppermute | solution.py:125
  127.8 1.6 collective-permute-start.39
  131.1 1.8 %collective-permute-start.42 = (f32[280,128]{1,0:T(8,128)S(1)}, f32[280,128]{1,0:T(8,128)S(1)}, u32[]{:S(2)}, u32[]{:S(2)}) collective-permute-start(f32[280,128]{1,0:T(8,128)S(1)} %add_add_fusion.1.refs_0_), channel_id=1, source_target_pairs={{0,5},{1,4},{2,7},{3,6},{4,1},{5,0},{6,3},{7,2},{8,13},{9,12},{10,... | collective-permute-start | bytes 430088 | tf_op jit(solution)/shard_map/ppermute | solution.py:125
  132.8 6.8 %attention_rest.3 = f32[1024,512]{1,0:T(8,128)} custom-call(s32[5]{0:T(128)S(1)} %stack.20.meta, f32[1024,512]{1,0:T(8,128)} %get-tuple-element.135.back_ref, bf16[4,1024,384]{2,1,0:T(8,128)(2,1)} %get-tuple-element.117.qkv, f32[4,8,256,128]{3,2,1,0:T(8,128)} %get-tuple-element.118.prob, ...), custom_call_target="tpu_custom_call", output_to_operand_aliasing={{}: (7, {})} | custom-call | flops 68719476736 | bytes 1024 | tf_op jit(solution)/shard_map/attention_rest/pallas_call | solution.py:696
  146.0 2.9 %collective-permute-start.52 = (f32[8,128]{1,0:T(8,128)S(1)}, f32[8,128]{1,0:T(8,128)S(1)}, u32[]{:S(2)}, u32[]{:S(2)}) collective-permute-start(f32[8,128]{1,0:T(8,128)S(1)} %squares.1), channel_id=1, source_target_pairs={{0,24},{8,16},{16,8},{24,0},{1,25},{9,17},{17,9},{25,1},{2,26},{10... | collective-permute-start | bytes 12296 | tf_op jit(solution)/shard_map/ppermute | solution.py:128
  149.0 2.4 %ready.1 = (f32[2240,128]{1,0:T(8,128)S(1)}, f32[4096,128]{1,0:T(8,128)S(1)}, f32[3,512,128]{2,1,0:T(8,128)S(1)}, f32[128,512]{1,0:T(8,128)S(1)}, f32[2048,128]{1,0:T(8,128)S(1)}, /*index=5*/f32[512,512]{1,0:T(8,128)S(1)}) custom-call(s32[5]{0:T(128)S(1)} %stack.20.meta, f32[280,128]{1,0:T(8,128)S(1)} %add_add_fusion.1.refs_0_, ...), custom_call_target="tpu_custom_call" | custom-call | flops 68719476736 | bytes 1024 | tf_op jit(solution)/shard_map/ready/pallas_call | solution.py:801
  151.6 6.7 %adam.1 = (f32[1,1]{1,0:T(1,128)}, f32[3,512,128]{2,1,0:T(8,128)}, f32[3,512,128]{2,1,0:T(8,128)}, f32[3,512,128]{2,1,0:T(8,128)}, f32[128,512]{1,0:T(8,128)}, /...) custom-call(s32[5]{0:T(128)S(1)} %stack.20.meta, ...), custom_call_target="tpu_custom_call" | custom-call | tf_op jit(solution)/shard_map/adam/pallas_call | solution.py:894
  (171 shorter events, 29.3 us)
Async XLA Ops:
  2.5 10.7 %collective-permute-start.1 = (f32[264,128]{1,0:T(8,128)S(1)}, f32[264,128]{1,0:T(8,128)S(1)}, u32[]{:S(2)}, u32[]{:S(2)}) collective-permute-start(f32[264,128]{1,0:T(8,128)S(1)} %get-tuple-element.104), channel_id=1, source_target_pairs={{0,16},{8,24},{16,0},{24,8},{1,17},{9,25},{17,1},{25,9},{2,18},{10... | collective-permute-start | bytes 405512 | tf_op jit(solution)/shard_map/ppermute | solution.py:128
  6.6 16.0 %collective-permute-start.4 = (f32[512,128]{1,0:T(8,128)S(1)}, f32[512,128]{1,0:T(8,128)S(1)}, u32[]{:S(2)}, u32[]{:S(2)}) collective-permute-start(f32[512,128]{1,0:T(8,128)S(1)} %get-tuple-element.105), channel_id=1, source_target_pairs={{0,8},{8,0},{16,24},{24,16},{1,9},{9,1},{17,25},{25,17},{2,10},{10... | collective-permute-start | bytes 786440 | tf_op jit(solution)/shard_map/ppermute | solution.py:128
  8.2 12.8 %collective-permute-start = (f32[264,128]{1,0:T(8,128)S(1)}, f32[264,128]{1,0:T(8,128)S(1)}, u32[]{:S(2)}, u32[]{:S(2)}) collective-permute-start(f32[264,128]{1,0:T(8,128)S(1)} %get-tuple-element.104), channel_id=1, source_target_pairs={{0,8},{8,0},{16,24},{24,16},{1,9},{9,1},{17,25},{25,17},{2,10},{10... | collective-permute-start | bytes 405512 | tf_op jit(solution)/shard_map/ppermute | solution.py:128
  8.6 12.4 %collective-permute-start.2 = (f32[264,128]{1,0:T(8,128)S(1)}, f32[264,128]{1,0:T(8,128)S(1)}, u32[]{:S(2)}, u32[]{:S(2)}) collective-permute-start(f32[264,128]{1,0:T(8,128)S(1)} %get-tuple-element.104), channel_id=1, source_target_pairs={{8,16},{16,8},{9,17},{17,9},{10,18},{18,10},{11,19},{19,11},{12,20... | collective-permute-start | bytes 405512 | tf_op jit(solution)/shard_map/ppermute | solution.py:131
  13.2 9.2 %collective-permute-start.3 = (f32[264,128]{1,0:T(8,128)S(1)}, f32[264,128]{1,0:T(8,128)S(1)}, u32[]{:S(2)}, u32[]{:S(2)}) collective-permute-start(f32[264,128]{1,0:T(8,128)S(1)} %collective-permute-done.1.refs_6_.refs_8_), channel_id=1, source_target_pairs={{8,0},{16,24},{9,1},{17,25},{10,2},{18,26},{11,3},{19,27},{12,4},{... | collective-permute-start | bytes 405512 | tf_op jit(solution)/shard_map/ppermute | solution.py:135
  14.5 16.7 %collective-permute-start.14 = (f32[512,128]{1,0:T(8,128)S(1)}, f32[512,128]{1,0:T(8,128)S(1)}, u32[]{:S(2)}, u32[]{:S(2)}) collective-permute-start(f32[512,128]{1,0:T(8,128)S(1)} %get-tuple-element.105), channel_id=1, source_target_pairs={{0,16},{8,24},{16,0},{24,8},{1,17},{9,25},{17,1},{25,9},{2,18},{10... | collective-permute-start | bytes 786440 | tf_op jit(solution)/shard_map/ppermute | solution.py:128
  22.6 17.7 %collective-permute-start.5 = (f32[768,128]{1,0:T(8,128)S(1)}, f32[768,128]{1,0:T(8,128)S(1)}, u32[]{:S(2)}, u32[]{:S(2)}) collective-permute-start(f32[768,128]{1,0:T(8,128)S(1)} %pad_maximum_fusion.1), channel_id=1, source_target_pairs={{0,4},{2,6},{4,0},{6,2},{1,5},{3,7},{5,1},{7,3},{8,12},{10,14},{12... | collective-permute-start | bytes 1179656 | tf_op jit(solution)/shard_map/ppermute | solution.py:119
  24.2 17.7 %collective-permute-start.6 = (f32[768,128]{1,0:T(8,128)S(1)}, f32[768,128]{1,0:T(8,128)S(1)}, u32[]{:S(2)}, u32[]{:S(2)}) collective-permute-start(f32[768,128]{1,0:T(8,128)S(1)} %pad_maximum_fusion.1), channel_id=1, source_target_pairs={{0,1},{1,0},{2,3},{3,2},{4,5},{5,4},{6,7},{7,6},{8,9},{9,8},{10,11... | collective-permute-start | bytes 1179656 | tf_op jit(solution)/shard_map/ppermute | solution.py:122
  31.1 9.1 %collective-permute-start.16 = (f32[512,128]{1,0:T(8,128)S(1)}, f32[512,128]{1,0:T(8,128)S(1)}, u32[]{:S(2)}, u32[]{:S(2)}) collective-permute-start(f32[512,128]{1,0:T(8,128)S(1)} %collective-permute-done.14.refs_11_), channel_id=1, source_target_pairs={{8,0},{16,24},{9,1},{17,25},{10,2},{18,26},{11,3},{19,27},{12,4},{... | collective-permute-start | bytes 786440 | tf_op jit(solution)/shard_map/ppermute | solution.py:135
  32.4 15.6 %collective-permute-start.9 = (f32[768,128]{1,0:T(8,128)S(1)}, f32[768,128]{1,0:T(8,128)S(1)}, u32[]{:S(2)}, u32[]{:S(2)}) collective-permute-start(f32[768,128]{1,0:T(8,128)S(1)} %pad_maximum_fusion.1), channel_id=1, source_target_pairs={{0,2},{2,0},{4,6},{6,4},{1,3},{3,1},{5,7},{7,5},{8,10},{10,8},{12,... | collective-permute-start | bytes 1179656 | tf_op jit(solution)/shard_map/ppermute | solution.py:116
  40.3 7.7 %collective-permute-start.7 = (f32[384,128]{1,0:T(8,128)S(1)}, f32[384,128]{1,0:T(8,128)S(1)}, u32[]{:S(2)}, u32[]{:S(2)}) collective-permute-start(f32[384,128]{1,0:T(8,128)S(1)} %slice.39), channel_id=1, source_target_pairs={{0,1},{1,0},{2,3},{3,2},{4,5},{5,4},{6,7},{7,6},{8,9},{9,8},{10,11... | collective-permute-start | bytes 589832 | tf_op jit(solution)/shard_map/ppermute | solution.py:122
  41.9 7.9 %collective-permute-start.8 = (f32[384,128]{1,0:T(8,128)S(1)}, f32[384,128]{1,0:T(8,128)S(1)}, u32[]{:S(2)}, u32[]{:S(2)}) collective-permute-start(f32[384,128]{1,0:T(8,128)S(1)} %slice.40), channel_id=1, source_target_pairs={{0,4},{2,6},{4,0},{6,2},{1,5},{3,7},{5,1},{7,3},{8,12},{10,14},{12... | collective-permute-start | bytes 589832 | tf_op jit(solution)/shard_map/ppermute | solution.py:119
  43.6 19.9 %collective-permute-start.17 = (f32[1536,128]{1,0:T(8,128)S(1)}, f32[1536,128]{1,0:T(8,128)S(1)}, u32[]{:S(2)}, u32[]{:S(2)}) collective-permute-start(f32[1536,128]{1,0:T(8,128)S(1)} %pad_maximum_fusion), channel_id=1, source_target_pairs={{0,4},{2,6},{4,0},{6,2},{1,5},{3,7},{5,1},{7,3},{8,12},{10,14},{12... | collective-permute-start | bytes 2359304 | tf_op jit(solution)/shard_map/ppermute | solution.py:119
  44.2 19.3 %collective-permute-start.18 = (f32[1536,128]{1,0:T(8,128)S(1)}, f32[1536,128]{1,0:T(8,128)S(1)}, u32[]{:S(2)}, u32[]{:S(2)}) collective-permute-start(f32[1536,128]{1,0:T(8,128)S(1)} %pad_maximum_fusion), channel_id=1, source_target_pairs={{0,1},{1,0},{2,3},{3,2},{4,5},{5,4},{6,7},{7,6},{8,9},{9,8},{10,11... | collective-permute-start | bytes 2359304 | tf_op jit(solution)/shard_map/ppermute | solution.py:122
  63.5 8.6 %collective-permute-start.19 = (f32[768,128]{1,0:T(8,128)S(1)}, f32[768,128]{1,0:T(8,128)S(1)}, u32[]{:S(2)}, u32[]{:S(2)}) collective-permute-start(f32[768,128]{1,0:T(8,128)S(1)} %slice.32), channel_id=1, source_target_pairs={{0,1},{1,0},{2,3},{3,2},{4,5},{5,4},{6,7},{7,6},{8,9},{9,8},{10,11... | collective-permute-start | bytes 1179656 | tf_op jit(solution)/shard_map/ppermute | solution.py:122
  64.1 8.2 %collective-permute-start.20 = (f32[768,128]{1,0:T(8,128)S(1)}, f32[768,128]{1,0:T(8,128)S(1)}, u32[]{:S(2)}, u32[]{:S(2)}) collective-permute-start(f32[768,128]{1,0:T(8,128)S(1)} %slice.33), channel_id=1, source_target_pairs={{0,4},{2,6},{4,0},{6,2},{1,5},{3,7},{5,1},{7,3},{8,12},{10,14},{12... | collective-permute-start | bytes 1179656 | tf_op jit(solution)/shard_map/ppermute | solution.py:119
  65.7 8.8 %collective-permute-start.21 = (f32[1536,128]{1,0:T(8,128)S(1)}, f32[1536,128]{1,0:T(8,128)S(1)}, u32[]{:S(2)}, u32[]{:S(2)}) collective-permute-start(f32[1536,128]{1,0:T(8,128)S(1)} %pad_maximum_fusion), channel_id=1, source_target_pairs={{0,2},{2,0},{4,6},{6,4},{1,3},{3,1},{5,7},{7,5},{8,10},{10,8},{12,... | collective-permute-start | bytes 2359304 | tf_op jit(solution)/shard_map/ppermute | solution.py:116
  65.7 8.8 %collective-permute-start.22 = (f32[1536,128]{1,0:T(8,128)S(1)}, f32[1536,128]{1,0:T(8,128)S(1)}, u32[]{:S(2)}, u32[]{:S(2)}) collective-permute-start(f32[1536,128]{1,0:T(8,128)S(1)} %collective-permute-done.17.refs_13_), channel_id=1, source_target_pairs={{0,2},{2,0},{4,6},{6,4},{1,3},{3,1},{5,7},{7,5},{8,10},{10,8},{12,... | collective-permute-start | bytes 2359304 | tf_op jit(solution)/shard_map/ppermute | solution.py:116
  66.2 8.3 %collective-permute-start.23 = (f32[1536,128]{1,0:T(8,128)S(1)}, f32[1536,128]{1,0:T(8,128)S(1)}, u32[]{:S(2)}, u32[]{:S(2)}) collective-permute-start(f32[1536,128]{1,0:T(8,128)S(1)} %collective-permute-done.18.refs_14_), channel_id=1, source_target_pairs={{0,2},{2,0},{4,6},{6,4},{1,3},{3,1},{5,7},{7,5},{8,10},{10,8},{12,... | collective-permute-start | bytes 2359304 | tf_op jit(solution)/shard_map/ppermute | solution.py:116
  95.8 10.1 %collective-permute-start.28 = (f32[512,128]{1,0:T(8,128)S(1)}, f32[512,128]{1,0:T(8,128)S(1)}, u32[]{:S(2)}, u32[]{:S(2)}) collective-permute-start(f32[512,128]{1,0:T(8,128)S(1)} %get-tuple-element.185), channel_id=1, source_target_pairs={{0,4},{2,6},{4,0},{6,2},{1,5},{3,7},{5,1},{7,3},{8,12},{10,14},{12... | collective-permute-start | bytes 786440 | tf_op jit(solution)/shard_map/ppermute | solution.py:119
  97.3 13.7 %collective-permute-start.29 = (f32[512,128]{1,0:T(8,128)S(1)}, f32[512,128]{1,0:T(8,128)S(1)}, u32[]{:S(2)}, u32[]{:S(2)}) collective-permute-start(f32[512,128]{1,0:T(8,128)S(1)} %get-tuple-element.186), channel_id=1, source_target_pairs={{0,1},{1,0},{2,3},{3,2},{4,5},{5,4},{6,7},{7,6},{8,9},{9,8},{10,11... | collective-permute-start | bytes 786440 | tf_op jit(solution)/shard_map/ppermute | solution.py:122
  98.6 12.4 %collective-permute-start.30 = (f32[512,128]{1,0:T(8,128)S(1)}, f32[512,128]{1,0:T(8,128)S(1)}, u32[]{:S(2)}, u32[]{:S(2)}) collective-permute-start(f32[512,128]{1,0:T(8,128)S(1)} %get-tuple-element.184), channel_id=1, source_target_pairs={{0,5},{1,4},{2,7},{3,6},{4,1},{5,0},{6,3},{7,2},{8,13},{9,12},{10,... | collective-permute-start | bytes 786440 | tf_op jit(solution)/shard_map/ppermute | solution.py:125
  111.2 15.6 %collective-permute-start.36 = (f32[512,128]{1,0:T(8,128)S(1)}, f32[512,128]{1,0:T(8,128)S(1)}, u32[]{:S(2)}, u32[]{:S(2)}) collective-permute-start(f32[512,128]{1,0:T(8,128)S(1)} %add_add_fusion.refs_8_), channel_id=1, source_target_pairs={{0,4},{2,6},{4,0},{6,2},{1,5},{3,7},{5,1},{7,3},{8,12},{10,14},{12... | collective-permute-start | bytes 786440 | tf_op jit(solution)/shard_map/ppermute | solution.py:119
  112.3 14.6 %collective-permute-start.37 = (f32[512,128]{1,0:T(8,128)S(1)}, f32[512,128]{1,0:T(8,128)S(1)}, u32[]{:S(2)}, u32[]{:S(2)}) collective-permute-start(f32[512,128]{1,0:T(8,128)S(1)} %add_add_fusion.refs_8_), channel_id=1, source_target_pairs={{0,1},{1,0},{2,3},{3,2},{4,5},{5,4},{6,7},{7,6},{8,9},{9,8},{10,11... | collective-permute-start | bytes 786440 | tf_op jit(solution)/shard_map/ppermute | solution.py:122
  113.2 10.3 %collective-permute-start.32 = (f32[280,128]{1,0:T(8,128)S(1)}, f32[280,128]{1,0:T(8,128)S(1)}, u32[]{:S(2)}, u32[]{:S(2)}) collective-permute-start(f32[280,128]{1,0:T(8,128)S(1)} %get-tuple-element.189), channel_id=1, source_target_pairs={{0,4},{2,6},{4,0},{6,2},{1,5},{3,7},{5,1},{7,3},{8,12},{10,14},{12... | collective-permute-start | bytes 430088 | tf_op jit(solution)/shard_map/ppermute | solution.py:119
  114.8 9.4 %collective-permute-start.33 = (f32[280,128]{1,0:T(8,128)S(1)}, f32[280,128]{1,0:T(8,128)S(1)}, u32[]{:S(2)}, u32[]{:S(2)}) collective-permute-start(f32[280,128]{1,0:T(8,128)S(1)} %get-tuple-element.190), channel_id=1, source_target_pairs={{0,1},{1,0},{2,3},{3,2},{4,5},{5,4},{6,7},{7,6},{8,9},{9,8},{10,11... | collective-permute-start | bytes 430088 | tf_op jit(solution)/shard_map/ppermute | solution.py:122
  115.6 11.2 %collective-permute-start.34 = (f32[280,128]{1,0:T(8,128)S(1)}, f32[280,128]{1,0:T(8,128)S(1)}, u32[]{:S(2)}, u32[]{:S(2)}) collective-permute-start(f32[280,128]{1,0:T(8,128)S(1)} %get-tuple-element.188), channel_id=1, source_target_pairs={{0,5},{1,4},{2,7},{3,6},{4,1},{5,0},{6,3},{7,2},{8,13},{9,12},{10,... | collective-permute-start | bytes 430088 | tf_op jit(solution)/shard_map/ppermute | solution.py:125
  126.9 12.7 %collective-permute-start.38 = (f32[256,128]{1,0:T(8,128)S(1)}, f32[256,128]{1,0:T(8,128)S(1)}, u32[]{:S(2)}, u32[]{:S(2)}) collective-permute-start(f32[256,128]{1,0:T(8,128)S(1)} %slice.34), channel_id=1, source_target_pairs={{0,1},{1,0},{2,3},{3,2},{4,5},{5,4},{6,7},{7,6},{8,9},{9,8},{10,11... | collective-permute-start | bytes 393224 | tf_op jit(solution)/shard_map/ppermute | solution.py:122
  127.8 11.8 %collective-permute-start.39 = (f32[256,128]{1,0:T(8,128)S(1)}, f32[256,128]{1,0:T(8,128)S(1)}, u32[]{:S(2)}, u32[]{:S(2)}) collective-permute-start(f32[256,128]{1,0:T(8,128)S(1)} %slice.35), channel_id=1, source_target_pairs={{0,4},{2,6},{4,0},{6,2},{1,5},{3,7},{5,1},{7,3},{8,12},{10,14},{12... | collective-permute-start | bytes 393224 | tf_op jit(solution)/shard_map/ppermute | solution.py:119
  129.3 10.3 %collective-permute-start.40 = (f32[280,128]{1,0:T(8,128)S(1)}, f32[280,128]{1,0:T(8,128)S(1)}, u32[]{:S(2)}, u32[]{:S(2)}) collective-permute-start(f32[280,128]{1,0:T(8,128)S(1)} %add_add_fusion.1.refs_0_), channel_id=1, source_target_pairs={{0,1},{1,0},{2,3},{3,2},{4,5},{5,4},{6,7},{7,6},{8,9},{9,8},{10,11... | collective-permute-start | bytes 430088 | tf_op jit(solution)/shard_map/ppermute | solution.py:122
  130.1 9.5 %collective-permute-start.41 = (f32[280,128]{1,0:T(8,128)S(1)}, f32[280,128]{1,0:T(8,128)S(1)}, u32[]{:S(2)}, u32[]{:S(2)}) collective-permute-start(f32[280,128]{1,0:T(8,128)S(1)} %add_add_fusion.1.refs_0_), channel_id=1, source_target_pairs={{0,4},{2,6},{4,0},{6,2},{1,5},{3,7},{5,1},{7,3},{8,12},{10,14},{12... | collective-permute-start | bytes 430088 | tf_op jit(solution)/shard_map/ppermute | solution.py:119
  131.1 9.2 %collective-permute-start.42 = (f32[280,128]{1,0:T(8,128)S(1)}, f32[280,128]{1,0:T(8,128)S(1)}, u32[]{:S(2)}, u32[]{:S(2)}) collective-permute-start(f32[280,128]{1,0:T(8,128)S(1)} %add_add_fusion.1.refs_0_), channel_id=1, source_target_pairs={{0,5},{1,4},{2,7},{3,6},{4,1},{5,0},{6,3},{7,2},{8,13},{9,12},{10,... | collective-permute-start | bytes 430088 | tf_op jit(solution)/shard_map/ppermute | solution.py:125
  (55 other events, 614.6 us)
